TPU v7x, 32 devices: a whole 2x2x4 slice. The times are simulated.
32 devices in a mesh: gz: 4 (over y, core), xy: 8 (over z, x).
Axes of the slice: x: 2, y: 2, z: 4, core: 2. Of those that a mesh axis runs over, the one named last changes fastest.
Arguments:
- density: float32 [128, 256, 1024], P('gz', 'xy')
- uptake: float32 [128, 256, 1024], P('gz', 'xy'), may hold values from 0.5 to 50
- brick_values: bfloat16 [2304, 4096], P(('gz', 'xy'))
- brick_ids: int32 [2304], P(('gz', 'xy')), may hold values from 0 to 8191, as said below
- slot_counts: int32 [32, 9], P(('gz', 'xy')), may hold values from 0 to 8, as said below
Outputs:
- supply: float32 [128, 256, 1024], P('gz', 'xy')
- concentration: float32 [128, 256, 1024], P('gz', 'xy')
Inputs may be any that keep to these rules, and one draw needn't show every extreme that they name: `brick_ids`: the slots 8 j to 8 j + 7 of each device (j = 0 to 8) name bricks of the device whose gz index differs by j // 3 - 1 and whose xy index differs by j % 3 - 1, or of the device itself where no such device exists; the first and the last brick of the grid are both named. `slot_counts`: entry j of a device counts the live slots at the start of its block j; it is 0 where block j's device does not exist, and 8 for j = 4.
All inputs are finite; a program needn't handle non-finite values.
Results may differ from a plain program's by a relative error of at most 0.0014.
Values may be sent and summed in bfloat16 or wider, within the bound.
No kernel may reach another device: no remote copies, remote signals or barrier semaphores. Data moves between devices by JAX's collectives and lax.ppermute only.
A program may use at most 576 MiB of HBM per device.

v0:
```python
import jax
import jax.numpy as jnp
from jax import lax
from jax.experimental import pallas as pl
from jax.experimental.pallas import tpu as pltpu
from jax.sharding import PartitionSpec as P

EDGE = 16
CAP = 8
BRICK = 4096
SLOTS = 72
KAPPA = 32.0
OMEGA = 0.8
KEEP = 1.0 - OMEGA

C = 32
NT = 8
F32 = jnp.float32
BF16 = jnp.bfloat16


def spread(level):
    return KAPPA / 4.0**level


def shifted(values, distance, axis):
    return pltpu.roll(values, distance % values.shape[axis], axis)


def iota(shape, dim):
    return lax.broadcasted_iota(jnp.int32, shape, dim)


def lanes(t):
    return slice(t * 128, (t + 1) * 128)


def plane(ref, p):
    count = ref.shape[2] // 128
    rows = ref.shape[1]
    lane = iota((rows, 128), 1)
    before, here = None, ref[p, :, lanes(0)]
    for t in range(count):
        after = ref[p, :, lanes(t + 1)] if t + 1 < count else None
        low = jnp.where(lane == 127, 0.0 if before is None else before, here)
        high = jnp.where(lane == 0, 0.0 if after is None else after, here)
        sums = shifted(low, 1, 1) + shifted(high, -1, 1)
        sums = sums + (shifted(here, 1, 0) + shifted(here, -1, 0))
        sums = sums + (ref[p - 1, :, lanes(t)] + ref[p + 1, :, lanes(t)])
        yield t, here, sums
        before, here = here, after


def loop(start, stop, body, unroll=1):
    def step(i, carry):
        body(i)
        return carry

    lax.fori_loop(start, stop, step, 0, unroll=unroll)


def split_dot(a, b):
    high = a.astype(BF16)
    low = (a - high.astype(F32)).astype(BF16)
    return jnp.dot(high, b, preferred_element_type=F32) + jnp.dot(low, b, preferred_element_type=F32)


def pooling():
    return jnp.where(iota((256, 128), 0) // 2 == iota((256, 128), 1), 0.125, 0.0).astype(BF16)


def doubling():
    return jnp.where(iota((128, 256), 1) // 2 == iota((128, 256), 0), 1.0, 0.0).astype(BF16)


def halve_rows(values, rs, t):
    rows = values.shape[0]
    rs[t, 0:rows, :] = values
    return rs[t, pl.ds(0, rows // 2, stride=2), :] + rs[t, pl.ds(1, rows // 2, stride=2), :]


def halve_lanes(xp, planes, rows):
    matrix = pooling()
    tiles = []
    for t in range(0, xp.shape[0], 2):
        pair = jnp.concatenate([xp[t].reshape(planes * rows, 128), xp[t + 1].reshape(planes * rows, 128)], axis=1)
        tiles.append(split_dot(pair, matrix).reshape(planes, rows, 128))
    return tiles


def inside(shape, dim, first, wrap, index, size, count):
    place = iota(shape, dim) + first
    if wrap is not None:
        place = jnp.where(place < wrap, place, place - shape[dim])
    place = place + index * size
    return (place >= 0) & (place < count * size)


BLOCK = 272
Z_ROWS = BLOCK + 5 * 64
X_ROWS = BLOCK + 3 * 80 + 128


def z_part(t):
    return slice(BLOCK + 64 * (t // 3), BLOCK + 64 * (t // 3) + 64), lanes(t % 3)


def x_part(t):
    return slice(BLOCK + 80 * (t // 3), BLOCK + 80 * (t // 3) + 80), lanes(t % 3)


def transposed_bricks(bricks_x, ids, counts, bricks, xs, targets):
    xs[...] = bricks[...].astype(F32)
    row = iota((1, 8, 128), 1)
    group = iota((1, 8, 128), 2) // 16
    group16 = iota((16, 128), 1) // 16
    per_y = 64

    def block(j, out, part):
        start = pl.multiple_of(j * 8, 8)
        x = jnp.stack([xs[pl.ds(start, 8), lanes(k)] for k in range(32)])
        for s in (4, 2, 1):
            up = shifted(shifted(x, -s, 1), 16 * s, 2)
            down = shifted(shifted(x, s, 1), -16 * s, 2)
            row_bit = (row // s) % 2
            group_bit = (group // s) % 2
            x = jnp.where(row_bit == group_bit, x, jnp.where(row_bit == 0, up, down))
        x = jnp.where(group < counts[0, j], x, 0.0)
        out[0:256, part] = x.reshape(256, 128).astype(BF16)
        names = jnp.zeros((16, 128), jnp.int32)
        for e in range(CAP):
            number = ids[j * 8 + e]
            by = lax.rem(number, per_y)
            rest = lax.div(number, per_y)
            bx = lax.rem(rest, 2)
            bz = lax.rem(lax.div(rest, bricks_x), 2)
            names = jnp.where(group16 == e, (bz * 2 + bx) * per_y + by, names)
        out[256:272, part] = names.astype(F32).astype(BF16)

    for i, out in enumerate(targets):
        for d in range(3):
            block(3 * i + d, out, lanes(d))


def first_kernel(bricks_x, nz, info, ids, counts, bricks, uptake, own, r1, r2, zl, zh, z2l, z2h, xl, xh, rs, xp, rs1, xp1, xs):
    transposed_bricks(bricks_x, ids, counts, bricks, xs, (zl, own, zh))

    def pair(m):
        for t in range(NT):
            both = uptake[2 * m, :, lanes(t)] + uptake[2 * m + 1, :, lanes(t)]
            xp[t, m] = halve_rows(both, rs, t)

    loop(0, 16, pair)
    for t, tile in enumerate(halve_lanes(xp, 16, 16)):
        r1[:, :, lanes(t)] = tile

    def pair1(m):
        for t in range(4):
            both = r1[2 * m, :, lanes(t)] + r1[2 * m + 1, :, lanes(t)]
            xp1[t, m] = halve_rows(both, rs1, t)

    loop(0, 8, pair1)
    coarse = []
    for t, tile in enumerate(halve_lanes(xp1, 8, 8)):
        r2[:, lanes(t)] = tile.reshape(64, 128)
        coarse.append(tile.reshape(64, 128).astype(BF16))
    low, high = far_along_z(nz, info[0], r2[0:32, :], r2[32:64, :])
    z2l[...] = low.astype(BF16)
    z2h[...] = high.astype(BF16)
    for ref, u, r in ((zl, slice(0, 2), slice(0, 4)), (zh, slice(30, 32), slice(12, 16))):
        for t in range(8):
            ref[z_part(t)] = uptake[u, :, lanes(t)].reshape(64, 128).astype(BF16)
        for t in range(4):
            ref[z_part(8 + t)] = r1[r, :, lanes(t)].reshape(64, 128).astype(BF16)
        for t in range(2):
            ref[z_part(12 + t)] = coarse[t]
        ref[z_part(14)] = jnp.zeros((64, 128), BF16)

    sub = iota((8, 1024), 0)

    def columns(i):
        lows, highs = [], []
        for j in range(2):
            low, high = jnp.zeros((8, 1024), F32), jnp.zeros((8, 1024), F32)
            for n in range(4):
                z = 8 * i + 4 * j + n
                low = jnp.where(sub // 2 == n, shifted(uptake[z, 0:8, :], 2 * n, 0), low)
                high = jnp.where(sub // 2 == n, shifted(uptake[z, 24:32, :], 2 * n + 2, 0), high)
            lows.append(low)
            highs.append(high)
        rows = pl.ds(pl.multiple_of(16 * i, 16), 16)
        xl[rows, :] = jnp.concatenate(lows, axis=0).astype(BF16)
        xh[rows, :] = jnp.concatenate(highs, axis=0).astype(BF16)

    loop(0, 4, columns)


def far_along_z(nz, iz, to_low, to_high):
    if nz != 4:
        return to_low, to_high
    one = jnp.where(iz < 2, to_high, to_low)
    return one, one


def halves(sub, first, second):
    return jnp.where(sub < 4, first, shifted(second, 4, 1))


def uppers(sub, first, second):
    return jnp.where(sub < 4, shifted(first, 4, 1), second)


def far_messages(window):
    planes, _, width = window.shape
    pairs = window.reshape(planes // 2, 2, 8, width)
    sub = iota((planes // 2, 8, width), 1)
    size = (planes * 4, width)
    return halves(sub, pairs[:, 0], pairs[:, 1]).reshape(size), uppers(sub, pairs[:, 0], pairs[:, 1]).reshape(size)


def far_tile(from_low, from_high):
    width = from_low.shape[-1]
    low, high = from_low.reshape(-1, 8, width), from_high.reshape(-1, 8, width)
    sub = iota(low.shape, 1)
    even = jnp.where(sub < 4, high, shifted(low, 4, 1))
    odd = jnp.where(sub < 4, shifted(high, 4, 1), low)
    return jnp.stack([even, odd], axis=1).reshape(-1, 8, width)


def rates_window_kernel(own, r1, r2, uxl, uxh, zl, zh, z2l, z2h, q1, q2, xl, xh):
    for ref, d in ((xl, 0), (xh, 2)):
        for n, src in enumerate((own, zl, zh)):
            ref[0:BLOCK, lanes(n)] = src[0:BLOCK, lanes(d)]
    sub = iota((16, 128), 0)
    for t in range(8):
        rows, part = x_part(t)
        rows = rows.start
        xl[rows : rows + 64, part] = uxl[:, lanes(t)]
        xh[rows : rows + 64, part] = uxh[:, lanes(t)]
        both = [ref[z_part(t)].astype(F32) for ref in (zl, zh)]
        planes = [both[0][0:32], both[0][32:64], both[1][0:32], both[1][32:64]]
        to_low, to_high = jnp.zeros((16, 128), F32), jnp.zeros((16, 128), F32)
        for n, p in enumerate(planes):
            here = sub // 2 == n
            to_low = jnp.where(here, shifted(p[0:16], 2 * n, 0), to_low)
            to_high = jnp.where(here, shifted(p[16:32], 2 * n + 2, 0), to_high)
        xl[rows + 64 : rows + 80, part] = to_low.astype(BF16)
        xh[rows + 64 : rows + 80, part] = to_high.astype(BF16)
    rows, part = x_part(8)
    for ref in (xl, xh):
        ref[rows, part] = jnp.zeros((80, 128), BF16)

    low = jnp.concatenate([zl[z_part(8 + t)].astype(F32) for t in range(6)], axis=1)
    high = jnp.concatenate([zh[z_part(8 + t)].astype(F32) for t in range(6)], axis=1)
    q1[0:4, 0:16, :] = low[:, 0:512].reshape(4, 16, 512)
    q1[4:20, 0:16, :] = r1[...]
    q1[20:24, 0:16, :] = high[:, 0:512].reshape(4, 16, 512)
    q1[:, 16:24, :] = jnp.zeros((24, 8, 512), F32)
    sub1 = iota((12, 8, 512), 1)
    first = q1[:, 0:8, :].reshape(12, 2, 8, 512)
    last = q1[:, 8:16, :].reshape(12, 2, 8, 512)
    to_low = halves(sub1, first[:, 0], first[:, 1]).reshape(96, 512).astype(BF16)
    to_high = uppers(sub1, last[:, 0], last[:, 1]).reshape(96, 512).astype(BF16)
    start = X_ROWS - 128
    for ref, message in ((xl, to_low), (xh, to_high)):
        for t in range(3):
            ref[start : start + 96, lanes(t)] = message[:, lanes(t)]
            ref[start + 96 : start + 128, lanes(t)] = message[32 * t : 32 * t + 32, lanes(3)]
    q2[...] = window_planes(r2[...], low[:, 512:768], high[:, 512:768], z2l[...].astype(F32), z2h[...].astype(F32))


def rates_from_x(ref):
    start = X_ROWS - 128
    last = jnp.concatenate([ref[start + 96 : start + 128, lanes(t)] for t in range(3)], axis=0)
    tiles = [ref[start : start + 96, lanes(t)] for t in range(3)] + [last]
    return jnp.concatenate([a.astype(F32) for a in tiles], axis=1).reshape(12, 8, 512)


def window_planes(own, low, high, low2, high2):
    parts = (low2, low, own, high, high2)
    return jnp.concatenate([a.reshape(-1, 8, 256) for a in parts], axis=0)


def source_window_kernel(own, low, high, low2, high2, q2, window, near, fl, fh):
    planes = window_planes(own[...], low[...], high[...], low2[...], high2[...])
    window[...] = planes
    near[...] = planes.reshape(256, 256).astype(BF16)
    for i, values in enumerate((planes, q2[...])):
        to_low, to_high = far_messages(values)
        fl[128 * i : 128 * i + 128, :] = to_low.astype(BF16)
        fh[128 * i : 128 * i + 128, :] = to_high.astype(BF16)


def pre_kernel(
    nz, nx, info, density, uptake, own, zl, zh, xl, xh,
    supply, c1, mzl, mzh, pxl, pxh, v_out, g_out,
    va, vb, dd, gg, hot, rs, xp, usl, ush, sems,
):
    iz, ix = info[0], info[1]
    k = spread(0)
    base = 1.0 + 6.0 * k
    O = 5
    Q = 2

    for p in (0, 1, 2, 3, 4, 37, 38, 39, 40, 41):
        va[p] = jnp.zeros((40, 1024), F32)
    for p in (2, 3, 38, 39):
        vb[p] = jnp.zeros((40, 1024), F32)

    sub8 = iota((8, 1024), 0)

    for t in range(NT):
        usl[:, lanes(t)] = xl[x_part(t)].astype(F32)
        ush[:, lanes(t)] = xh[x_part(t)].astype(F32)

    def set_plane(q, rates, low, high, valid_z):
        gz = jnp.where(valid_z, OMEGA, 0.0)
        d = rates + base
        dd[q, 0:32, :] = d
        gg[q, 0:32, :] = gz / d
        d = jnp.where(sub8 < 2, high, jnp.where(sub8 >= 6, low, 0.0)) + base
        dd[q, 32:40, :] = d
        omega = jnp.where(sub8 < 2, jnp.where(ix < nx - 1, gz, 0.0), jnp.where(sub8 >= 6, jnp.where(ix > 0, gz, 0.0), 0.0))
        gg[q, 32:40, :] = omega / d

    def own_planes(i):
        rows = pl.ds(pl.multiple_of(8 * i, 8), 8)
        low, high = usl[rows, :], ush[rows, :]
        for n in range(4):
            z = 4 * i + n
            va[z + O, 0:32, :] = density[z]
            va[z + O, 32:40, :] = jnp.zeros((8, 1024), F32)
            set_plane(z + Q, uptake[z], shifted(low, 6 - 2 * n, 0), shifted(high, -2 * n, 0), True)

    loop(0, C // 4, own_planes)
    low, high = usl[64:72, :], ush[64:72, :]
    for n in range(4):
        ref = zl if n < 2 else zh
        rates = [ref[z_part(t)].astype(F32)[32 * (n % 2) : 32 * (n % 2) + 32] for t in range(NT)]
        rates = jnp.concatenate(rates, axis=1)
        exists = iz > 0 if n < 2 else iz < nz - 1
        set_plane(n if n < 2 else 32 + n, rates, shifted(low, 6 - 2 * n, 0), shifted(high, -2 * n, 0), exists)

    blocks = [(ref, lanes(1)) for ref in (own, zl, zh)] + [(ref, lanes(n)) for ref in (xl, xh) for n in range(3)]
    lane = iota((1, 128), 1)
    at_y = iota((1024, 128), 0)
    tiles = []
    for i, (ref, part) in enumerate(blocks):
        name = ref[256:272, part].astype(F32).astype(jnp.int32)[0:1]
        tiles.append(lax.shift_right_logical(name, 6))
        y = (name & 63) * 16 + (lane & 15)
        hot[:, lanes(i)] = jnp.where(at_y == y, 1.0, 0.0).astype(BF16)
    for tile in range(4):
        bz, bx = tile // 2, tile % 2
        left = jnp.concatenate(
            [jnp.where(tiles[i] == tile, ref[0:256, part].astype(F32), 0.0).astype(BF16) for i, (ref, part) in enumerate(blocks)],
            axis=1,
        )
        for n in range(4):
            cols = slice(n * 256, (n + 1) * 256)
            part = lax.dot_general(left, hot[cols, :], (((1,), (1,)), ((), ())), preferred_element_type=F32)
            zs, xs = slice(16 * bz, 16 * bz + 16), slice(16 * bx, 16 * bx + 16)
            supply[zs, xs, cols] = density[zs, xs, cols] + part.reshape(16, 16, 256)

    def sweep(src, dst, z, sourced):
        for t, here, sums in plane(src, z + O):
            inner = k * sums
            g = gg[z + Q, :, lanes(t)]
            if sourced:
                body = inner[0:32] + supply[z, :, lanes(t)]
                dst[z + O, 0:32, lanes(t)] = KEEP * here[0:32] + g[0:32] * body
                dst[z + O, 32:40, lanes(t)] = KEEP * here[32:40] + g[32:40] * inner[32:40]
            else:
                dst[z + O, :, lanes(t)] = KEEP * here + g * inner

    def halo_planes(src, dst, width):
        def step(i):
            sweep(src, dst, jnp.where(i < width, i - width, i - width + C), False)

        loop(0, 2 * width, step)

    loop(0, C, lambda z: sweep(va, vb, z, True), 2)
    halo_planes(va, vb, 1)
    loop(0, C, lambda z: sweep(vb, va, z, True), 2)
    halo_planes(vb, va, 2)

    v_copy = pltpu.make_async_copy(va.at[3:39], v_out, sems.at[0])
    g_copy = pltpu.make_async_copy(gg, g_out, sems.at[1])
    v_copy.start()
    g_copy.start()

    def residual(z, sourced, edge):
        for t, here, sums in plane(va, z + O):
            r = k * sums
            if not edge:
                r = r - dd[z + Q, :, lanes(t)] * here
            if sourced:
                r = jnp.concatenate([r[0:32] + supply[z, :, lanes(t)], r[32:40]], axis=0)
            yield t, r

    def coarse(m, sourced):
        both = zip(residual(2 * m - 4, sourced, False), residual(2 * m - 3, sourced, False))
        for (t, first), (_, second) in both:
            xp[t, m, 0:20, :] = halve_rows(first + second, rs, t)

    loop(2, 18, lambda m: coarse(m, True))
    loop(0, 2, lambda i: coarse(1 + 17 * i, False))

    def outer(i):
        for t, r in residual(jnp.where(i == 0, -3, 34), False, True):
            xp[t, 19 * i, 0:20, :] = halve_rows(r, rs, t)

    loop(0, 2, outer)

    sub = iota((20, 8, 128), 1)
    for t, tile in enumerate(halve_lanes(xp, 20, 24)):
        last = tile[:, 16:24]
        last = jnp.where(sub < 2, last, jnp.where(sub >= 6, shifted(last, 4, 1), 0.0))
        c1[:, 0:16, lanes(t)] = tile[:, 0:16]
        c1[:, 16:24, lanes(t)] = last

    empty = jnp.zeros((1, 8, 1024), F32)
    blank = jnp.zeros((8, 1024), F32)
    for ref, planes, values, z in ((mzl, slice(0, 6), va[3:7], 0), (mzh, slice(14, 20), va[35:39], 31)):
        source = c1[planes].reshape(144, 512)
        ref[0:80, 0:512] = source[0:80].astype(BF16)
        ref[0:64, 512:1024] = source[80:144].astype(BF16)
        ref[64:80, 512:1024] = jnp.zeros((16, 512), BF16)
        level0 = jnp.concatenate([values, jnp.concatenate([supply[z : z + 1], empty], axis=1)], axis=0)
        ref[80:288, :] = jnp.concatenate([level0.reshape(200, 1024), blank], axis=0).astype(BF16)

    def sides(i):
        lows, highs = [], []
        for j in range(2):
            p = 4 * i + 2 * j + 3
            lows.append(pack_low(va[p], va[p + 1]))
            highs.append(pack_high(va[p], va[p + 1]))
        rows = pl.ds(pl.multiple_of(16 * i, 16), 16)
        pxl[rows, :] = jnp.concatenate(lows, axis=0).astype(BF16)
        pxh[rows, :] = jnp.concatenate(highs, axis=0).astype(BF16)

    loop(0, 9, sides)

    def sources(i):
        lows, highs = [], []
        for j in range(2):
            low, high = jnp.zeros((8, 1024), F32), jnp.zeros((8, 1024), F32)
            for n in range(8):
                z = 16 * i + 8 * j + n
                low = jnp.where(sub8 == n, shifted(supply[z, 0:8, :], n, 0), low)
                high = jnp.where(sub8 == n, shifted(supply[z, 24:32, :], n + 1, 0), high)
            lows.append(low)
            highs.append(high)
        rows = pl.ds(pl.multiple_of(16 * i + 144, 16), 16)
        pxl[rows, :] = jnp.concatenate(lows, axis=0).astype(BF16)
        pxh[rows, :] = jnp.concatenate(highs, axis=0).astype(BF16)

    loop(0, 2, sources)
    v_copy.wait()
    g_copy.wait()


def outer_rows(sub):
    return (sub < 2) | (sub >= 6)


def pack_pair(sub, a, b):
    return jnp.where(outer_rows(sub), a, shifted(b, 4, 0))


def pack_low(first, second):
    sub = iota((8, 1024), 0)
    a, b = [jnp.where(sub < 4, v[0:8], v[32:40]) for v in (first, second)]
    return pack_pair(sub, a, b)


def pack_high(first, second):
    sub = iota((8, 1024), 0)
    a, b = [jnp.where(sub >= 4, v[24:32], v[32:40]) for v in (first, second)]
    return pack_pair(sub, a, b)


def sides_kernel(pxl, pxh, mzl, mzh, q2, out_l, out_h):
    for ref, out in ((pxl, out_l), (pxh, out_h)):
        out[0:176, :] = ref[...]
        for n in range(4):
            out[176:240, n * 256 : n * 256 + 256] = q2[8 * n : 8 * n + 8].reshape(64, 256).astype(BF16)
    for message, start in ((mzl, 0), (mzh, 128)):
        planes = message[80:240, :].astype(F32).reshape(4, 40, 1024)
        rows = slice(start, start + 16)
        for ref, out, pack in ((pxl, out_l, pack_low), (pxh, out_h, pack_high)):
            added = [pack(planes[2 * i], planes[2 * i + 1]) for i in range(2)]
            out[rows, :] = (ref[rows, :].astype(F32) + jnp.concatenate(added, axis=0)).astype(BF16)


def in_three(sub, tiles, free, turns):
    spare = (sub == free) | (sub == free + 1)
    last = tiles[:, 3]
    parts = [jnp.where(spare, shifted(last, turn, 1), tiles[:, i]) for i, turn in enumerate(turns)]
    return jnp.stack(parts, axis=1)


def out_of_three(sub, parts, free, turns):
    last = None
    for i, turn in enumerate(turns):
        back = shifted(parts[:, i], -turn, 1)
        home = (free - turn) % 8
        here = (sub == home) | (sub == home + 1)
        last = jnp.where(here, back, 0.0 if last is None else last)
    return jnp.stack([parts[:, 0], parts[:, 1], parts[:, 2], last], axis=1)


HIGH_PACK = (2, (-2, 4, 2))
LOW_PACK = (4, (-2, 4, 2))


def merge_kernel(c1, mzl, mzh, f1, mxl, mxh):
    zeros = jnp.zeros((24, 512), F32)
    for p in (0, 1, 22, 23):
        f1[p] = zeros
    f1[2:22] = c1[...]
    for ref, planes in ((mzl, slice(0, 6)), (mzh, slice(18, 24))):
        parts = [ref[0:80, 0:512].astype(F32), ref[0:64, 512:1024].astype(F32)]
        f1[planes] = f1[planes] + jnp.concatenate(parts, axis=0).reshape(6, 24, 512)
    sub = iota((6, 8, 512), 1)
    first, last, halo = [f1[:, 8 * n : 8 * n + 8].reshape(6, 4, 8, 512) for n in range(3)]
    sub4 = iota((6, 4, 8, 512), 2)
    to_high = in_three(sub, jnp.where(sub4 >= 4, last, halo), *HIGH_PACK)
    to_low = in_three(sub, jnp.where(sub4 >= 4, halo, first), *LOW_PACK)
    mxh[...] = to_high.reshape(144, 512).astype(BF16)
    mxl[...] = to_low.reshape(144, 512).astype(BF16)


def middle_kernel(nz, nx, info, f0, q_in, xl, xh, mxl, mxh, f1, g1, v1, g2, g2l, g2h, q0, va, rs, xp):
    iz, ix = info[0], info[1]
    k = spread(1)
    base = 1.0 + 6.0 * k
    sub6 = iota((6, 8, 512), 1)
    low = out_of_three(sub6, mxl[...].astype(F32).reshape(6, 3, 8, 512), *HIGH_PACK).reshape(24, 8, 512)
    high = out_of_three(sub6, mxh[...].astype(F32).reshape(6, 3, 8, 512), *LOW_PACK).reshape(24, 8, 512)
    sub = iota((24, 8, 512), 1)
    f1[:, 0:8] = f0[:, 0:8] + jnp.where(sub < 2, low, 0.0)
    f1[:, 8:16] = f0[:, 8:16] + jnp.where(sub >= 6, high, 0.0)
    f1[:, 16:24] = f0[:, 16:24] + jnp.where(sub >= 4, low, high)
    low, high = rates_from_x(xl), rates_from_x(xh)
    sub12 = iota((12, 8, 512), 1)
    even = jnp.where(sub12 >= 4, shifted(low, 4, 1), high)
    odd = jnp.where(sub12 >= 4, low, shifted(high, 4, 1))
    q0[:, 0:16] = q_in[:, 0:16]
    q0[:, 16:24] = jnp.stack([even, odd], axis=1).reshape(24, 8, 512)
    shape = (24, 24, 128)
    valid = inside(shape, 0, -4, None, iz, 16, nz) & inside(shape, 1, 0, 20, ix, 16, nx)
    for t in range(4):
        g = jnp.where(valid, OMEGA, 0.0) / (q0[:, :, lanes(t)] + base)
        g1[:, :, lanes(t)] = g
        va[:, :, lanes(t)] = g * f1[:, :, lanes(t)]
    v1[0] = va[0]
    v1[23] = va[23]

    def sweep(p):
        for t, here, sums in plane(va, p):
            v1[p, :, lanes(t)] = KEEP * here + g1[p, :, lanes(t)] * (f1[p, :, lanes(t)] + k * sums)

    loop(1, 23, sweep, 2)

    def residual(p):
        for t, here, sums in plane(v1, p):
            yield t, f1[p, :, lanes(t)] + k * sums - (q0[p, :, lanes(t)] + base) * here

    def coarse(m):
        for (t, first), (_, second) in zip(residual(2 * m + 4), residual(2 * m + 5)):
            xp[t, m] = halve_rows((first + second)[0:16], rs, t)

    loop(0, 8, coarse)
    for t, tile in enumerate(halve_lanes(xp, 8, 8)):
        g2[:, lanes(t)] = tile.reshape(64, 128)
        low, high = far_along_z(nz, iz, tile[0:4].reshape(32, 128), tile[4:8].reshape(32, 128))
        g2l[:, lanes(t)] = low
        g2h[:, lanes(t)] = high


def back_kernel(
    nz, nx, info, f1, g1, v1, vzl, vzh, vxl, vxh, own2, n2l, n2h, m2l, m2h, q_own, v_in, g_in, s_in,
    out,
    f2, q2, h2, a2, b2, rs, xp, xpr, wa, w1, zsl, zsh, vb, ws,
    v2, gg, supply, fsl, fsh, sems,
):
    iz, ix = info[0], info[1]
    matrix = doubling()
    level0 = [
        pltpu.make_async_copy(src, dst, sems.at[i])
        for i, (src, dst) in enumerate(((v_in, v2), (g_in, gg), (s_in, supply)))
    ]
    for copy in level0:
        copy.start()

    f2[:, 0:8, :] = own2[...]
    f2[:, 8:16, :] = n2h[...].astype(F32).reshape(32, 8, 256)
    f2[:, 16:24, :] = far_tile(m2l[0:128, :].astype(F32), m2h[0:128, :].astype(F32))
    f2[:, 24:32, :] = n2l[...].astype(F32).reshape(32, 8, 256)
    q2[:, 0:8, :] = q_own[...]
    q2[:, 16:24, :] = far_tile(m2l[128:256, :].astype(F32), m2h[128:256, :].astype(F32))
    for ref, rows in ((vxh, slice(8, 16)), (vxl, slice(24, 32))):
        for n in range(4):
            q2[8 * n : 8 * n + 8, rows, :] = ref[176:240, n * 256 : n * 256 + 256].astype(F32).reshape(8, 8, 256)

    k = spread(2)
    base = 1.0 + 6.0 * k
    shape = (32, 32, 128)
    valid = inside(shape, 0, -12, None, iz, 8, nz) & inside(shape, 1, 0, 20, ix, 8, nx)
    for t in range(2):
        g = jnp.where(valid, OMEGA, 0.0) / (q2[:, :, lanes(t)] + base)
        h2[:, :, lanes(t)] = g
        a2[:, :, lanes(t)] = g * f2[:, :, lanes(t)]
    b2[0] = a2[0]
    b2[31] = a2[31]

    def sweep2(src, dst):
        def body(p):
            for t, here, sums in plane(src, p):
                dst[p, :, lanes(t)] = KEEP * here + h2[p, :, lanes(t)] * (f2[p, :, lanes(t)] + k * sums)

        return body

    loop(1, 31, sweep2(a2, b2), 2)

    def coarse(m):
        total, rates = [0.0, 0.0], [0.0, 0.0]
        for j in range(2):
            p = 2 * m + j
            for t, here, sums in plane(b2, p):
                r = f2[p, :, lanes(t)] + k * sums - (q2[p, :, lanes(t)] + base) * here
                total[t] = total[t] + r
                rates[t] = rates[t] + q2[p, :, lanes(t)]
        for t in range(2):
            xp[t, m] = halve_rows(total[t], rs, t)
            xpr[t, m] = halve_rows(rates[t], rs, t + 2)

    for t in range(2):
        for m in (0, 15):
            xp[t, m] = jnp.zeros((16, 128), F32)
            xpr[t, m] = jnp.zeros((16, 128), F32)
    loop(1, 15, coarse)

    shape = (16, 16, 128)
    valid = inside(shape, 0, -6, None, iz, 4, nz) & inside(shape, 1, 0, 10, ix, 4, nx)
    k3 = spread(3)
    (source,) = halve_lanes(xp, 16, 16)
    (rates,) = halve_lanes(xpr, 16, 16)
    g = jnp.where(valid, OMEGA, 0.0) / (rates + (1.0 + 6.0 * k3))
    v = g * source
    lane = iota(shape, 2)
    for repeat in range(3):
        edge = jnp.zeros((1, 16, 128), F32)
        sums = jnp.concatenate([v[1:], edge], axis=0) + jnp.concatenate([edge, v[:-1]], axis=0)
        sums = sums + shifted(v, 1, 1) + shifted(v, -1, 1)
        sums = sums + jnp.where(lane == 0, 0.0, shifted(v, 1, 2)) + jnp.where(lane == 127, 0.0, shifted(v, -1, 2))
        v = KEEP * v + g * (source + k3 * sums)

    wide = split_dot(v[4:12].reshape(128, 128), matrix).reshape(8, 16, 256)
    for m in range(8):
        for t in range(2):
            part = wide[m, :, lanes(t)]
            rs[t, pl.ds(0, 16, stride=2), :] = part
            rs[t, pl.ds(1, 16, stride=2), :] = part
            for j in range(2):
                p = 8 + 2 * m + j
                b2[p, :, lanes(t)] = b2[p, :, lanes(t)] + rs[t, 0:32, :]
    loop(9, 23, sweep2(b2, a2), 2)
    loop(10, 22, sweep2(a2, b2), 2)

    w = b2[10:22]
    near, far = w[:, 8:16], w[:, 24:32]
    near = jnp.where(iota((12, 8, 256), 1) < 2, near, shifted(far, 4, 1))
    w = jnp.concatenate([w[:, 0:8], near], axis=1).reshape(192, 256)
    wide = [split_dot(w[:, lanes(t)], matrix) for t in range(2)]
    wide = jnp.concatenate(wide, axis=1).reshape(12, 16, 512)
    for m in range(12):
        for t in range(4):
            part = wide[m, :, lanes(t)]
            rs[t, pl.ds(0, 16, stride=2), :] = part
            rs[t, pl.ds(1, 16, stride=2), :] = part
            for j in range(2):
                p = 2 * m + j
                wa[p, :, lanes(t)] = v1[p, :, lanes(t)] + rs[t, 0:24, :]
    k1 = spread(1)

    def sweep1(src, dst):
        def body(p):
            for t, here, sums in plane(src, p):
                dst[p, :, lanes(t)] = KEEP * here + g1[p, :, lanes(t)] * (f1[p, :, lanes(t)] + k1 * sums)

        return body

    loop(2, 22, sweep1(wa, w1), 2)
    loop(3, 21, sweep1(w1, wa), 2)

    sub = iota((18, 8, 128), 1)
    for t in range(4):
        halo = wa[3:21, 16:24, lanes(t)]
        halo = jnp.where(sub < 2, halo, shifted(halo, 4, 1))
        w = jnp.concatenate([wa[3:21, 0:16, lanes(t)], halo], axis=1)
        ws[:, :, t * 256 : t * 256 + 256] = split_dot(w.reshape(432, 128), matrix).reshape(18, 24, 256)

    for copy in level0:
        copy.wait()
    zsl[...] = vzl[80:288, :].astype(F32)
    zsh[...] = vzh[80:288, :].astype(F32)
    for i in range(4):
        v2[i] = v2[i] + zsl[40 * i : 40 * i + 40, :]
        v2[32 + i] = v2[32 + i] + zsh[40 * i : 40 * i + 40, :]

    s8 = iota((8, 128), 0)

    outer = outer_rows(s8)

    def correct(i):
        rows = pl.ds(pl.multiple_of(16 * i, 16), 16)
        for t in range(NT):
            low = vxl[rows, lanes(t)].astype(F32)
            high = vxh[rows, lanes(t)].astype(F32)
            for n in range(2):
                part = ws[2 * i + n, :, lanes(t)]
                rs[t, pl.ds(0, 24, stride=2), :] = part
                rs[t, pl.ds(1, 24, stride=2), :] = part
                for j in range(2):
                    p = 4 * i + 2 * n + j
                    lo, hi = low[8 * n : 8 * n + 8], high[8 * n : 8 * n + 8]
                    if j:
                        lo, hi = shifted(lo, 4, 0), shifted(hi, 4, 0)
                    v2[p, 0:8, lanes(t)] = v2[p, 0:8, lanes(t)] + rs[t, 0:8, :] + jnp.where(s8 < 2, lo, 0.0)
                    v2[p, 8:24, lanes(t)] = v2[p, 8:24, lanes(t)] + rs[t, 8:24, :]
                    v2[p, 24:32, lanes(t)] = v2[p, 24:32, lanes(t)] + rs[t, 24:32, :] + jnp.where(s8 >= 6, hi, 0.0)
                    extra = jnp.where(outer, jnp.where(s8 >= 4, lo, hi), 0.0)
                    v2[p, 32:40, lanes(t)] = v2[p, 32:40, lanes(t)] + rs[t, 32:40, :] + extra

    loop(0, 9, correct)
    k0 = spread(0)

    def first(i):
        rows = pl.ds(pl.multiple_of(16 * i + 144, 16), 16)
        for t in range(NT):
            fsl[:, lanes(t)] = vxl[rows, lanes(t)].astype(F32)
            fsh[:, lanes(t)] = vxh[rows, lanes(t)].astype(F32)

        def step(j):
            z = 16 * i + j
            start = pl.multiple_of((j // 8) * 8, 8)
            turn = lax.rem(j, 8)
            for t, here, sums in plane(v2, z + 2):
                lo = pltpu.roll(fsl[pl.ds(start, 8), lanes(t)], 7 - turn, 0)
                hi = pltpu.roll(fsh[pl.ds(start, 8), lanes(t)], lax.rem(8 - turn, 8), 0)
                f = jnp.where(s8 == 7, lo, jnp.where(s8 == 0, hi, 0.0))
                g = gg[z + 2, :, lanes(t)]
                inner = k0 * sums
                vb[z + 1, 0:32, lanes(t)] = KEEP * here[0:32] + g[0:32] * (supply[z, :, lanes(t)] + inner[0:32])
                vb[z + 1, 32:40, lanes(t)] = KEEP * here[32:40] + g[32:40] * (f + inner[32:40])

        loop(0, 16, step, 2)

    loop(0, 2, first)
    for p, ref in ((1, zsl), (34, zsh)):
        for t, here, sums in plane(v2, p):
            g = gg[p, :, lanes(t)]
            vb[p - 1, :, lanes(t)] = KEEP * here + g * (ref[160:200, lanes(t)] + k0 * sums)

    def second(z):
        for t, here, sums in plane(vb, z + 1):
            g = gg[z + 2, 0:32, lanes(t)]
            out[z, :, lanes(t)] = KEEP * here[0:32] + g * (supply[z, :, lanes(t)] + k0 * sums[0:32])

    loop(0, C, second, 2)


VMEM = pl.BlockSpec(memory_space=pltpu.VMEM)
SMEM = pl.BlockSpec(memory_space=pltpu.SMEM)
ANY = pl.BlockSpec(memory_space=pl.ANY)


def call(kernel, outs, scratch, smem, args, out_specs=None, in_hbm=0):
    moved = sum(a.size * a.dtype.itemsize for a in list(args) + list(outs))
    return pl.pallas_call(
        kernel,
        out_shape=tuple(outs),
        in_specs=[SMEM] * smem + [VMEM] * (len(args) - smem - in_hbm) + [ANY] * in_hbm,
        out_specs=tuple(out_specs or [VMEM] * len(outs)),
        scratch_shapes=scratch,
        compiler_params=pltpu.CompilerParams(vmem_limit_bytes=58 * 2**20),
        cost_estimate=pl.CostEstimate(flops=20 * moved, bytes_accessed=moved, transcendentals=0),
    )(*args)


def shaped(shape, dtype=F32):
    return jax.ShapeDtypeStruct(shape, dtype)


def both_ways(to_low, to_high, axis, distance=1):
    count = lax.axis_size(axis)
    up = [(i, i + distance) for i in range(count - distance)]
    down = [(j, i) for i, j in up]
    return lax.ppermute(to_high, axis, up), lax.ppermute(to_low, axis, down)


def two_away(to_low, to_high):
    count = lax.axis_size("gz")
    if count != 4:
        return both_ways(to_low, to_high, "gz", 2)
    came = lax.ppermute(to_low, "gz", [(i, (i + 2) % 4) for i in range(4)])
    return came, came


def shards(density, uptake, brick_values, brick_ids, slot_counts):
    nz, nx = lax.axis_size("gz"), lax.axis_size("xy")
    info = jnp.stack([lax.axis_index("gz"), lax.axis_index("xy")]).astype(jnp.int32)
    scratch = pltpu.VMEM
    half = lambda *shape: shaped(shape, BF16)
    full = lambda *shape: shaped(shape, F32)

    own, r1, r2, zl, zh, z2l, z2h, uxl, uxh = call(
        lambda *refs: first_kernel(2 * nx, nz, *refs),
        [
            half(BLOCK, 384), full(16, 16, 512), full(64, 256), half(Z_ROWS, 384), half(Z_ROWS, 384),
            half(32, 256), half(32, 256), half(64, 1024), half(64, 1024),
        ],
        [
            scratch((8, 32, 128), F32), scratch((8, 16, 16, 128), F32), scratch((4, 16, 128), F32),
            scratch((4, 8, 8, 128), F32), scratch((SLOTS, BRICK), F32),
        ],
        3,
        (info, brick_ids, slot_counts, brick_values, uptake),
    )
    zl, zh = both_ways(zl, zh, "gz")
    z2l, z2h = two_away(z2l, z2h)
    q1, q2, xl, xh = call(
        rates_window_kernel,
        [full(24, 24, 512), full(32, 8, 256), half(X_ROWS, 384), half(X_ROWS, 384)],
        [],
        0,
        (own, r1, r2, uxl, uxh, zl, zh, z2l, z2h),
    )
    xl, xh = both_ways(xl, xh, "xy")

    supply, c1, mzl, mzh, pxl, pxh, v2, gg = call(
        lambda *refs: pre_kernel(nz, nx, *refs),
        [
            full(C, C, 1024),
            full(20, 24, 512),
            half(288, 1024),
            half(288, 1024),
            half(176, 1024),
            half(176, 1024),
            full(36, 40, 1024),
            full(36, 40, 1024),
        ],
        [
            scratch((42, 40, 1024), F32),
            scratch((42, 40, 1024), F32),
            scratch((36, 40, 1024), F32),
            scratch((36, 40, 1024), F32),
            scratch((1024, 1152), BF16),
            scratch((8, 40, 128), F32),
            scratch((8, 20, 24, 128), F32),
            scratch((80, 1024), F32),
            scratch((80, 1024), F32),
            pltpu.SemaphoreType.DMA((2,)),
        ],
        1,
        (info, density, uptake, own, zl, zh, xl, xh),
        [VMEM] * 6 + [ANY] * 2,
    )
    mzl, mzh = both_ways(mzl, mzh, "gz")
    f1, mxl, mxh = call(
        merge_kernel,
        [full(24, 24, 512), half(144, 512), half(144, 512)],
        [],
        0,
        (c1, mzl, mzh),
    )
    mxl, mxh = both_ways(mxl, mxh, "xy")
    pxl, pxh = call(
        sides_kernel,
        [half(240, 1024), half(240, 1024)],
        [],
        0,
        (pxl, pxh, mzl, mzh, q2),
    )
    vxl, vxh = both_ways(pxl, pxh, "xy")
    f1, pxl, pxh = lax.optimization_barrier((f1, pxl, pxh))
    f1, g1, v1, g2, g2l, g2h = call(
        lambda *refs: middle_kernel(nz, nx, *refs),
        [full(24, 24, 512), full(24, 24, 512), full(24, 24, 512), full(64, 256), full(32, 256), full(32, 256)],
        [scratch((24, 24, 512), F32), scratch((24, 24, 512), F32), scratch((4, 16, 128), F32), scratch((4, 8, 8, 128), F32)],
        1,
        (info, f1, q1, xl, xh, mxl, mxh),
    )
    low, high = both_ways(g2, g2, "gz")
    low2, high2 = two_away(g2l, g2h)
    own2, near, fl, fh = call(
        source_window_kernel,
        [full(32, 8, 256), half(256, 256), half(256, 256), half(256, 256)],
        [],
        0,
        (g2, low, high, low2, high2, q2),
    )
    nl, nh = both_ways(near, near, "xy")
    fl, fh = both_ways(fl, fh, "xy", 2)
    window2 = scratch((32, 32, 256), F32)
    window1 = scratch((24, 24, 512), F32)
    (concentration,) = call(
        lambda *refs: back_kernel(nz, nx, *refs),
        [full(C, C, 1024)],
        [
            window2, window2, window2, window2, window2,
            scratch((8, 48, 128), F32),
            scratch((2, 16, 16, 128), F32),
            scratch((2, 16, 16, 128), F32),
            window1, window1,
            scratch((208, 1024), F32),
            scratch((208, 1024), F32),
            scratch((34, 40, 1024), F32),
            scratch((18, 24, 1024), F32),
            scratch((36, 40, 1024), F32),
            scratch((36, 40, 1024), F32),
            scratch((C, C, 1024), F32),
            scratch((16, 1024), F32),
            scratch((16, 1024), F32),
            pltpu.SemaphoreType.DMA((3,)),
        ],
        1,
        (info, f1, g1, v1, mzl, mzh, vxl, vxh, own2, nl, nh, fl, fh, q2, v2, gg, supply),
        in_hbm=3,
    )
    return supply, concentration


def solution(mesh):
    return jax.shard_map(
        shards,
        mesh=mesh,
        in_specs=(
            P("gz", "xy", None),
            P("gz", "xy", None),
            P(("gz", "xy"), None),
            P(("gz", "xy")),
            P(("gz", "xy"), None),
        ),
        out_specs=(P("gz", "xy", None), P("gz", "xy", None)),
        check_vma=False,
    )
```

profile of v0, /device:TPU:0, one launch (start us, length us, event | category | flops | bytes accessed | tf_op | source)
XLA Modules:
  0.0 173.0 jit_solution(1902371531258695422)
XLA Ops:
  1.2 7.3 %shard_map.68 = (bf16[272,384]{1,0:T(8,128)(2,1)}, f32[16,16,512]{2,1,0:T(8,128)}, f32[64,256]{1,0:T(8,128)}, bf16[592,384]{1,0:T(8,128)(2,1)}, bf16[592,384]{1,...) custom-call(s32[2]{0:T(128)} %pad_add_fusion.refs_0_, ...), custom_call_target="tpu_custom_call" | custom-call | flops 135748080 | bytes 6787404 | tf_op jit(solution)/shard_map/pallas_call | solution.py:782
  8.5 2.4 %collective-permute-start = (bf16[592,384]{1,0:T(8,128)(2,1)}, bf16[592,384]{1,0:T(8,128)(2,1)S(1)}, u32[]{:S(2)}, u32[]{:S(2)}) collective-permute-start(bf16[592,384]{1,0:T(8,128)(2,1)} %get-tuple-element.38), channel_id=1, source_target_pairs={{0,8},{8,16},{16,24},{1,9},{9,17},{17,25},{2,10},{10,18},{18,26},{... | collective-permute-start | bytes 1363976 | tf_op jit(solution)/shard_map/ppermute | solution.py:801
  10.8 1.3 collective-permute-start.1
  12.1 4.9 %collective-permute-start.2 = (bf16[32,256]{1,0:T(8,128)(2,1)}, bf16[32,256]{1,0:T(8,128)(2,1)S(1)}, u32[]{:S(2)}, u32[]{:S(2)}) collective-permute-start(bf16[32,256]{1,0:T(8,128)(2,1)} %get-tuple-element.44), channel_id=1, source_target_pairs={{0,16},{8,24},{16,0},{24,8},{1,17},{9,25},{17,1},{25,9},{2,18},{10... | collective-permute-start | bytes 49160 | tf_op jit(solution)/shard_map/ppermute | solution.py:808
  17.1 6.7 %collective-permute-done.2.z2l.z2h = bf16[32,256]{1,0:T(8,128)(2,1)S(1)} collective-permute-done((bf16[32,256]{1,0:T(8,128)(2,1)}, bf16[32,256]{1,0:T(8,128)(2,1)S(1)}, u32[]{:S(2)}, u32[]{:S(2)}) %collective-permute-start.2) | collective-permute-done | bytes 16416 | tf_op jit(solution)/shard_map/ppermute | solution.py:808
  24.7 3.1 %shard_map.69 = (f32[24,24,512]{2,1,0:T(8,128)}, f32[32,8,256]{2,1,0:T(8,128)}, bf16[640,384]{1,0:T(8,128)(2,1)}, bf16[640,384]{1,0:T(8,128)(2,1)}) custom-call(bf16[272,384]{1,0:T(8,128)(2,1)} %get-tuple-element.37.own.refs_3_, f32[16,16,512]{2,1,0:T(8,128)} %get-tuple-element.40.r1, f32[64,256]{1,0:T(8,128)} %get-tuple-element.41.r2, ...), custom_call_target="tpu_custom_call" | custom-call | flops 88555520 | bytes 4427776 | tf_op jit(solution)/shard_map/pallas_call | solution.py:782
  27.8 3.4 %collective-permute-start.3 = (bf16[640,384]{1,0:T(8,128)(2,1)}, bf16[640,384]{1,0:T(8,128)(2,1)S(1)}, u32[]{:S(2)}, u32[]{:S(2)}) collective-permute-start(bf16[640,384]{1,0:T(8,128)(2,1)} %get-tuple-element.45), channel_id=1, source_target_pairs={{0,1},{1,2},{2,3},{3,4},{4,5},{5,6},{6,7},{8,9},{9,10},{10,11},{11... | collective-permute-start | bytes 1474568 | tf_op jit(solution)/shard_map/ppermute | solution.py:801
  31.2 1.3 collective-permute-start.4
  32.5 19.6 %collective-permute-done.3.refs_6_.refs_3_ = bf16[640,384]{1,0:T(8,128)(2,1)S(1)} collective-permute-done((bf16[640,384]{1,0:T(8,128)(2,1)}, bf16[640,384]{1,0:T(8,128)(2,1)S(1)}, u32[]{:S(2)}, u32[]{:S(2)}) %collective-permute-start.3) | collective-permute-done | bytes 491552 | tf_op jit(solution)/shard_map/ppermute | solution.py:801
  53.7 27.1 %shard_map.70 = (f32[32,32,1024]{2,1,0:T(8,128)}, f32[20,24,512]{2,1,0:T(8,128)}, bf16[288,1024]{1,0:T(8,128)(2,1)}, bf16[288,1024]{1,0:T(8,128)(2,1)}, bf16[176...) custom-call(s32[2]{0:T(128)} %pad_add_fusion.refs_0_, ...), custom_call_target="tpu_custom_call" | custom-call | flops 587284608 | bytes 29364232 | tf_op jit(solution)/shard_map/pallas_call | solution.py:782
  80.8 1.3 collective-permute-start.5
  82.2 1.3 collective-permute-start.6
  83.9 2.3 %collective-permute-done.6.mzh.refs_5_ = bf16[288,1024]{1,0:T(8,128)(2,1)S(1)} collective-permute-done((bf16[288,1024]{1,0:T(8,128)(2,1)}, bf16[288,1024]{1,0:T(8,128)(2,1)S(1)}, u32[]{:S(2)}, u32[]{:S(2)}) %collective-permute-start.6) | collective-permute-done | bytes 589856 | tf_op jit(solution)/shard_map/ppermute | solution.py:801
  87.1 2.8 %shard_map.71 = (f32[24,24,512]{2,1,0:T(8,128)}, bf16[144,512]{1,0:T(8,128)(2,1)}, bf16[144,512]{1,0:T(8,128)(2,1)}) custom-call(f32[20,24,512]{2,1,0:T(8,128)} %get-tuple-element.48.c1, bf16[288,1024]{1,0:T(8,128)(2,1)} %copy-done, bf16[288,1024]{1,0:T(8,128)(2,1)} %copy-done.1), custom_call_target="tpu_custom_call" | custom-call | flops 72744960 | bytes 3637248 | tf_op jit(solution)/shard_map/pallas_call | solution.py:782
  89.9 4.3 %collective-permute-start.7 = (bf16[144,512]{1,0:T(8,128)(2,1)}, bf16[144,512]{1,0:T(8,128)(2,1)S(1)}, u32[]{:S(2)}, u32[]{:S(2)}) collective-permute-start(bf16[144,512]{1,0:T(8,128)(2,1)} %get-tuple-element.59), channel_id=1, source_target_pairs={{0,1},{1,2},{2,3},{3,4},{4,5},{5,6},{6,7},{8,9},{9,10},{10,11},{11... | collective-permute-start | bytes 442376 | tf_op jit(solution)/shard_map/ppermute | solution.py:801
  94.2 1.3 collective-permute-start.8
  95.5 2.6 %shard_map.72 = (bf16[240,1024]{1,0:T(8,128)(2,1)}, bf16[240,1024]{1,0:T(8,128)(2,1)}) custom-call(bf16[176,1024]{1,0:T(8,128)(2,1)} %get-tuple-element.52.pxl, bf16[176,1024]{1,0:T(8,128)(2,1)} %get-tuple-element.53.pxh, bf16[288,1024]{1,0:T(8,128)(2,1)} %copy-done, bf16[288,1024]{1,0:T(8,128)(2,1)} %copy-done.1, f32[32,8,256]{2,1,0:T(8,128)} %get-tuple-element.54.q2.refs_13_), custom_call_target="tpu_custom_call" | custom-call | flops 62914560 | bytes 3145728 | tf_op jit(solution)/shard_map/pallas_call | solution.py:782
  98.1 1.3 collective-permute-start.10
  99.4 5.5 %collective-permute-start.9 = (bf16[240,1024]{1,0:T(8,128)(2,1)}, bf16[240,1024]{1,0:T(8,128)(2,1)S(1)}, u32[]{:S(2)}, u32[]{:S(2)}) collective-permute-start(bf16[240,1024]{1,0:T(8,128)(2,1)} %get-tuple-element.56), channel_id=1, source_target_pairs={{0,1},{1,2},{2,3},{3,4},{4,5},{5,6},{6,7},{8,9},{9,10},{10,11},{11... | collective-permute-start | bytes 1474568 | tf_op jit(solution)/shard_map/ppermute | solution.py:801
  105.6 6.9 %shard_map.73 = (f32[24,24,512]{2,1,0:T(8,128)}, f32[24,24,512]{2,1,0:T(8,128)}, f32[24,24,512]{2,1,0:T(8,128)}, f32[64,256]{1,0:T(8,128)}, f32[32,256]{1,0:T(8,128)}, /*index=5*/f32[32,256]{1,0:T(8,128)}) custom-call(s32[2]{0:T(128)} %pad_add_fusion.refs_0_, f32[24,24,512]{2,1,0:T(8,128)} %get-tuple-element.57.refs_1_, ...), custom_call_target="tpu_custom_call" | custom-call | flops 146145440 | bytes 7307272 | tf_op jit(solution)/shard_map/pallas_call | solution.py:782
  112.5 1.3 collective-permute-start.12
  113.8 9.3 %collective-permute-start.11 = (f32[64,256]{1,0:T(8,128)}, f32[64,256]{1,0:T(8,128)S(1)}, u32[]{:S(2)}, u32[]{:S(2)}) collective-permute-start(f32[64,256]{1,0:T(8,128)} %get-tuple-element.64.own), channel_id=1, source_target_pairs={{0,8},{8,16},{16,24},{1,9},{9,17},{17,25},{2,10},{10,18},{18,26},{... | collective-permute-start | bytes 196616 | tf_op jit(solution)/shard_map/ppermute | solution.py:801
  123.0 1.7 collective-permute-start.13
  124.7 2.5 %collective-permute-done.13.low2.high2 = f32[32,256]{1,0:T(8,128)S(1)} collective-permute-done((f32[32,256]{1,0:T(8,128)}, f32[32,256]{1,0:T(8,128)S(1)}, u32[]{:S(2)}, u32[]{:S(2)}) %collective-permute-start.13) | collective-permute-done | bytes 32800 | tf_op jit(solution)/shard_map/ppermute | solution.py:808
  128.5 2.0 %shard_map.74 = (f32[32,8,256]{2,1,0:T(8,128)}, bf16[256,256]{1,0:T(8,128)(2,1)}, bf16[256,256]{1,0:T(8,128)(2,1)}, bf16[256,256]{1,0:T(8,128)(2,1)}) custom-call(f32[64,256]{1,0:T(8,128)} %get-tuple-element.64.own, f32[64,256]{1,0:T(8,128)} %copy-done.17, f32[64,256]{1,0:T(8,128)} %copy-done.16, f32[32,256]{1,0:T(8,128)} %copy-done.14, ...), custom_call_target="tpu_custom_call" | custom-call | flops 23592960 | bytes 1179648 | tf_op jit(solution)/shard_map/pallas_call | solution.py:782
  130.5 5.6 %collective-permute-start.16 = (bf16[256,256]{1,0:T(8,128)(2,1)}, bf16[256,256]{1,0:T(8,128)(2,1)S(1)}, u32[]{:S(2)}, u32[]{:S(2)}) collective-permute-start(bf16[256,256]{1,0:T(8,128)(2,1)} %get-tuple-element.68), channel_id=1, source_target_pairs={{0,2},{1,3},{2,4},{3,5},{4,6},{5,7},{8,10},{9,11},{10,12},{11,13},... | collective-permute-start | bytes 393224 | tf_op jit(solution)/shard_map/ppermute | solution.py:801
  136.1 1.3 collective-permute-start.17
  137.4 1.3 collective-permute-start.15
  138.7 1.1 collective-permute-done.16.refs_11_
  139.8 3.7 %collective-permute-start.14 = (bf16[256,256]{1,0:T(8,128)(2,1)}, bf16[256,256]{1,0:T(8,128)(2,1)S(1)}, u32[]{:S(2)}, u32[]{:S(2)}) collective-permute-start(bf16[256,256]{1,0:T(8,128)(2,1)} %get-tuple-element.67), channel_id=1, source_target_pairs={{0,1},{1,2},{2,3},{3,4},{4,5},{5,6},{6,7},{8,9},{9,10},{10,11},{11... | collective-permute-start | bytes 393224 | tf_op jit(solution)/shard_map/ppermute | solution.py:801
  145.1 3.4 %collective-permute-done.14.refs_9_ = bf16[256,256]{1,0:T(8,128)(2,1)S(1)} collective-permute-done((bf16[256,256]{1,0:T(8,128)(2,1)}, bf16[256,256]{1,0:T(8,128)(2,1)S(1)}, u32[]{:S(2)}, u32[]{:S(2)}) %collective-permute-start.14) | collective-permute-done | bytes 131104 | tf_op jit(solution)/shard_map/ppermute | solution.py:801
  149.5 23.3 %shard_map.75 = f32[32,32,1024]{2,1,0:T(8,128)} custom-call(s32[2]{0:T(128)} %pad_add_fusion.refs_0_, f32[24,24,512]{2,1,0:T(8,128)} %get-tuple-element.61.refs_1_, f32[24,24,512]{2,1,0:T(8,128)} %get-tuple-element.62.refs_2_, f32[24,24,512]{2,1,0:T(8,128)} %get-tuple-element.63.refs_3_, bf16[288,1024]{1,0:T(8,128)(2,1)} %copy-done, ...), custom_call_target="tpu_custom_call" | custom-call | flops 538706048 | bytes 26935304 | tf_op jit(solution)/shard_map/pallas_call | solution.py:782
  (49 shorter events, 9.0 us)
Async XLA Ops:
  8.5 15.3 %collective-permute-start = (bf16[592,384]{1,0:T(8,128)(2,1)}, bf16[592,384]{1,0:T(8,128)(2,1)S(1)}, u32[]{:S(2)}, u32[]{:S(2)}) collective-permute-start(bf16[592,384]{1,0:T(8,128)(2,1)} %get-tuple-element.38), channel_id=1, source_target_pairs={{0,8},{8,16},{16,24},{1,9},{9,17},{17,25},{2,10},{10,18},{18,26},{... | collective-permute-start | bytes 1363976 | tf_op jit(solution)/shard_map/ppermute | solution.py:801
  10.8 12.9 %collective-permute-start.1 = (bf16[592,384]{1,0:T(8,128)(2,1)}, bf16[592,384]{1,0:T(8,128)(2,1)S(1)}, u32[]{:S(2)}, u32[]{:S(2)}) collective-permute-start(bf16[592,384]{1,0:T(8,128)(2,1)} %get-tuple-element.39), channel_id=1, source_target_pairs={{8,0},{16,8},{24,16},{9,1},{17,9},{25,17},{10,2},{18,10},{26,18},{... | collective-permute-start | bytes 1363976 | tf_op jit(solution)/shard_map/ppermute | solution.py:801
  12.1 11.6 %collective-permute-start.2 = (bf16[32,256]{1,0:T(8,128)(2,1)}, bf16[32,256]{1,0:T(8,128)(2,1)S(1)}, u32[]{:S(2)}, u32[]{:S(2)}) collective-permute-start(bf16[32,256]{1,0:T(8,128)(2,1)} %get-tuple-element.44), channel_id=1, source_target_pairs={{0,16},{8,24},{16,0},{24,8},{1,17},{9,25},{17,1},{25,9},{2,18},{10... | collective-permute-start | bytes 49160 | tf_op jit(solution)/shard_map/ppermute | solution.py:808
  23.8 0.8 copy-start.4
  23.8 0.9 copy-start.5
  27.8 24.4 %collective-permute-start.3 = (bf16[640,384]{1,0:T(8,128)(2,1)}, bf16[640,384]{1,0:T(8,128)(2,1)S(1)}, u32[]{:S(2)}, u32[]{:S(2)}) collective-permute-start(bf16[640,384]{1,0:T(8,128)(2,1)} %get-tuple-element.45), channel_id=1, source_target_pairs={{0,1},{1,2},{2,3},{3,4},{4,5},{5,6},{6,7},{8,9},{9,10},{10,11},{11... | collective-permute-start | bytes 1474568 | tf_op jit(solution)/shard_map/ppermute | solution.py:801
  31.2 20.9 %collective-permute-start.4 = (bf16[640,384]{1,0:T(8,128)(2,1)}, bf16[640,384]{1,0:T(8,128)(2,1)S(1)}, u32[]{:S(2)}, u32[]{:S(2)}) collective-permute-start(bf16[640,384]{1,0:T(8,128)(2,1)} %get-tuple-element.46), channel_id=1, source_target_pairs={{1,0},{2,1},{3,2},{4,3},{5,4},{6,5},{7,6},{9,8},{10,9},{11,10},{12... | collective-permute-start | bytes 1474568 | tf_op jit(solution)/shard_map/ppermute | solution.py:801
  52.1 0.8 copy-start.2
  52.9 0.8 copy-start.3
  80.8 3.1 %collective-permute-start.5 = (bf16[288,1024]{1,0:T(8,128)(2,1)}, bf16[288,1024]{1,0:T(8,128)(2,1)S(1)}, u32[]{:S(2)}, u32[]{:S(2)}) collective-permute-start(bf16[288,1024]{1,0:T(8,128)(2,1)} %get-tuple-element.49), channel_id=1, source_target_pairs={{0,8},{8,16},{16,24},{1,9},{9,17},{17,25},{2,10},{10,18},{18,26},{... | collective-permute-start | bytes 1769480 | tf_op jit(solution)/shard_map/ppermute | solution.py:801
  82.2 4.1 %collective-permute-start.6 = (bf16[288,1024]{1,0:T(8,128)(2,1)}, bf16[288,1024]{1,0:T(8,128)(2,1)S(1)}, u32[]{:S(2)}, u32[]{:S(2)}) collective-permute-start(bf16[288,1024]{1,0:T(8,128)(2,1)} %get-tuple-element.50), channel_id=1, source_target_pairs={{8,0},{16,8},{24,16},{9,1},{17,9},{25,17},{10,2},{18,10},{26,18},{... | collective-permute-start | bytes 1769480 | tf_op jit(solution)/shard_map/ppermute | solution.py:801
  83.9 2.3 %copy-start = (bf16[288,1024]{1,0:T(8,128)(2,1)}, bf16[288,1024]{1,0:T(8,128)(2,1)S(1)}, u32[]{:S(2)}) copy-start(bf16[288,1024]{1,0:T(8,128)(2,1)S(1)} %collective-permute-done.5.mzl.refs_4_) | copy-start | bytes 1769476
  86.3 0.8 copy-start.1
  89.9 15.0 %collective-permute-start.7 = (bf16[144,512]{1,0:T(8,128)(2,1)}, bf16[144,512]{1,0:T(8,128)(2,1)S(1)}, u32[]{:S(2)}, u32[]{:S(2)}) collective-permute-start(bf16[144,512]{1,0:T(8,128)(2,1)} %get-tuple-element.59), channel_id=1, source_target_pairs={{0,1},{1,2},{2,3},{3,4},{4,5},{5,6},{6,7},{8,9},{9,10},{10,11},{11... | collective-permute-start | bytes 442376 | tf_op jit(solution)/shard_map/ppermute | solution.py:801
  94.2 10.7 %collective-permute-start.8 = (bf16[144,512]{1,0:T(8,128)(2,1)}, bf16[144,512]{1,0:T(8,128)(2,1)S(1)}, u32[]{:S(2)}, u32[]{:S(2)}) collective-permute-start(bf16[144,512]{1,0:T(8,128)(2,1)} %get-tuple-element.60), channel_id=1, source_target_pairs={{1,0},{2,1},{3,2},{4,3},{5,4},{6,5},{7,6},{9,8},{10,9},{11,10},{12... | collective-permute-start | bytes 442376 | tf_op jit(solution)/shard_map/ppermute | solution.py:801
  98.1 50.4 %collective-permute-start.10 = (bf16[240,1024]{1,0:T(8,128)(2,1)}, bf16[240,1024]{1,0:T(8,128)(2,1)S(1)}, u32[]{:S(2)}, u32[]{:S(2)}) collective-permute-start(bf16[240,1024]{1,0:T(8,128)(2,1)} %get-tuple-element.55), channel_id=1, source_target_pairs={{1,0},{2,1},{3,2},{4,3},{5,4},{6,5},{7,6},{9,8},{10,9},{11,10},{12... | collective-permute-start | bytes 1474568 | tf_op jit(solution)/shard_map/ppermute | solution.py:801
  99.4 49.1 %collective-permute-start.9 = (bf16[240,1024]{1,0:T(8,128)(2,1)}, bf16[240,1024]{1,0:T(8,128)(2,1)S(1)}, u32[]{:S(2)}, u32[]{:S(2)}) collective-permute-start(bf16[240,1024]{1,0:T(8,128)(2,1)} %get-tuple-element.56), channel_id=1, source_target_pairs={{0,1},{1,2},{2,3},{3,4},{4,5},{5,6},{6,7},{8,9},{9,10},{10,11},{11... | collective-permute-start | bytes 1474568 | tf_op jit(solution)/shard_map/ppermute | solution.py:801
  104.9 0.7 copy-start.8
  104.9 0.7 copy-start.9
  112.5 14.8 %collective-permute-start.12 = (f32[64,256]{1,0:T(8,128)}, f32[64,256]{1,0:T(8,128)S(1)}, u32[]{:S(2)}, u32[]{:S(2)}) collective-permute-start(f32[64,256]{1,0:T(8,128)} %get-tuple-element.64.own), channel_id=1, source_target_pairs={{8,0},{16,8},{24,16},{9,1},{17,9},{25,17},{10,2},{18,10},{26,18},{... | collective-permute-start | bytes 196616 | tf_op jit(solution)/shard_map/ppermute | solution.py:801
  113.8 13.5 %collective-permute-start.11 = (f32[64,256]{1,0:T(8,128)}, f32[64,256]{1,0:T(8,128)S(1)}, u32[]{:S(2)}, u32[]{:S(2)}) collective-permute-start(f32[64,256]{1,0:T(8,128)} %get-tuple-element.64.own), channel_id=1, source_target_pairs={{0,8},{8,16},{16,24},{1,9},{9,17},{17,25},{2,10},{10,18},{18,26},{... | collective-permute-start | bytes 196616 | tf_op jit(solution)/shard_map/ppermute | solution.py:801
  123.0 4.2 %collective-permute-start.13 = (f32[32,256]{1,0:T(8,128)}, f32[32,256]{1,0:T(8,128)S(1)}, u32[]{:S(2)}, u32[]{:S(2)}) collective-permute-start(f32[32,256]{1,0:T(8,128)} %get-tuple-element.65), channel_id=1, source_target_pairs={{0,16},{8,24},{16,0},{24,8},{1,17},{9,25},{17,1},{25,9},{2,18},{10... | collective-permute-start | bytes 98312 | tf_op jit(solution)/shard_map/ppermute | solution.py:808
  130.5 9.3 %collective-permute-start.16 = (bf16[256,256]{1,0:T(8,128)(2,1)}, bf16[256,256]{1,0:T(8,128)(2,1)S(1)}, u32[]{:S(2)}, u32[]{:S(2)}) collective-permute-start(bf16[256,256]{1,0:T(8,128)(2,1)} %get-tuple-element.68), channel_id=1, source_target_pairs={{0,2},{1,3},{2,4},{3,5},{4,6},{5,7},{8,10},{9,11},{10,12},{11,13},... | collective-permute-start | bytes 393224 | tf_op jit(solution)/shard_map/ppermute | solution.py:801
  136.1 8.4 %collective-permute-start.17 = (bf16[256,256]{1,0:T(8,128)(2,1)}, bf16[256,256]{1,0:T(8,128)(2,1)S(1)}, u32[]{:S(2)}, u32[]{:S(2)}) collective-permute-start(bf16[256,256]{1,0:T(8,128)(2,1)} %get-tuple-element.69), channel_id=1, source_target_pairs={{2,0},{3,1},{4,2},{5,3},{6,4},{7,5},{10,8},{11,9},{12,10},{13,11},... | collective-permute-start | bytes 393224 | tf_op jit(solution)/shard_map/ppermute | solution.py:801
  137.4 7.7 %collective-permute-start.15 = (bf16[256,256]{1,0:T(8,128)(2,1)}, bf16[256,256]{1,0:T(8,128)(2,1)S(1)}, u32[]{:S(2)}, u32[]{:S(2)}) collective-permute-start(bf16[256,256]{1,0:T(8,128)(2,1)} %get-tuple-element.67), channel_id=1, source_target_pairs={{1,0},{2,1},{3,2},{4,3},{5,4},{6,5},{7,6},{9,8},{10,9},{11,10},{12... | collective-permute-start | bytes 393224 | tf_op jit(solution)/shard_map/ppermute | solution.py:801
  139.8 8.7 %copy-start.10 = (bf16[256,256]{1,0:T(8,128)(2,1)}, bf16[256,256]{1,0:T(8,128)(2,1)S(1)}, u32[]{:S(2)}) copy-start(bf16[256,256]{1,0:T(8,128)(2,1)S(1)} %collective-permute-done.16.refs_11_) | copy-start | bytes 393220
  139.8 8.7 %collective-permute-start.14 = (bf16[256,256]{1,0:T(8,128)(2,1)}, bf16[256,256]{1,0:T(8,128)(2,1)S(1)}, u32[]{:S(2)}, u32[]{:S(2)}) collective-permute-start(bf16[256,256]{1,0:T(8,128)(2,1)} %get-tuple-element.67), channel_id=1, source_target_pairs={{0,1},{1,2},{2,3},{3,4},{4,5},{5,6},{6,7},{8,9},{9,10},{10,11},{11... | collective-permute-start | bytes 393224 | tf_op jit(solution)/shard_map/ppermute | solution.py:801
  144.5 4.0 %copy-start.11 = (bf16[256,256]{1,0:T(8,128)(2,1)}, bf16[256,256]{1,0:T(8,128)(2,1)S(1)}, u32[]{:S(2)}) copy-start(bf16[256,256]{1,0:T(8,128)(2,1)S(1)} %collective-permute-done.17.refs_12_) | copy-start | bytes 393220
  145.1 3.4 %copy-start.12 = (bf16[256,256]{1,0:T(8,128)(2,1)}, bf16[256,256]{1,0:T(8,128)(2,1)S(1)}, u32[]{:S(2)}) copy-start(bf16[256,256]{1,0:T(8,128)(2,1)S(1)} %collective-permute-done.15.refs_10_) | copy-start | bytes 393220
  148.5 0.6 copy-start.13
  148.5 0.9 copy-start.6
  148.5 1.0 copy-start.7
  (4 other events, 2.5 us)
where the time goes:
time: 174 us; the launch traced here: 173 us
  Pallas kernels  75 us (43%)
  starting transfers between devices  52.3 us (30%)
  waiting for transfers between devices  37.8 us (22%)
  local copies, waits for them, and re-layouts  6.26 us (4%)
    pallas_call x8, Pallas kernels, call(): pl.pallas_call(kernel, out_shape=tuple(outs), in_specs=[SMEM] * smem + [V...  75 us
    ppermute x16, starting transfers between devices, both_ways(): return (lax.ppermute(to_high, axis, up), lax.ppermute(to_low, axis, down))  45.7 us
    ppermute x16, waiting for transfers between devices, both_ways(): return (lax.ppermute(to_high, axis, up), lax.ppermute(to_low, axis, down))  28.6 us
    ppermute x2, waiting for transfers between devices, two_away(): came = lax.ppermute(to_low, 'gz', [(i, (i + 2) % 4) for i in range(4)])  9.2 us
    ppermute x2, starting transfers between devices, two_away(): came = lax.ppermute(to_low, 'gz', [(i, (i + 2) % 4) for i in range(4)])  6.61 us
    unnamed x36, local copies, waits for them, and re-layouts  6.26 us
  transfers between devices with their start and end apart: 18, of which 9 were waited for; matrix products, arithmetic and copies ran while one was open for 0% of the time, Pallas kernels for 7%

commit v1 on v0

--- a/solution.py
+++ b/solution.py
@@ -97,16 +97,11 @@
 
 
 BLOCK = 272
-Z_ROWS = BLOCK + 5 * 64
-X_ROWS = BLOCK + 3 * 80 + 128
-
-
-def z_part(t):
+FIRST_ROWS = BLOCK + 3 * 64
+
+
+def uptake_part(t):
     return slice(BLOCK + 64 * (t // 3), BLOCK + 64 * (t // 3) + 64), lanes(t % 3)
-
-
-def x_part(t):
-    return slice(BLOCK + 80 * (t // 3), BLOCK + 80 * (t // 3) + 80), lanes(t % 3)
 
 
 def transposed_bricks(bricks_x, ids, counts, bricks, xs, targets):
@@ -142,9 +137,19 @@
             block(3 * i + d, out, lanes(d))
 
 
-def first_kernel(bricks_x, nz, info, ids, counts, bricks, uptake, own, r1, r2, zl, zh, z2l, z2h, xl, xh, rs, xp, rs1, xp1, xs):
+def first_kernel(bricks_x, ids, counts, bricks, uptake, own, zl, zh, xs, edges, sems):
+    copies = [pltpu.make_async_copy(uptake.at[pl.ds(30 * i, 2)], edges.at[i], sems.at[i]) for i in range(2)]
+    for copy in copies:
+        copy.start()
     transposed_bricks(bricks_x, ids, counts, bricks, xs, (zl, own, zh))
-
+    for i, ref in enumerate((zl, zh)):
+        copies[i].wait()
+        for t in range(8):
+            ref[uptake_part(t)] = edges[i, :, :, lanes(t)].reshape(64, 128).astype(BF16)
+        ref[uptake_part(8)] = jnp.zeros((64, 128), BF16)
+
+
+def rates_kernel(uptake, r1, r2, xl, xh, rs, xp, rs1, xp1):
     def pair(m):
         for t in range(NT):
             both = uptake[2 * m, :, lanes(t)] + uptake[2 * m + 1, :, lanes(t)]
@@ -160,21 +165,8 @@
             xp1[t, m] = halve_rows(both, rs1, t)
 
     loop(0, 8, pair1)
-    coarse = []
     for t, tile in enumerate(halve_lanes(xp1, 8, 8)):
         r2[:, lanes(t)] = tile.reshape(64, 128)
-        coarse.append(tile.reshape(64, 128).astype(BF16))
-    low, high = far_along_z(nz, info[0], r2[0:32, :], r2[32:64, :])
-    z2l[...] = low.astype(BF16)
-    z2h[...] = high.astype(BF16)
-    for ref, u, r in ((zl, slice(0, 2), slice(0, 4)), (zh, slice(30, 32), slice(12, 16))):
-        for t in range(8):
-            ref[z_part(t)] = uptake[u, :, lanes(t)].reshape(64, 128).astype(BF16)
-        for t in range(4):
-            ref[z_part(8 + t)] = r1[r, :, lanes(t)].reshape(64, 128).astype(BF16)
-        for t in range(2):
-            ref[z_part(12 + t)] = coarse[t]
-        ref[z_part(14)] = jnp.zeros((64, 128), BF16)
 
     sub = iota((8, 1024), 0)
 
@@ -227,53 +219,26 @@
     return jnp.stack([even, odd], axis=1).reshape(-1, 8, width)
 
 
-def rates_window_kernel(own, r1, r2, uxl, uxh, zl, zh, z2l, z2h, q1, q2, xl, xh):
+def first_x_kernel(own, uxl, uxh, zl, zh, xl, xh):
     for ref, d in ((xl, 0), (xh, 2)):
         for n, src in enumerate((own, zl, zh)):
             ref[0:BLOCK, lanes(n)] = src[0:BLOCK, lanes(d)]
-    sub = iota((16, 128), 0)
+    sub = iota((8, 128), 0)
+    lows, highs = [], []
     for t in range(8):
-        rows, part = x_part(t)
-        rows = rows.start
-        xl[rows : rows + 64, part] = uxl[:, lanes(t)]
-        xh[rows : rows + 64, part] = uxh[:, lanes(t)]
-        both = [ref[z_part(t)].astype(F32) for ref in (zl, zh)]
+        xl[uptake_part(t)] = uxl[:, lanes(t)]
+        xh[uptake_part(t)] = uxh[:, lanes(t)]
+        both = [ref[uptake_part(t)].astype(F32) for ref in (zl, zh)]
         planes = [both[0][0:32], both[0][32:64], both[1][0:32], both[1][32:64]]
-        to_low, to_high = jnp.zeros((16, 128), F32), jnp.zeros((16, 128), F32)
+        to_low, to_high = jnp.zeros((8, 128), F32), jnp.zeros((8, 128), F32)
         for n, p in enumerate(planes):
             here = sub // 2 == n
-            to_low = jnp.where(here, shifted(p[0:16], 2 * n, 0), to_low)
-            to_high = jnp.where(here, shifted(p[16:32], 2 * n + 2, 0), to_high)
-        xl[rows + 64 : rows + 80, part] = to_low.astype(BF16)
-        xh[rows + 64 : rows + 80, part] = to_high.astype(BF16)
-    rows, part = x_part(8)
-    for ref in (xl, xh):
-        ref[rows, part] = jnp.zeros((80, 128), BF16)
-
-    low = jnp.concatenate([zl[z_part(8 + t)].astype(F32) for t in range(6)], axis=1)
-    high = jnp.concatenate([zh[z_part(8 + t)].astype(F32) for t in range(6)], axis=1)
-    q1[0:4, 0:16, :] = low[:, 0:512].reshape(4, 16, 512)
-    q1[4:20, 0:16, :] = r1[...]
-    q1[20:24, 0:16, :] = high[:, 0:512].reshape(4, 16, 512)
-    q1[:, 16:24, :] = jnp.zeros((24, 8, 512), F32)
-    sub1 = iota((12, 8, 512), 1)
-    first = q1[:, 0:8, :].reshape(12, 2, 8, 512)
-    last = q1[:, 8:16, :].reshape(12, 2, 8, 512)
-    to_low = halves(sub1, first[:, 0], first[:, 1]).reshape(96, 512).astype(BF16)
-    to_high = uppers(sub1, last[:, 0], last[:, 1]).reshape(96, 512).astype(BF16)
-    start = X_ROWS - 128
-    for ref, message in ((xl, to_low), (xh, to_high)):
-        for t in range(3):
-            ref[start : start + 96, lanes(t)] = message[:, lanes(t)]
-            ref[start + 96 : start + 128, lanes(t)] = message[32 * t : 32 * t + 32, lanes(3)]
-    q2[...] = window_planes(r2[...], low[:, 512:768], high[:, 512:768], z2l[...].astype(F32), z2h[...].astype(F32))
-
-
-def rates_from_x(ref):
-    start = X_ROWS - 128
-    last = jnp.concatenate([ref[start + 96 : start + 128, lanes(t)] for t in range(3)], axis=0)
-    tiles = [ref[start : start + 96, lanes(t)] for t in range(3)] + [last]
-    return jnp.concatenate([a.astype(F32) for a in tiles], axis=1).reshape(12, 8, 512)
+            to_low = jnp.where(here, shifted(p[0:8], 2 * n, 0), to_low)
+            to_high = jnp.where(here, shifted(p[24:32], 2 * n + 2, 0), to_high)
+        lows.append(to_low)
+        highs.append(to_high)
+    xl[uptake_part(8)] = jnp.concatenate(lows, axis=0).astype(BF16)
+    xh[uptake_part(8)] = jnp.concatenate(highs, axis=0).astype(BF16)
 
 
 def window_planes(own, low, high, low2, high2):
@@ -281,67 +246,26 @@
     return jnp.concatenate([a.reshape(-1, 8, 256) for a in parts], axis=0)
 
 
-def source_window_kernel(own, low, high, low2, high2, q2, window, near, fl, fh):
-    planes = window_planes(own[...], low[...], high[...], low2[...], high2[...])
-    window[...] = planes
-    near[...] = planes.reshape(256, 256).astype(BF16)
-    for i, values in enumerate((planes, q2[...])):
+def source_window_kernel(own, low, high, low2, high2, r2, zl, zh, f2, q2, near, fl, fh):
+    planes = window_planes(own[...], low[...], high[...], low2[0:32, :], high2[0:32, :])
+    f2[...] = planes
+    below, above = [ref[80:144, 512:768].astype(F32) for ref in (zl, zh)]
+    rates = window_planes(r2[...], below, above, low2[32:64, :], high2[32:64, :])
+    q2[...] = rates
+    near[0:256, :] = planes.reshape(256, 256).astype(BF16)
+    near[256:320, :] = jnp.concatenate([low2[32:64, :], high2[32:64, :]], axis=0).astype(BF16)
+    for i, values in enumerate((planes, rates)):
         to_low, to_high = far_messages(values)
         fl[128 * i : 128 * i + 128, :] = to_low.astype(BF16)
         fh[128 * i : 128 * i + 128, :] = to_high.astype(BF16)
 
 
-def pre_kernel(
-    nz, nx, info, density, uptake, own, zl, zh, xl, xh,
-    supply, c1, mzl, mzh, pxl, pxh, v_out, g_out,
-    va, vb, dd, gg, hot, rs, xp, usl, ush, sems,
-):
-    iz, ix = info[0], info[1]
-    k = spread(0)
-    base = 1.0 + 6.0 * k
-    O = 5
-    Q = 2
-
-    for p in (0, 1, 2, 3, 4, 37, 38, 39, 40, 41):
-        va[p] = jnp.zeros((40, 1024), F32)
-    for p in (2, 3, 38, 39):
-        vb[p] = jnp.zeros((40, 1024), F32)
-
-    sub8 = iota((8, 1024), 0)
-
-    for t in range(NT):
-        usl[:, lanes(t)] = xl[x_part(t)].astype(F32)
-        ush[:, lanes(t)] = xh[x_part(t)].astype(F32)
-
-    def set_plane(q, rates, low, high, valid_z):
-        gz = jnp.where(valid_z, OMEGA, 0.0)
-        d = rates + base
-        dd[q, 0:32, :] = d
-        gg[q, 0:32, :] = gz / d
-        d = jnp.where(sub8 < 2, high, jnp.where(sub8 >= 6, low, 0.0)) + base
-        dd[q, 32:40, :] = d
-        omega = jnp.where(sub8 < 2, jnp.where(ix < nx - 1, gz, 0.0), jnp.where(sub8 >= 6, jnp.where(ix > 0, gz, 0.0), 0.0))
-        gg[q, 32:40, :] = omega / d
-
-    def own_planes(i):
-        rows = pl.ds(pl.multiple_of(8 * i, 8), 8)
-        low, high = usl[rows, :], ush[rows, :]
-        for n in range(4):
-            z = 4 * i + n
-            va[z + O, 0:32, :] = density[z]
-            va[z + O, 32:40, :] = jnp.zeros((8, 1024), F32)
-            set_plane(z + Q, uptake[z], shifted(low, 6 - 2 * n, 0), shifted(high, -2 * n, 0), True)
-
-    loop(0, C // 4, own_planes)
-    low, high = usl[64:72, :], ush[64:72, :]
-    for n in range(4):
-        ref = zl if n < 2 else zh
-        rates = [ref[z_part(t)].astype(F32)[32 * (n % 2) : 32 * (n % 2) + 32] for t in range(NT)]
-        rates = jnp.concatenate(rates, axis=1)
-        exists = iz > 0 if n < 2 else iz < nz - 1
-        set_plane(n if n < 2 else 32 + n, rates, shifted(low, 6 - 2 * n, 0), shifted(high, -2 * n, 0), exists)
-
-    blocks = [(ref, lanes(1)) for ref in (own, zl, zh)] + [(ref, lanes(n)) for ref in (xl, xh) for n in range(3)]
+O = 5
+Q = 2
+BASE = 1.0 + 6.0 * KAPPA
+
+
+def spots(blocks, hot):
     lane = iota((1, 128), 1)
     at_y = iota((1024, 128), 0)
     tiles = []
@@ -350,42 +274,152 @@
         tiles.append(lax.shift_right_logical(name, 6))
         y = (name & 63) * 16 + (lane & 15)
         hot[:, lanes(i)] = jnp.where(at_y == y, 1.0, 0.0).astype(BF16)
+    return tiles
+
+
+def scatter(blocks, hot):
+    tiles = spots(blocks, hot)
     for tile in range(4):
         bz, bx = tile // 2, tile % 2
-        left = jnp.concatenate(
-            [jnp.where(tiles[i] == tile, ref[0:256, part].astype(F32), 0.0).astype(BF16) for i, (ref, part) in enumerate(blocks)],
-            axis=1,
-        )
+        left = [
+            jnp.where(tiles[i] == tile, ref[0:256, part].astype(F32), 0.0).astype(BF16)
+            for i, (ref, part) in enumerate(blocks)
+        ]
+        left = jnp.concatenate(left, axis=1)
         for n in range(4):
             cols = slice(n * 256, (n + 1) * 256)
-            part = lax.dot_general(left, hot[cols, :], (((1,), (1,)), ((), ())), preferred_element_type=F32)
-            zs, xs = slice(16 * bz, 16 * bz + 16), slice(16 * bx, 16 * bx + 16)
-            supply[zs, xs, cols] = density[zs, xs, cols] + part.reshape(16, 16, 256)
-
-    def sweep(src, dst, z, sourced):
-        for t, here, sums in plane(src, z + O):
-            inner = k * sums
-            g = gg[z + Q, :, lanes(t)]
-            if sourced:
-                body = inner[0:32] + supply[z, :, lanes(t)]
-                dst[z + O, 0:32, lanes(t)] = KEEP * here[0:32] + g[0:32] * body
-                dst[z + O, 32:40, lanes(t)] = KEEP * here[32:40] + g[32:40] * inner[32:40]
-            else:
-                dst[z + O, :, lanes(t)] = KEEP * here + g * inner
-
-    def halo_planes(src, dst, width):
-        def step(i):
-            sweep(src, dst, jnp.where(i < width, i - width, i - width + C), False)
-
-        loop(0, 2 * width, step)
-
-    loop(0, C, lambda z: sweep(va, vb, z, True), 2)
-    halo_planes(va, vb, 1)
-    loop(0, C, lambda z: sweep(vb, va, z, True), 2)
-    halo_planes(vb, va, 2)
-
-    v_copy = pltpu.make_async_copy(va.at[3:39], v_out, sems.at[0])
-    g_copy = pltpu.make_async_copy(gg, g_out, sems.at[1])
+            sums = lax.dot_general(left, hot[cols, :], (((1,), (1,)), ((), ())), preferred_element_type=F32)
+            yield 16 * bz, slice(16 * bx, 16 * bx + 16), cols, sums.reshape(16, 16, 256)
+
+
+def sweep(src, dst, source, gg, z, sourced):
+    for t, here, sums in plane(src, z + O):
+        inner = KAPPA * sums
+        g = gg[z + Q, :, lanes(t)]
+        if sourced:
+            body = inner[0:32] + source[z, :, lanes(t)]
+            dst[z + O, 0:32, lanes(t)] = KEEP * here[0:32] + g[0:32] * body
+            dst[z + O, 32:40, lanes(t)] = KEEP * here[32:40] + g[32:40] * inner[32:40]
+        else:
+            dst[z + O, :, lanes(t)] = KEEP * here + g * inner
+
+
+def own_kernel(nz, info, density, uptake, own, zl, zh, s0, g0, d0, v1, edge, va, hot):
+    iz = info[0]
+    for p in (3, 4, 37, 38):
+        va[p] = jnp.zeros((40, 1024), F32)
+
+    def own_plane(z):
+        va[z + O, 0:32, :] = density[z]
+        va[z + O, 32:40, :] = jnp.zeros((8, 1024), F32)
+        d = uptake[z] + BASE
+        d0[z + Q] = d
+        g0[z + Q] = OMEGA / d
+
+    loop(0, C, own_plane)
+    for n in range(4):
+        ref, valid = (zl, iz > 0) if n < 2 else (zh, iz < nz - 1)
+        q = n if n < 2 else 32 + n
+        rows = slice(32 * (n % 2), 32 * (n % 2) + 32)
+        for t in range(NT):
+            d = ref[uptake_part(t)].astype(F32)[rows] + BASE
+            d0[q, :, lanes(t)] = d
+            g0[q, :, lanes(t)] = jnp.where(valid, OMEGA, 0.0) / d
+
+    blocks = [(ref, lanes(1)) for ref in (own, zl, zh)]
+    for z, rows, cols, sums in scatter(blocks, hot):
+        planes = slice(z, z + 16)
+        s0[planes, rows, cols] = density[planes, rows, cols] + sums
+
+    def first(z):
+        for t, here, sums in plane(va, z + O):
+            inner = KAPPA * sums
+            body = inner[0:32] + s0[z, :, lanes(t)]
+            v1[z + 1, :, lanes(t)] = KEEP * here[0:32] + g0[z + Q, :, lanes(t)] * body
+            edge[z, :, lanes(t)] = inner[32:40]
+
+    loop(0, C, first, 2)
+    for z in (-1, C):
+        for t in range(NT):
+            near = va[z + O + (1 if z < 0 else -1), 0:32, lanes(t)]
+            v1[z + 1, :, lanes(t)] = g0[z + Q, :, lanes(t)] * (KAPPA * near)
+
+
+def pre_kernel(
+    nz, nx, info, xl, xh, r1, r2, s0, g0, d0, v1, edge_in,
+    supply, c1, mzl, mzh, pxl, pxh, v_out, g_out,
+    va, vb, dd, gg, edge, hot, rs, xp, usl, ush, sems,
+):
+    iz, ix = info[0], info[1]
+    k = KAPPA
+    loads = [
+        pltpu.make_async_copy(src, dst, sems.at[i])
+        for i, (src, dst) in enumerate(
+            (
+                (s0, supply),
+                (v1, vb.at[4:38, 0:32, :]),
+                (g0, gg.at[:, 0:32, :]),
+                (edge_in, edge),
+                (d0, dd.at[:, 0:32, :]),
+            )
+        )
+    ]
+    for copy in loads:
+        copy.start()
+
+    for p in (1, 2, 39, 40):
+        va[p] = jnp.zeros((40, 1024), F32)
+    for p in (2, 3, 38, 39):
+        vb[p] = jnp.zeros((40, 1024), F32)
+    for p in (4, 37):
+        vb[p, 32:40, :] = jnp.zeros((8, 1024), F32)
+
+    sub8 = iota((8, 1024), 0)
+    for t in range(NT):
+        usl[0:64, lanes(t)] = xl[uptake_part(t)].astype(F32)
+        ush[0:64, lanes(t)] = xh[uptake_part(t)].astype(F32)
+        usl[64:72, lanes(t)] = xl[uptake_part(8)].astype(F32)[8 * t : 8 * t + 8]
+        ush[64:72, lanes(t)] = xh[uptake_part(8)].astype(F32)[8 * t : 8 * t + 8]
+
+    def set_halo(q, low, high, valid_z):
+        gz = jnp.where(valid_z, OMEGA, 0.0)
+        d = jnp.where(sub8 < 2, high, jnp.where(sub8 >= 6, low, 0.0)) + BASE
+        dd[q, 32:40, :] = d
+        omega = jnp.where(sub8 < 2, jnp.where(ix < nx - 1, gz, 0.0), jnp.where(sub8 >= 6, jnp.where(ix > 0, gz, 0.0), 0.0))
+        gg[q, 32:40, :] = omega / d
+
+    def halos(i):
+        rows = pl.ds(pl.multiple_of(8 * i, 8), 8)
+        low, high = usl[rows, :], ush[rows, :]
+        for n in range(4):
+            set_halo(4 * i + n + Q, shifted(low, 6 - 2 * n, 0), shifted(high, -2 * n, 0), True)
+
+    loop(0, C // 4, halos)
+    low, high = usl[64:72, :], ush[64:72, :]
+    for n in range(4):
+        exists = iz > 0 if n < 2 else iz < nz - 1
+        set_halo(n if n < 2 else 32 + n, shifted(low, 6 - 2 * n, 0), shifted(high, -2 * n, 0), exists)
+
+    blocks = [(ref, lanes(n)) for ref in (xl, xh) for n in range(3)]
+    waiting = list(loads[0:3])
+    for z, rows, cols, sums in scatter(blocks, hot):
+        while waiting:
+            waiting.pop().wait()
+        supply[z : z + 16, rows, cols] = supply[z : z + 16, rows, cols] + sums
+        g = gg[z + Q : z + Q + 16, rows, cols]
+        vb[z + O : z + O + 16, rows, cols] = vb[z + O : z + O + 16, rows, cols] + g * sums
+    loads[3].wait()
+
+    def edges(z):
+        vb[z + O, 32:40, :] = gg[z + Q, 32:40, :] * edge[z]
+
+    loop(0, C, edges)
+
+    loop(0, C, lambda z: sweep(vb, va, supply, gg, z, True), 2)
+    loop(0, 4, lambda i: sweep(vb, va, supply, gg, jnp.where(i < 2, i - 2, i + C - 2), False))
+    loads[4].wait()
+    v_copy = pltpu.make_async_copy(va.at[3:39], v_out, sems.at[5])
+    g_copy = pltpu.make_async_copy(gg, g_out, sems.at[6])
     v_copy.start()
     g_copy.start()
 
@@ -421,13 +455,20 @@
 
     empty = jnp.zeros((1, 8, 1024), F32)
     blank = jnp.zeros((8, 1024), F32)
-    for ref, planes, values, z in ((mzl, slice(0, 6), va[3:7], 0), (mzh, slice(14, 20), va[35:39], 31)):
+    edges = (
+        (mzl, slice(0, 6), slice(0, 4), va[3:7], 0),
+        (mzh, slice(14, 20), slice(12, 16), va[35:39], 31),
+    )
+    for ref, planes, rates, values, z in edges:
         source = c1[planes].reshape(144, 512)
         ref[0:80, 0:512] = source[0:80].astype(BF16)
         ref[0:64, 512:1024] = source[80:144].astype(BF16)
         ref[64:80, 512:1024] = jnp.zeros((16, 512), BF16)
+        ref[80:144, 0:512] = r1[rates].reshape(64, 512).astype(BF16)
+        ref[80:144, 512:768] = r2[...].astype(BF16)
+        ref[80:144, 768:1024] = jnp.zeros((64, 256), BF16)
         level0 = jnp.concatenate([values, jnp.concatenate([supply[z : z + 1], empty], axis=1)], axis=0)
-        ref[80:288, :] = jnp.concatenate([level0.reshape(200, 1024), blank], axis=0).astype(BF16)
+        ref[144:352, :] = jnp.concatenate([level0.reshape(200, 1024), blank], axis=0).astype(BF16)
 
     def sides(i):
         lows, highs = [], []
@@ -480,13 +521,14 @@
     return pack_pair(sub, a, b)
 
 
-def sides_kernel(pxl, pxh, mzl, mzh, q2, out_l, out_h):
+def sides_kernel(pxl, pxh, mzl, mzh, r2, out_l, out_h):
     for ref, out in ((pxl, out_l), (pxh, out_h)):
         out[0:176, :] = ref[...]
-        for n in range(4):
-            out[176:240, n * 256 : n * 256 + 256] = q2[8 * n : 8 * n + 8].reshape(64, 256).astype(BF16)
+        for n, rates in enumerate((mzl[80:144, 512:768], r2[...].astype(BF16), mzh[80:144, 512:768])):
+            out[176:240, n * 256 : n * 256 + 256] = rates
+        out[176:240, 768:1024] = jnp.zeros((64, 256), BF16)
     for message, start in ((mzl, 0), (mzh, 128)):
-        planes = message[80:240, :].astype(F32).reshape(4, 40, 1024)
+        planes = message[144:304, :].astype(F32).reshape(4, 40, 1024)
         rows = slice(start, start + 16)
         for ref, out, pack in ((pxl, out_l, pack_low), (pxh, out_h, pack_high)):
             added = [pack(planes[2 * i], planes[2 * i + 1]) for i in range(2)]
@@ -514,7 +556,7 @@
 LOW_PACK = (4, (-2, 4, 2))
 
 
-def merge_kernel(c1, mzl, mzh, f1, mxl, mxh):
+def merge_kernel(c1, r1, mzl, mzh, f1, q1, mxl, mxh):
     zeros = jnp.zeros((24, 512), F32)
     for p in (0, 1, 22, 23):
         f1[p] = zeros
@@ -527,26 +569,34 @@
     sub4 = iota((6, 4, 8, 512), 2)
     to_high = in_three(sub, jnp.where(sub4 >= 4, last, halo), *HIGH_PACK)
     to_low = in_three(sub, jnp.where(sub4 >= 4, halo, first), *LOW_PACK)
-    mxh[...] = to_high.reshape(144, 512).astype(BF16)
-    mxl[...] = to_low.reshape(144, 512).astype(BF16)
-
-
-def middle_kernel(nz, nx, info, f0, q_in, xl, xh, mxl, mxh, f1, g1, v1, g2, g2l, g2h, q0, va, rs, xp):
+    mxh[0:144, :] = to_high.reshape(144, 512).astype(BF16)
+    mxl[0:144, :] = to_low.reshape(144, 512).astype(BF16)
+    q1[0:4] = mzl[80:144, 0:512].astype(F32).reshape(4, 16, 512)
+    q1[4:20] = r1[...]
+    q1[20:24] = mzh[80:144, 0:512].astype(F32).reshape(4, 16, 512)
+    sub1 = iota((12, 8, 512), 1)
+    first = q1[:, 0:8, :].reshape(12, 2, 8, 512)
+    last = q1[:, 8:16, :].reshape(12, 2, 8, 512)
+    mxl[144:240, :] = halves(sub1, first[:, 0], first[:, 1]).reshape(96, 512).astype(BF16)
+    mxh[144:240, :] = uppers(sub1, last[:, 0], last[:, 1]).reshape(96, 512).astype(BF16)
+
+
+def middle_kernel(nz, nx, info, f0, q_in, r2, mxl, mxh, f1, g1, v1, g2, g2l, g2h, q0, va, rs, xp):
     iz, ix = info[0], info[1]
     k = spread(1)
     base = 1.0 + 6.0 * k
     sub6 = iota((6, 8, 512), 1)
-    low = out_of_three(sub6, mxl[...].astype(F32).reshape(6, 3, 8, 512), *HIGH_PACK).reshape(24, 8, 512)
-    high = out_of_three(sub6, mxh[...].astype(F32).reshape(6, 3, 8, 512), *LOW_PACK).reshape(24, 8, 512)
+    low = out_of_three(sub6, mxl[0:144, :].astype(F32).reshape(6, 3, 8, 512), *HIGH_PACK).reshape(24, 8, 512)
+    high = out_of_three(sub6, mxh[0:144, :].astype(F32).reshape(6, 3, 8, 512), *LOW_PACK).reshape(24, 8, 512)
     sub = iota((24, 8, 512), 1)
     f1[:, 0:8] = f0[:, 0:8] + jnp.where(sub < 2, low, 0.0)
     f1[:, 8:16] = f0[:, 8:16] + jnp.where(sub >= 6, high, 0.0)
     f1[:, 16:24] = f0[:, 16:24] + jnp.where(sub >= 4, low, high)
-    low, high = rates_from_x(xl), rates_from_x(xh)
+    low, high = [ref[144:240, :].astype(F32).reshape(12, 8, 512) for ref in (mxl, mxh)]
     sub12 = iota((12, 8, 512), 1)
     even = jnp.where(sub12 >= 4, shifted(low, 4, 1), high)
     odd = jnp.where(sub12 >= 4, low, shifted(high, 4, 1))
-    q0[:, 0:16] = q_in[:, 0:16]
+    q0[:, 0:16] = q_in[...]
     q0[:, 16:24] = jnp.stack([even, odd], axis=1).reshape(24, 8, 512)
     shape = (24, 24, 128)
     valid = inside(shape, 0, -4, None, iz, 16, nz) & inside(shape, 1, 0, 20, ix, 16, nx)
@@ -575,8 +625,11 @@
     for t, tile in enumerate(halve_lanes(xp, 8, 8)):
         g2[:, lanes(t)] = tile.reshape(64, 128)
         low, high = far_along_z(nz, iz, tile[0:4].reshape(32, 128), tile[4:8].reshape(32, 128))
-        g2l[:, lanes(t)] = low
-        g2h[:, lanes(t)] = high
+        g2l[0:32, lanes(t)] = low
+        g2h[0:32, lanes(t)] = high
+    low, high = far_along_z(nz, iz, r2[0:32, :], r2[32:64, :])
+    g2l[32:64, :] = low
+    g2h[32:64, :] = high
 
 
 def back_kernel(
@@ -595,14 +648,18 @@
         copy.start()
 
     f2[:, 0:8, :] = own2[...]
-    f2[:, 8:16, :] = n2h[...].astype(F32).reshape(32, 8, 256)
+    f2[:, 8:16, :] = n2h[0:256, :].astype(F32).reshape(32, 8, 256)
     f2[:, 16:24, :] = far_tile(m2l[0:128, :].astype(F32), m2h[0:128, :].astype(F32))
-    f2[:, 24:32, :] = n2l[...].astype(F32).reshape(32, 8, 256)
+    f2[:, 24:32, :] = n2l[0:256, :].astype(F32).reshape(32, 8, 256)
     q2[:, 0:8, :] = q_own[...]
     q2[:, 16:24, :] = far_tile(m2l[128:256, :].astype(F32), m2h[128:256, :].astype(F32))
     for ref, rows in ((vxh, slice(8, 16)), (vxl, slice(24, 32))):
-        for n in range(4):
-            q2[8 * n : 8 * n + 8, rows, :] = ref[176:240, n * 256 : n * 256 + 256].astype(F32).reshape(8, 8, 256)
+        for n in range(3):
+            q2[8 * n + 4 : 8 * n + 12, rows, :] = ref[176:240, n * 256 : n * 256 + 256].astype(F32).reshape(8, 8, 256)
+    for ref, rows in ((n2h, slice(8, 16)), (n2l, slice(24, 32))):
+        outer = ref[256:320, :].astype(F32).reshape(8, 8, 256)
+        q2[0:4, rows, :] = outer[0:4]
+        q2[28:32, rows, :] = outer[4:8]
 
     k = spread(2)
     base = 1.0 + 6.0 * k
@@ -704,8 +761,8 @@
 
     for copy in level0:
         copy.wait()
-    zsl[...] = vzl[80:288, :].astype(F32)
-    zsh[...] = vzh[80:288, :].astype(F32)
+    zsl[...] = vzl[144:352, :].astype(F32)
+    zsh[...] = vzh[144:352, :].astype(F32)
     for i in range(4):
         v2[i] = v2[i] + zsl[40 * i : 40 * i + 40, :]
         v2[32 + i] = v2[32 + i] + zsh[40 * i : 40 * i + 40, :]
@@ -816,27 +873,35 @@
     half = lambda *shape: shaped(shape, BF16)
     full = lambda *shape: shaped(shape, F32)
 
-    own, r1, r2, zl, zh, z2l, z2h, uxl, uxh = call(
-        lambda *refs: first_kernel(2 * nx, nz, *refs),
-        [
-            half(BLOCK, 384), full(16, 16, 512), full(64, 256), half(Z_ROWS, 384), half(Z_ROWS, 384),
-            half(32, 256), half(32, 256), half(64, 1024), half(64, 1024),
-        ],
-        [
-            scratch((8, 32, 128), F32), scratch((8, 16, 16, 128), F32), scratch((4, 16, 128), F32),
-            scratch((4, 8, 8, 128), F32), scratch((SLOTS, BRICK), F32),
-        ],
-        3,
-        (info, brick_ids, slot_counts, brick_values, uptake),
+    own, zl, zh = call(
+        lambda *refs: first_kernel(2 * nx, *refs),
+        [half(BLOCK, 384), half(FIRST_ROWS, 384), half(FIRST_ROWS, 384)],
+        [scratch((SLOTS, BRICK), F32), scratch((2, 2, C, 1024), F32), pltpu.SemaphoreType.DMA((2,))],
+        2,
+        (brick_ids, slot_counts, brick_values, uptake),
+        in_hbm=1,
     )
     zl, zh = both_ways(zl, zh, "gz")
-    z2l, z2h = two_away(z2l, z2h)
-    q1, q2, xl, xh = call(
-        rates_window_kernel,
-        [full(24, 24, 512), full(32, 8, 256), half(X_ROWS, 384), half(X_ROWS, 384)],
+    r1, r2, uxl, uxh = call(
+        rates_kernel,
+        [full(16, 16, 512), full(64, 256), half(64, 1024), half(64, 1024)],
+        [scratch((8, 32, 128), F32), scratch((8, 16, 16, 128), F32), scratch((4, 16, 128), F32), scratch((4, 8, 8, 128), F32)],
+        0,
+        (lax.optimization_barrier((uptake, own))[0],),
+    )
+    xl, xh = call(
+        first_x_kernel,
+        [half(FIRST_ROWS, 384), half(FIRST_ROWS, 384)],
         [],
         0,
-        (own, r1, r2, uxl, uxh, zl, zh, z2l, z2h),
+        (own, uxl, uxh, zl, zh),
+    )
+    s0, g0, d0, v1, edge = call(
+        lambda *refs: own_kernel(nz, *refs),
+        [full(C, C, 1024), full(36, C, 1024), full(36, C, 1024), full(34, C, 1024), full(C, 8, 1024)],
+        [scratch((42, 40, 1024), F32), scratch((1024, 384), BF16)],
+        1,
+        (info, density, uptake, own, zl, zh),
     )
     xl, xh = both_ways(xl, xh, "xy")
 
@@ -845,8 +910,8 @@
         [
             full(C, C, 1024),
             full(20, 24, 512),
-            half(288, 1024),
-            half(288, 1024),
+            half(352, 1024),
+            half(352, 1024),
             half(176, 1024),
             half(176, 1024),
             full(36, 40, 1024),
@@ -857,24 +922,26 @@
             scratch((42, 40, 1024), F32),
             scratch((36, 40, 1024), F32),
             scratch((36, 40, 1024), F32),
-            scratch((1024, 1152), BF16),
+            scratch((C, 8, 1024), F32),
+            scratch((1024, 768), BF16),
             scratch((8, 40, 128), F32),
             scratch((8, 20, 24, 128), F32),
-            scratch((80, 1024), F32),
-            scratch((80, 1024), F32),
-            pltpu.SemaphoreType.DMA((2,)),
+            scratch((72, 1024), F32),
+            scratch((72, 1024), F32),
+            pltpu.SemaphoreType.DMA((7,)),
         ],
         1,
-        (info, density, uptake, own, zl, zh, xl, xh),
+        (info, xl, xh, r1, r2, s0, g0, d0, v1, edge),
         [VMEM] * 6 + [ANY] * 2,
+        in_hbm=5,
     )
     mzl, mzh = both_ways(mzl, mzh, "gz")
-    f1, mxl, mxh = call(
+    f1, q1, mxl, mxh = call(
         merge_kernel,
-        [full(24, 24, 512), half(144, 512), half(144, 512)],
+        [full(24, 24, 512), full(24, 16, 512), half(240, 512), half(240, 512)],
         [],
         0,
-        (c1, mzl, mzh),
+        (c1, r1, mzl, mzh),
     )
     mxl, mxh = both_ways(mxl, mxh, "xy")
     pxl, pxh = call(
@@ -882,25 +949,25 @@
         [half(240, 1024), half(240, 1024)],
         [],
         0,
-        (pxl, pxh, mzl, mzh, q2),
+        (pxl, pxh, mzl, mzh, r2),
     )
     vxl, vxh = both_ways(pxl, pxh, "xy")
     f1, pxl, pxh = lax.optimization_barrier((f1, pxl, pxh))
     f1, g1, v1, g2, g2l, g2h = call(
         lambda *refs: middle_kernel(nz, nx, *refs),
-        [full(24, 24, 512), full(24, 24, 512), full(24, 24, 512), full(64, 256), full(32, 256), full(32, 256)],
+        [full(24, 24, 512), full(24, 24, 512), full(24, 24, 512), full(64, 256), full(64, 256), full(64, 256)],
         [scratch((24, 24, 512), F32), scratch((24, 24, 512), F32), scratch((4, 16, 128), F32), scratch((4, 8, 8, 128), F32)],
         1,
-        (info, f1, q1, xl, xh, mxl, mxh),
+        (info, f1, q1, r2, mxl, mxh),
     )
     low, high = both_ways(g2, g2, "gz")
     low2, high2 = two_away(g2l, g2h)
-    own2, near, fl, fh = call(
+    own2, q2, near, fl, fh = call(
         source_window_kernel,
-        [full(32, 8, 256), half(256, 256), half(256, 256), half(256, 256)],
+        [full(32, 8, 256), full(32, 8, 256), half(320, 256), half(256, 256), half(256, 256)],
         [],
         0,
-        (g2, low, high, low2, high2, q2),
+        (g2, low, high, low2, high2, r2, mzl, mzh),
     )
     nl, nh = both_ways(near, near, "xy")
     fl, fh = both_ways(fl, fh, "xy", 2)

time: 174 us -> 172 us (0.989)
  waiting for transfers between devices: 37.8 us -> 10.3 us
  Pallas kernels: 75 us -> 89 us
  starting transfers between devices: 52.3 us -> 65 us
    ppermute x16, waiting for transfers between devices: 28.6 us -> 10.3 us  [both_ways(): return (lax.ppermute(to_high, axis, up), lax.ppermute(to_low, axis, down))]
    pallas_call x8 -> x10, Pallas kernels: 75 us -> 89 us  [call(): pl.pallas_call(kernel, out_shape=tuple(outs), in_specs=[SMEM] * smem + [V...]
    ppermute x2 -> x1, starting transfers between devices: 6.61 us -> 17.4 us  [two_away(): came = lax.ppermute(to_low, 'gz', [(i, (i + 2) % 4) for i in range(4)])]
    ppermute x2 -> x1, waiting for transfers between devices: 9.2 us -> 0.01 us  [two_away(): came = lax.ppermute(to_low, 'gz', [(i, (i + 2) % 4) for i in range(4)])]
    ppermute x16, starting transfers between devices: 45.7 us -> 47.5 us  [both_ways(): return (lax.ppermute(to_high, axis, up), lax.ppermute(to_low, axis, down))]
    unnamed x36 -> x34, local copies, waits for them, and re-layouts: 6.26 us -> 5.03 us
  transfers between devices with their start and end apart: 18 -> 17, of which waited for: 9 -> 5; matrix products, arithmetic and copies ran while one was open for 0% -> 0% of each run, Pallas kernels for 7% -> 19%
where the time goes in v1:
time: 172 us; the launch traced here: 171 us
  Pallas kernels  89 us (52%)
  starting transfers between devices  65 us (38%)
  waiting for transfers between devices  10.3 us (6%)
  local copies, waits for them, and re-layouts  5.03 us (3%)
    pallas_call x10, Pallas kernels, call(): pl.pallas_call(kernel, out_shape=tuple(outs), in_specs=[SMEM] * smem + [V...  89 us
    ppermute x16, starting transfers between devices, both_ways(): return (lax.ppermute(to_high, axis, up), lax.ppermute(to_low, axis, down))  47.5 us
    ppermute x1, starting transfers between devices, two_away(): came = lax.ppermute(to_low, 'gz', [(i, (i + 2) % 4) for i in range(4)])  17.4 us
    ppermute x16, waiting for transfers between devices, both_ways(): return (lax.ppermute(to_high, axis, up), lax.ppermute(to_low, axis, down))  10.3 us
    unnamed x34, local copies, waits for them, and re-layouts  5.03 us
  transfers between devices with their start and end apart: 17, of which 5 were waited for; matrix products, arithmetic and copies ran while one was open for 0% of the time, Pallas kernels for 19%

profile of v1, /device:TPU:0, one launch (start us, length us, event | category | flops | bytes accessed | tf_op | source)
XLA Modules:
  0.0 171.1 jit_solution(1845797092487450661)
XLA Ops:
  0.6 4.7 %shard_map.68 = (bf16[272,384]{1,0:T(8,128)(2,1)}, bf16[464,384]{1,0:T(8,128)(2,1)}, bf16[464,384]{1,0:T(8,128)(2,1)}) custom-call(s32[72]{0:T(128)} %refs_0_.1, s32[1,9]{1,0:T(1,128)} %refs_1_.2, bf16[72,4096]{1,0:T(8,128)(2,1)} %refs_2_.2, f32[32,32,1024]{2,1,0:T(8,128)} %refs_2_.3), custom_call_target="tpu_custom_call" | custom-call | flops 114121040 | bytes 5706052 | tf_op jit(solution)/shard_map/pallas_call | solution.py:839
  5.3 2.4 %collective-permute-start = (bf16[464,384]{1,0:T(8,128)(2,1)}, bf16[464,384]{1,0:T(8,128)(2,1)S(1)}, u32[]{:S(2)}, u32[]{:S(2)}) collective-permute-start(bf16[464,384]{1,0:T(8,128)(2,1)} %get-tuple-element.46), channel_id=1, source_target_pairs={{0,8},{8,16},{16,24},{1,9},{9,17},{17,25},{2,10},{10,18},{18,26},{... | collective-permute-start | bytes 1069064 | tf_op jit(solution)/shard_map/ppermute | solution.py:858
  7.7 1.3 collective-permute-start.1
  9.0 4.5 %shard_map.69 = (f32[16,16,512]{2,1,0:T(8,128)}, f32[64,256]{1,0:T(8,128)}, bf16[64,1024]{1,0:T(8,128)(2,1)}, bf16[64,1024]{1,0:T(8,128)(2,1)}) custom-call(f32[32,32,1024]{2,1,0:T(8,128)} %refs_2_.3), custom_call_target="tpu_custom_call" | custom-call | flops 100925440 | bytes 5046272 | tf_op jit(solution)/shard_map/pallas_call | solution.py:839
  14.4 2.3 %shard_map.70 = (bf16[464,384]{1,0:T(8,128)(2,1)}, bf16[464,384]{1,0:T(8,128)(2,1)}) custom-call(bf16[272,384]{1,0:T(8,128)(2,1)} %get-tuple-element.42.own.refs_3_, bf16[64,1024]{1,0:T(8,128)(2,1)} %get-tuple-element.44.uxl, bf16[64,1024]{1,0:T(8,128)(2,1)} %get-tuple-element.45.uxh, bf16[464,384]{1,0:T(8,128)(2,1)} %copy-done.2, bf16[464,384]{1,0:T(8,128)(2,1)} %copy-done.3), custom_call_target="tpu_custom_call" | custom-call | flops 37928960 | bytes 1896448 | tf_op jit(solution)/shard_map/pallas_call | solution.py:839
  16.7 4.2 %collective-permute-start.2 = (bf16[464,384]{1,0:T(8,128)(2,1)}, bf16[464,384]{1,0:T(8,128)(2,1)S(1)}, u32[]{:S(2)}, u32[]{:S(2)}) collective-permute-start(bf16[464,384]{1,0:T(8,128)(2,1)} %get-tuple-element.48), channel_id=1, source_target_pairs={{0,1},{1,2},{2,3},{3,4},{4,5},{5,6},{6,7},{8,9},{9,10},{10,11},{11... | collective-permute-start | bytes 1069064 | tf_op jit(solution)/shard_map/ppermute | solution.py:858
  20.9 1.3 collective-permute-start.3
  22.8 16.7 %shard_map.71 = (f32[32,32,1024]{2,1,0:T(8,128)}, f32[36,32,1024]{2,1,0:T(8,128)}, f32[36,32,1024]{2,1,0:T(8,128)}, f32[34,32,1024]{2,1,0:T(8,128)}, f32[32,8,1024]{2,1,0:T(8,128)}) custom-call(s32[2]{0:T(128)} %pad_add_fusion.refs_0_, f32[32,32,1024]{2,1,0:T(8,128)} %refs_1_.3, f32[32,32,1024]{2,1,0:T(8,128)} %refs_2_.3, ...), custom_call_target="tpu_custom_call" | custom-call | flops 568934528 | bytes 28446728 | tf_op jit(solution)/shard_map/pallas_call | solution.py:839
  39.5 0.7 copy-done.6
  40.4 22.5 %shard_map.72 = (f32[32,32,1024]{2,1,0:T(8,128)}, f32[20,24,512]{2,1,0:T(8,128)}, bf16[352,1024]{1,0:T(8,128)(2,1)}, bf16[352,1024]{1,0:T(8,128)(2,1)}, bf16[176...) custom-call(s32[2]{0:T(128)} %pad_add_fusion.refs_0_, ...), custom_call_target="tpu_custom_call" | custom-call | flops 791511168 | bytes 39575560 | tf_op jit(solution)/shard_map/pallas_call | solution.py:839
  62.9 6.4 %collective-permute-start.4 = (bf16[352,1024]{1,0:T(8,128)(2,1)}, bf16[352,1024]{1,0:T(8,128)(2,1)S(1)}, u32[]{:S(2)}, u32[]{:S(2)}) collective-permute-start(bf16[352,1024]{1,0:T(8,128)(2,1)} %get-tuple-element.59), channel_id=1, source_target_pairs={{0,8},{8,16},{16,24},{1,9},{9,17},{17,25},{2,10},{10,18},{18,26},{... | collective-permute-start | bytes 2162696 | tf_op jit(solution)/shard_map/ppermute | solution.py:858
  69.3 1.3 collective-permute-start.5
  71.3 2.3 %collective-permute-done.5.mzh.zh.refs_5_ = bf16[352,1024]{1,0:T(8,128)(2,1)S(1)} collective-permute-done((bf16[352,1024]{1,0:T(8,128)(2,1)}, bf16[352,1024]{1,0:T(8,128)(2,1)S(1)}, u32[]{:S(2)}, u32[]{:S(2)}) %collective-permute-start.5) | collective-permute-done | bytes 720928 | tf_op jit(solution)/shard_map/ppermute | solution.py:858
  73.6 0.9 copy-done.1
  74.5 3.3 %shard_map.73 = (f32[24,24,512]{2,1,0:T(8,128)}, f32[24,16,512]{2,1,0:T(8,128)}, bf16[240,512]{1,0:T(8,128)(2,1)}, bf16[240,512]{1,0:T(8,128)(2,1)}) custom-call(f32[20,24,512]{2,1,0:T(8,128)} %get-tuple-element.58.c1, f32[16,16,512]{2,1,0:T(8,128)} %get-tuple-element.50.refs_3_.r1, bf16[352,1024]{1,0:T(8,128)(2,1)} %copy-done, bf16[352,1024]{1,0:T(8,128)(2,1)} %copy-done.1), custom_call_target="tpu_custom_call" | custom-call | flops 108134400 | bytes 5406720 | tf_op jit(solution)/shard_map/pallas_call | solution.py:839
  77.8 4.3 %collective-permute-start.6 = (bf16[240,512]{1,0:T(8,128)(2,1)}, bf16[240,512]{1,0:T(8,128)(2,1)S(1)}, u32[]{:S(2)}, u32[]{:S(2)}) collective-permute-start(bf16[240,512]{1,0:T(8,128)(2,1)} %get-tuple-element.68), channel_id=1, source_target_pairs={{0,1},{1,2},{2,3},{3,4},{4,5},{5,6},{6,7},{8,9},{9,10},{10,11},{11... | collective-permute-start | bytes 737288 | tf_op jit(solution)/shard_map/ppermute | solution.py:858
  82.0 1.3 collective-permute-start.7
  83.3 2.6 %shard_map.74 = (bf16[240,1024]{1,0:T(8,128)(2,1)}, bf16[240,1024]{1,0:T(8,128)(2,1)}) custom-call(bf16[176,1024]{1,0:T(8,128)(2,1)} %get-tuple-element.62.pxl, bf16[176,1024]{1,0:T(8,128)(2,1)} %get-tuple-element.63.pxh, bf16[352,1024]{1,0:T(8,128)(2,1)} %copy-done, bf16[352,1024]{1,0:T(8,128)(2,1)} %copy-done.1, f32[64,256]{1,0:T(8,128)} %get-tuple-element.51.refs_4_.r2.refs_3_), custom_call_target="tpu_custom_call" | custom-call | flops 64225280 | bytes 3211264 | tf_op jit(solution)/shard_map/pallas_call | solution.py:839
  86.0 1.3 collective-permute-start.9
  87.3 5.6 %collective-permute-start.8 = (bf16[240,1024]{1,0:T(8,128)(2,1)}, bf16[240,1024]{1,0:T(8,128)(2,1)S(1)}, u32[]{:S(2)}, u32[]{:S(2)}) collective-permute-start(bf16[240,1024]{1,0:T(8,128)(2,1)} %get-tuple-element.65), channel_id=1, source_target_pairs={{0,1},{1,2},{2,3},{3,4},{4,5},{5,6},{6,7},{8,9},{9,10},{10,11},{11... | collective-permute-start | bytes 1474568 | tf_op jit(solution)/shard_map/ppermute | solution.py:858
  93.7 6.6 %shard_map.75 = (f32[24,24,512]{2,1,0:T(8,128)}, f32[24,24,512]{2,1,0:T(8,128)}, f32[24,24,512]{2,1,0:T(8,128)}, f32[64,256]{1,0:T(8,128)}, f32[64,256]{1,0:T(8,128)}, /*index=5*/f32[64,256]{1,0:T(8,128)}) custom-call(s32[2]{0:T(128)} %pad_add_fusion.refs_0_, f32[24,24,512]{2,1,0:T(8,128)} %get-tuple-element.66.refs_1_, ...), custom_call_target="tpu_custom_call" | custom-call | flops 125173920 | bytes 6258696 | tf_op jit(solution)/shard_map/pallas_call | solution.py:839
  100.3 17.4 %collective-permute-start.12 = (f32[64,256]{1,0:T(8,128)}, f32[64,256]{1,0:T(8,128)S(1)}, u32[]{:S(2)}, u32[]{:S(2)}) collective-permute-start(f32[64,256]{1,0:T(8,128)} %get-tuple-element.74), channel_id=1, source_target_pairs={{0,16},{8,24},{16,0},{24,8},{1,17},{9,25},{17,1},{25,9},{2,18},{10... | collective-permute-start | bytes 196616 | tf_op jit(solution)/shard_map/ppermute | solution.py:865
  117.7 1.3 collective-permute-start.11
  119.0 3.0 %collective-permute-start.10 = (f32[64,256]{1,0:T(8,128)}, f32[64,256]{1,0:T(8,128)S(1)}, u32[]{:S(2)}, u32[]{:S(2)}) collective-permute-start(f32[64,256]{1,0:T(8,128)} %get-tuple-element.73.own), channel_id=1, source_target_pairs={{0,8},{8,16},{16,24},{1,9},{9,17},{17,25},{2,10},{10,18},{18,26},{... | collective-permute-start | bytes 196616 | tf_op jit(solution)/shard_map/ppermute | solution.py:858
  122.1 1.1 collective-permute-done.10.low
  123.7 2.5 %shard_map.76 = (f32[32,8,256]{2,1,0:T(8,128)}, f32[32,8,256]{2,1,0:T(8,128)}, bf16[320,256]{1,0:T(8,128)(2,1)}, bf16[256,256]{1,0:T(8,128)(2,1)}, bf16[256,256]{1,0:T(8,128)(2,1)}) custom-call(f32[64,256]{1,0:T(8,128)} %get-tuple-element.73.own, f32[64,256]{1,0:T(8,128)} %copy-done.16, f32[64,256]{1,0:T(8,128)} %copy-done.15, f32[64,256]{1,0:T(8,128)} %copy-done.8, ...), custom_call_target="tpu_custom_call" | custom-call | flops 55705600 | bytes 2785280 | tf_op jit(solution)/shard_map/pallas_call | solution.py:839
  126.2 6.5 %collective-permute-start.15 = (bf16[256,256]{1,0:T(8,128)(2,1)}, bf16[256,256]{1,0:T(8,128)(2,1)S(1)}, u32[]{:S(2)}, u32[]{:S(2)}) collective-permute-start(bf16[256,256]{1,0:T(8,128)(2,1)} %get-tuple-element.77), channel_id=1, source_target_pairs={{0,2},{1,3},{2,4},{3,5},{4,6},{5,7},{8,10},{9,11},{10,12},{11,13},... | collective-permute-start | bytes 393224 | tf_op jit(solution)/shard_map/ppermute | solution.py:858
  132.8 1.3 collective-permute-start.14
  134.1 4.6 %collective-permute-start.13 = (bf16[320,256]{1,0:T(8,128)(2,1)}, bf16[320,256]{1,0:T(8,128)(2,1)S(1)}, u32[]{:S(2)}, u32[]{:S(2)}) collective-permute-start(bf16[320,256]{1,0:T(8,128)(2,1)} %get-tuple-element.76), channel_id=1, source_target_pairs={{0,1},{1,2},{2,3},{3,4},{4,5},{5,6},{6,7},{8,9},{9,10},{10,11},{11... | collective-permute-start | bytes 491528 | tf_op jit(solution)/shard_map/ppermute | solution.py:858
  138.7 1.5 collective-permute-start.16
  140.2 6.2 %collective-permute-done.16.refs_12_ = bf16[256,256]{1,0:T(8,128)(2,1)S(1)} collective-permute-done((bf16[256,256]{1,0:T(8,128)(2,1)}, bf16[256,256]{1,0:T(8,128)(2,1)S(1)}, u32[]{:S(2)}, u32[]{:S(2)}) %collective-permute-start.16) | collective-permute-done | bytes 131104 | tf_op jit(solution)/shard_map/ppermute | solution.py:858
  147.5 23.4 %shard_map.77 = f32[32,32,1024]{2,1,0:T(8,128)} custom-call(s32[2]{0:T(128)} %pad_add_fusion.refs_0_, f32[24,24,512]{2,1,0:T(8,128)} %get-tuple-element.70.refs_1_, f32[24,24,512]{2,1,0:T(8,128)} %get-tuple-element.71.refs_2_, f32[24,24,512]{2,1,0:T(8,128)} %get-tuple-element.72.refs_3_, bf16[352,1024]{1,0:T(8,128)(2,1)} %copy-done, ...), custom_call_target="tpu_custom_call" | custom-call | flops 545259648 | bytes 27262984 | tf_op jit(solution)/shard_map/pallas_call | solution.py:839
  (47 shorter events, 4.8 us)
Async XLA Ops:
  5.3 8.2 %collective-permute-start = (bf16[464,384]{1,0:T(8,128)(2,1)}, bf16[464,384]{1,0:T(8,128)(2,1)S(1)}, u32[]{:S(2)}, u32[]{:S(2)}) collective-permute-start(bf16[464,384]{1,0:T(8,128)(2,1)} %get-tuple-element.46), channel_id=1, source_target_pairs={{0,8},{8,16},{16,24},{1,9},{9,17},{17,25},{2,10},{10,18},{18,26},{... | collective-permute-start | bytes 1069064 | tf_op jit(solution)/shard_map/ppermute | solution.py:858
  7.7 5.9 %collective-permute-start.1 = (bf16[464,384]{1,0:T(8,128)(2,1)}, bf16[464,384]{1,0:T(8,128)(2,1)S(1)}, u32[]{:S(2)}, u32[]{:S(2)}) collective-permute-start(bf16[464,384]{1,0:T(8,128)(2,1)} %get-tuple-element.47), channel_id=1, source_target_pairs={{8,0},{16,8},{24,16},{9,1},{17,9},{25,17},{10,2},{18,10},{26,18},{... | collective-permute-start | bytes 1069064 | tf_op jit(solution)/shard_map/ppermute | solution.py:858
  13.5 0.7 copy-start.2
  13.6 0.8 copy-start.3
  16.7 22.8 %collective-permute-start.2 = (bf16[464,384]{1,0:T(8,128)(2,1)}, bf16[464,384]{1,0:T(8,128)(2,1)S(1)}, u32[]{:S(2)}, u32[]{:S(2)}) collective-permute-start(bf16[464,384]{1,0:T(8,128)(2,1)} %get-tuple-element.48), channel_id=1, source_target_pairs={{0,1},{1,2},{2,3},{3,4},{4,5},{5,6},{6,7},{8,9},{9,10},{10,11},{11... | collective-permute-start | bytes 1069064 | tf_op jit(solution)/shard_map/ppermute | solution.py:858
  20.9 18.6 %collective-permute-start.3 = (bf16[464,384]{1,0:T(8,128)(2,1)}, bf16[464,384]{1,0:T(8,128)(2,1)S(1)}, u32[]{:S(2)}, u32[]{:S(2)}) collective-permute-start(bf16[464,384]{1,0:T(8,128)(2,1)} %get-tuple-element.49), channel_id=1, source_target_pairs={{1,0},{2,1},{3,2},{4,3},{5,4},{6,5},{7,6},{9,8},{10,9},{11,10},{12... | collective-permute-start | bytes 1069064 | tf_op jit(solution)/shard_map/ppermute | solution.py:858
  39.5 0.7 copy-start.6
  39.5 0.9 copy-start.7
  62.9 8.4 %collective-permute-start.4 = (bf16[352,1024]{1,0:T(8,128)(2,1)}, bf16[352,1024]{1,0:T(8,128)(2,1)S(1)}, u32[]{:S(2)}, u32[]{:S(2)}) collective-permute-start(bf16[352,1024]{1,0:T(8,128)(2,1)} %get-tuple-element.59), channel_id=1, source_target_pairs={{0,8},{8,16},{16,24},{1,9},{9,17},{17,25},{2,10},{10,18},{18,26},{... | collective-permute-start | bytes 2162696 | tf_op jit(solution)/shard_map/ppermute | solution.py:858
  69.3 4.3 %collective-permute-start.5 = (bf16[352,1024]{1,0:T(8,128)(2,1)}, bf16[352,1024]{1,0:T(8,128)(2,1)S(1)}, u32[]{:S(2)}, u32[]{:S(2)}) collective-permute-start(bf16[352,1024]{1,0:T(8,128)(2,1)} %get-tuple-element.60), channel_id=1, source_target_pairs={{8,0},{16,8},{24,16},{9,1},{17,9},{25,17},{10,2},{18,10},{26,18},{... | collective-permute-start | bytes 2162696 | tf_op jit(solution)/shard_map/ppermute | solution.py:858
  71.3 2.3 %copy-start = (bf16[352,1024]{1,0:T(8,128)(2,1)}, bf16[352,1024]{1,0:T(8,128)(2,1)S(1)}, u32[]{:S(2)}) copy-start(bf16[352,1024]{1,0:T(8,128)(2,1)S(1)} %collective-permute-done.4.mzl.zl.refs_4_) | copy-start | bytes 2162692
  73.6 0.9 copy-start.1
  77.8 15.1 %collective-permute-start.6 = (bf16[240,512]{1,0:T(8,128)(2,1)}, bf16[240,512]{1,0:T(8,128)(2,1)S(1)}, u32[]{:S(2)}, u32[]{:S(2)}) collective-permute-start(bf16[240,512]{1,0:T(8,128)(2,1)} %get-tuple-element.68), channel_id=1, source_target_pairs={{0,1},{1,2},{2,3},{3,4},{4,5},{5,6},{6,7},{8,9},{9,10},{10,11},{11... | collective-permute-start | bytes 737288 | tf_op jit(solution)/shard_map/ppermute | solution.py:858
  82.0 10.9 %collective-permute-start.7 = (bf16[240,512]{1,0:T(8,128)(2,1)}, bf16[240,512]{1,0:T(8,128)(2,1)S(1)}, u32[]{:S(2)}, u32[]{:S(2)}) collective-permute-start(bf16[240,512]{1,0:T(8,128)(2,1)} %get-tuple-element.69), channel_id=1, source_target_pairs={{1,0},{2,1},{3,2},{4,3},{5,4},{6,5},{7,6},{9,8},{10,9},{11,10},{12... | collective-permute-start | bytes 737288 | tf_op jit(solution)/shard_map/ppermute | solution.py:858
  86.0 60.4 %collective-permute-start.9 = (bf16[240,1024]{1,0:T(8,128)(2,1)}, bf16[240,1024]{1,0:T(8,128)(2,1)S(1)}, u32[]{:S(2)}, u32[]{:S(2)}) collective-permute-start(bf16[240,1024]{1,0:T(8,128)(2,1)} %get-tuple-element.64), channel_id=1, source_target_pairs={{1,0},{2,1},{3,2},{4,3},{5,4},{6,5},{7,6},{9,8},{10,9},{11,10},{12... | collective-permute-start | bytes 1474568 | tf_op jit(solution)/shard_map/ppermute | solution.py:858
  87.3 59.2 %collective-permute-start.8 = (bf16[240,1024]{1,0:T(8,128)(2,1)}, bf16[240,1024]{1,0:T(8,128)(2,1)S(1)}, u32[]{:S(2)}, u32[]{:S(2)}) collective-permute-start(bf16[240,1024]{1,0:T(8,128)(2,1)} %get-tuple-element.65), channel_id=1, source_target_pairs={{0,1},{1,2},{2,3},{3,4},{4,5},{5,6},{6,7},{8,9},{9,10},{10,11},{11... | collective-permute-start | bytes 1474568 | tf_op jit(solution)/shard_map/ppermute | solution.py:858
  92.9 0.7 copy-start.9
  92.9 0.8 copy-start.10
  100.3 21.8 %collective-permute-start.12 = (f32[64,256]{1,0:T(8,128)}, f32[64,256]{1,0:T(8,128)S(1)}, u32[]{:S(2)}, u32[]{:S(2)}) collective-permute-start(f32[64,256]{1,0:T(8,128)} %get-tuple-element.74), channel_id=1, source_target_pairs={{0,16},{8,24},{16,0},{24,8},{1,17},{9,25},{17,1},{25,9},{2,18},{10... | collective-permute-start | bytes 196616 | tf_op jit(solution)/shard_map/ppermute | solution.py:865
  117.7 4.4 %collective-permute-start.11 = (f32[64,256]{1,0:T(8,128)}, f32[64,256]{1,0:T(8,128)S(1)}, u32[]{:S(2)}, u32[]{:S(2)}) collective-permute-start(f32[64,256]{1,0:T(8,128)} %get-tuple-element.73.own), channel_id=1, source_target_pairs={{8,0},{16,8},{24,16},{9,1},{17,9},{25,17},{10,2},{18,10},{26,18},{... | collective-permute-start | bytes 196616 | tf_op jit(solution)/shard_map/ppermute | solution.py:858
  119.0 4.1 %collective-permute-start.10 = (f32[64,256]{1,0:T(8,128)}, f32[64,256]{1,0:T(8,128)S(1)}, u32[]{:S(2)}, u32[]{:S(2)}) collective-permute-start(f32[64,256]{1,0:T(8,128)} %get-tuple-element.73.own), channel_id=1, source_target_pairs={{0,8},{8,16},{16,24},{1,9},{9,17},{17,25},{2,10},{10,18},{18,26},{... | collective-permute-start | bytes 196616 | tf_op jit(solution)/shard_map/ppermute | solution.py:858
  122.0 1.1 copy-start.8
  122.1 1.1 copy-start.15
  126.2 12.4 %collective-permute-start.15 = (bf16[256,256]{1,0:T(8,128)(2,1)}, bf16[256,256]{1,0:T(8,128)(2,1)S(1)}, u32[]{:S(2)}, u32[]{:S(2)}) collective-permute-start(bf16[256,256]{1,0:T(8,128)(2,1)} %get-tuple-element.77), channel_id=1, source_target_pairs={{0,2},{1,3},{2,4},{3,5},{4,6},{5,7},{8,10},{9,11},{10,12},{11,13},... | collective-permute-start | bytes 393224 | tf_op jit(solution)/shard_map/ppermute | solution.py:858
  132.8 13.6 %collective-permute-start.14 = (bf16[320,256]{1,0:T(8,128)(2,1)}, bf16[320,256]{1,0:T(8,128)(2,1)S(1)}, u32[]{:S(2)}, u32[]{:S(2)}) collective-permute-start(bf16[320,256]{1,0:T(8,128)(2,1)} %get-tuple-element.76), channel_id=1, source_target_pairs={{1,0},{2,1},{3,2},{4,3},{5,4},{6,5},{7,6},{9,8},{10,9},{11,10},{12... | collective-permute-start | bytes 491528 | tf_op jit(solution)/shard_map/ppermute | solution.py:858
  134.1 12.3 %collective-permute-start.13 = (bf16[320,256]{1,0:T(8,128)(2,1)}, bf16[320,256]{1,0:T(8,128)(2,1)S(1)}, u32[]{:S(2)}, u32[]{:S(2)}) collective-permute-start(bf16[320,256]{1,0:T(8,128)(2,1)} %get-tuple-element.76), channel_id=1, source_target_pairs={{0,1},{1,2},{2,3},{3,4},{4,5},{5,6},{6,7},{8,9},{9,10},{10,11},{11... | collective-permute-start | bytes 491528 | tf_op jit(solution)/shard_map/ppermute | solution.py:858
  138.7 7.8 %copy-start.13 = (bf16[256,256]{1,0:T(8,128)(2,1)}, bf16[256,256]{1,0:T(8,128)(2,1)S(1)}, u32[]{:S(2)}) copy-start(bf16[256,256]{1,0:T(8,128)(2,1)S(1)} %collective-permute-done.15.refs_11_) | copy-start | bytes 393220
  138.7 7.7 %collective-permute-start.16 = (bf16[256,256]{1,0:T(8,128)(2,1)}, bf16[256,256]{1,0:T(8,128)(2,1)S(1)}, u32[]{:S(2)}, u32[]{:S(2)}) collective-permute-start(bf16[256,256]{1,0:T(8,128)(2,1)} %get-tuple-element.78), channel_id=1, source_target_pairs={{2,0},{3,1},{4,2},{5,3},{6,4},{7,5},{10,8},{11,9},{12,10},{13,11},... | collective-permute-start | bytes 393224 | tf_op jit(solution)/shard_map/ppermute | solution.py:858
  146.4 0.7 copy-start.11
  146.4 0.8 copy-start.12
  146.4 0.9 copy-start.4
  146.4 1.1 copy-start.5
  (2 other events, 1.3 us)

commit v2 on v1

--- a/solution.py
+++ b/solution.py
@@ -304,32 +304,44 @@
             dst[z + O, :, lanes(t)] = KEEP * here + g * inner
 
 
-def own_kernel(nz, info, density, uptake, own, zl, zh, s0, g0, d0, v1, edge, va, hot):
+def own_kernel(
+    nz, info, own, zl, zh, density, uptake, s_out, g_out, v_out, edge_out,
+    dens, upt, s0, g0, v1, edge, va, hot, sems,
+):
     iz = info[0]
+    loads = [pltpu.make_async_copy(density, dens, sems.at[0]), pltpu.make_async_copy(uptake, upt, sems.at[1])]
+    stores = [
+        pltpu.make_async_copy(src, dst, sems.at[2 + i])
+        for i, (src, dst) in enumerate(((s0, s_out), (g0, g_out), (v1, v_out), (edge, edge_out)))
+    ]
+    for copy in loads:
+        copy.start()
     for p in (3, 4, 37, 38):
         va[p] = jnp.zeros((40, 1024), F32)
-
-    def own_plane(z):
-        va[z + O, 0:32, :] = density[z]
-        va[z + O, 32:40, :] = jnp.zeros((8, 1024), F32)
-        d = uptake[z] + BASE
-        d0[z + Q] = d
-        g0[z + Q] = OMEGA / d
-
-    loop(0, C, own_plane)
     for n in range(4):
         ref, valid = (zl, iz > 0) if n < 2 else (zh, iz < nz - 1)
         q = n if n < 2 else 32 + n
         rows = slice(32 * (n % 2), 32 * (n % 2) + 32)
         for t in range(NT):
-            d = ref[uptake_part(t)].astype(F32)[rows] + BASE
-            d0[q, :, lanes(t)] = d
-            g0[q, :, lanes(t)] = jnp.where(valid, OMEGA, 0.0) / d
+            g0[q, :, lanes(t)] = jnp.where(valid, OMEGA, 0.0) / (ref[uptake_part(t)].astype(F32)[rows] + BASE)
 
     blocks = [(ref, lanes(1)) for ref in (own, zl, zh)]
+    waiting = list(loads[0:1])
     for z, rows, cols, sums in scatter(blocks, hot):
+        while waiting:
+            waiting.pop().wait()
         planes = slice(z, z + 16)
-        s0[planes, rows, cols] = density[planes, rows, cols] + sums
+        s0[planes, rows, cols] = dens[planes, rows, cols] + sums
+    stores[0].start()
+    loads[1].wait()
+
+    def own_plane(z):
+        va[z + O, 0:32, :] = dens[z]
+        va[z + O, 32:40, :] = jnp.zeros((8, 1024), F32)
+        g0[z + Q] = OMEGA / (upt[z] + BASE)
+
+    loop(0, C, own_plane)
+    stores[1].start()
 
     def first(z):
         for t, here, sums in plane(va, z + O):
@@ -343,12 +355,16 @@
         for t in range(NT):
             near = va[z + O + (1 if z < 0 else -1), 0:32, lanes(t)]
             v1[z + 1, :, lanes(t)] = g0[z + Q, :, lanes(t)] * (KAPPA * near)
+    for copy in stores[2:]:
+        copy.start()
+    for copy in stores:
+        copy.wait()
 
 
 def pre_kernel(
-    nz, nx, info, xl, xh, r1, r2, s0, g0, d0, v1, edge_in,
-    supply, c1, mzl, mzh, pxl, pxh, v_out, g_out,
-    va, vb, dd, gg, edge, hot, rs, xp, usl, ush, sems,
+    nz, nx, info, xl, xh, zl, zh, r1, r2, s0, g0, v1, edge_in, uptake,
+    c1, mzl, mzh, vzl, vzh, pxl, pxh, v_out, g_out, s_out,
+    va, vb, supply, upt, dh, gg, edge, hot, rs, xp, usl, ush, sems,
 ):
     iz, ix = info[0], info[1]
     k = KAPPA
@@ -360,7 +376,7 @@
                 (v1, vb.at[4:38, 0:32, :]),
                 (g0, gg.at[:, 0:32, :]),
                 (edge_in, edge),
-                (d0, dd.at[:, 0:32, :]),
+                (uptake, upt),
             )
         )
     ]
@@ -384,7 +400,7 @@
     def set_halo(q, low, high, valid_z):
         gz = jnp.where(valid_z, OMEGA, 0.0)
         d = jnp.where(sub8 < 2, high, jnp.where(sub8 >= 6, low, 0.0)) + BASE
-        dd[q, 32:40, :] = d
+        dh[q] = d
         omega = jnp.where(sub8 < 2, jnp.where(ix < nx - 1, gz, 0.0), jnp.where(sub8 >= 6, jnp.where(ix > 0, gz, 0.0), 0.0))
         gg[q, 32:40, :] = omega / d
 
@@ -410,6 +426,9 @@
         vb[z + O : z + O + 16, rows, cols] = vb[z + O : z + O + 16, rows, cols] + g * sums
     loads[3].wait()
 
+    s_copy = pltpu.make_async_copy(supply, s_out, sems.at[7])
+    s_copy.start()
+
     def edges(z):
         vb[z + O, 32:40, :] = gg[z + Q, 32:40, :] * edge[z]
 
@@ -423,25 +442,34 @@
     v_copy.start()
     g_copy.start()
 
-    def residual(z, sourced, edge):
+    def residual(z, rates, sourced):
         for t, here, sums in plane(va, z + O):
             r = k * sums
-            if not edge:
-                r = r - dd[z + Q, :, lanes(t)] * here
-            if sourced:
-                r = jnp.concatenate([r[0:32] + supply[z, :, lanes(t)], r[32:40]], axis=0)
+            if rates is not None:
+                inner = r[0:32] - (rates(t) + BASE) * here[0:32]
+                if sourced:
+                    inner = inner + supply[z, :, lanes(t)]
+                r = jnp.concatenate([inner, r[32:40] - dh[z + Q, :, lanes(t)] * here[32:40]], axis=0)
             yield t, r
 
-    def coarse(m, sourced):
-        both = zip(residual(2 * m - 4, sourced, False), residual(2 * m - 3, sourced, False))
-        for (t, first), (_, second) in both:
+    def coarse(m, zs, rates, sourced):
+        parts = [residual(zs[i], rates[i], sourced) for i in range(2)]
+        for (t, first), (_, second) in zip(*parts):
             xp[t, m, 0:20, :] = halve_rows(first + second, rs, t)
 
-    loop(2, 18, lambda m: coarse(m, True))
-    loop(0, 2, lambda i: coarse(1 + 17 * i, False))
+    def from_message(ref, n):
+        return lambda t: ref[uptake_part(t)].astype(F32)[32 * n : 32 * n + 32]
+
+    def inner(m):
+        zs = (2 * m - 4, 2 * m - 3)
+        coarse(m, zs, [lambda t, z=z: upt[z, :, lanes(t)] for z in zs], True)
+
+    loop(2, 18, inner)
+    for m, ref, z in ((1, zl, -2), (18, zh, C)):
+        coarse(m, (z, z + 1), [from_message(ref, 0), from_message(ref, 1)], False)
 
     def outer(i):
-        for t, r in residual(jnp.where(i == 0, -3, 34), False, True):
+        for t, r in residual(jnp.where(i == 0, -3, 34), None, False):
             xp[t, 19 * i, 0:20, :] = halve_rows(r, rs, t)
 
     loop(0, 2, outer)
@@ -456,19 +484,23 @@
     empty = jnp.zeros((1, 8, 1024), F32)
     blank = jnp.zeros((8, 1024), F32)
     edges = (
-        (mzl, slice(0, 6), slice(0, 4), va[3:7], 0),
-        (mzh, slice(14, 20), slice(12, 16), va[35:39], 31),
-    )
-    for ref, planes, rates, values, z in edges:
+        (mzl, vzl, slice(0, 6), slice(0, 4), 3, 0),
+        (mzh, vzh, slice(14, 20), slice(12, 16), 35, 31),
+    )
+    for ref, level0, planes, rates, p, z in edges:
         source = c1[planes].reshape(144, 512)
         ref[0:80, 0:512] = source[0:80].astype(BF16)
         ref[0:64, 512:1024] = source[80:144].astype(BF16)
         ref[64:80, 512:1024] = jnp.zeros((16, 512), BF16)
         ref[80:144, 0:512] = r1[rates].reshape(64, 512).astype(BF16)
         ref[80:144, 512:768] = r2[...].astype(BF16)
-        ref[80:144, 768:1024] = jnp.zeros((64, 256), BF16)
-        level0 = jnp.concatenate([values, jnp.concatenate([supply[z : z + 1], empty], axis=1)], axis=0)
-        ref[144:352, :] = jnp.concatenate([level0.reshape(200, 1024), blank], axis=0).astype(BF16)
+        corner = jnp.concatenate([pack_low(va[p], va[p + 1]), pack_low(va[p + 2], va[p + 3])], axis=0).astype(BF16)
+        for n in range(4):
+            ref[80 + 16 * n : 96 + 16 * n, 768:1024] = corner[:, n * 256 : n * 256 + 256]
+        corner = jnp.concatenate([pack_high(va[p], va[p + 1]), pack_high(va[p + 2], va[p + 3])], axis=0).astype(BF16)
+        ref[144:160, :] = corner
+        values = jnp.concatenate([va[p : p + 4], jnp.concatenate([supply[z : z + 1], empty], axis=1)], axis=0)
+        level0[...] = jnp.concatenate([values.reshape(200, 1024), blank], axis=0).astype(BF16)
 
     def sides(i):
         lows, highs = [], []
@@ -499,6 +531,7 @@
     loop(0, 2, sources)
     v_copy.wait()
     g_copy.wait()
+    s_copy.wait()
 
 
 def outer_rows(sub):
@@ -528,11 +561,10 @@
             out[176:240, n * 256 : n * 256 + 256] = rates
         out[176:240, 768:1024] = jnp.zeros((64, 256), BF16)
     for message, start in ((mzl, 0), (mzh, 128)):
-        planes = message[144:304, :].astype(F32).reshape(4, 40, 1024)
+        low = jnp.concatenate([message[80 + 16 * n : 96 + 16 * n, 768:1024] for n in range(4)], axis=1)
         rows = slice(start, start + 16)
-        for ref, out, pack in ((pxl, out_l, pack_low), (pxh, out_h, pack_high)):
-            added = [pack(planes[2 * i], planes[2 * i + 1]) for i in range(2)]
-            out[rows, :] = (ref[rows, :].astype(F32) + jnp.concatenate(added, axis=0)).astype(BF16)
+        for ref, out, corner in ((pxl, out_l, low), (pxh, out_h, message[144:160, :])):
+            out[rows, :] = (ref[rows, :].astype(F32) + corner.astype(F32)).astype(BF16)
 
 
 def in_three(sub, tiles, free, turns):
@@ -634,9 +666,9 @@
 
 def back_kernel(
     nz, nx, info, f1, g1, v1, vzl, vzh, vxl, vxh, own2, n2l, n2h, m2l, m2h, q_own, v_in, g_in, s_in,
-    out,
+    out_hbm,
     f2, q2, h2, a2, b2, rs, xp, xpr, wa, w1, zsl, zsh, vb, ws,
-    v2, gg, supply, fsl, fsh, sems,
+    v2, gg, supply, fsl, fsh, out, sems,
 ):
     iz, ix = info[0], info[1]
     matrix = doubling()
@@ -761,8 +793,8 @@
 
     for copy in level0:
         copy.wait()
-    zsl[...] = vzl[144:352, :].astype(F32)
-    zsh[...] = vzh[144:352, :].astype(F32)
+    zsl[...] = vzl[...].astype(F32)
+    zsh[...] = vzh[...].astype(F32)
     for i in range(4):
         v2[i] = v2[i] + zsl[40 * i : 40 * i + 40, :]
         v2[32 + i] = v2[32 + i] + zsh[40 * i : 40 * i + 40, :]
@@ -826,7 +858,14 @@
             g = gg[z + 2, 0:32, lanes(t)]
             out[z, :, lanes(t)] = KEEP * here[0:32] + g * (supply[z, :, lanes(t)] + k0 * sums[0:32])
 
-    loop(0, C, second, 2)
+    stores = []
+    for i in range(4):
+        part = pl.ds(8 * i, 8)
+        loop(8 * i, 8 * i + 8, second, 2)
+        stores.append(pltpu.make_async_copy(out.at[part], out_hbm.at[part], sems.at[3 + i]))
+        stores[i].start()
+    for copy in stores:
+        copy.wait()
 
 
 VMEM = pl.BlockSpec(memory_space=pltpu.VMEM)
@@ -896,31 +935,47 @@
         0,
         (own, uxl, uxh, zl, zh),
     )
-    s0, g0, d0, v1, edge = call(
+    s0, g0, v1, edge = call(
         lambda *refs: own_kernel(nz, *refs),
-        [full(C, C, 1024), full(36, C, 1024), full(36, C, 1024), full(34, C, 1024), full(C, 8, 1024)],
-        [scratch((42, 40, 1024), F32), scratch((1024, 384), BF16)],
+        [full(C, C, 1024), full(36, C, 1024), full(34, C, 1024), full(C, 8, 1024)],
+        [
+            scratch((C, C, 1024), F32),
+            scratch((C, C, 1024), F32),
+            scratch((C, C, 1024), F32),
+            scratch((36, C, 1024), F32),
+            scratch((34, C, 1024), F32),
+            scratch((C, 8, 1024), F32),
+            scratch((42, 40, 1024), F32),
+            scratch((1024, 384), BF16),
+            pltpu.SemaphoreType.DMA((6,)),
+        ],
         1,
-        (info, density, uptake, own, zl, zh),
+        (info, own, zl, zh, density, uptake),
+        [ANY] * 4,
+        in_hbm=2,
     )
     xl, xh = both_ways(xl, xh, "xy")
 
-    supply, c1, mzl, mzh, pxl, pxh, v2, gg = call(
+    c1, mzl, mzh, vzl, vzh, pxl, pxh, v2, gg, supply = call(
         lambda *refs: pre_kernel(nz, nx, *refs),
         [
-            full(C, C, 1024),
             full(20, 24, 512),
-            half(352, 1024),
-            half(352, 1024),
+            half(160, 1024),
+            half(160, 1024),
+            half(208, 1024),
+            half(208, 1024),
             half(176, 1024),
             half(176, 1024),
             full(36, 40, 1024),
             full(36, 40, 1024),
+            full(C, C, 1024),
         ],
         [
             scratch((42, 40, 1024), F32),
             scratch((42, 40, 1024), F32),
-            scratch((36, 40, 1024), F32),
+            scratch((C, C, 1024), F32),
+            scratch((C, C, 1024), F32),
+            scratch((36, 8, 1024), F32),
             scratch((36, 40, 1024), F32),
             scratch((C, 8, 1024), F32),
             scratch((1024, 768), BF16),
@@ -928,11 +983,11 @@
             scratch((8, 20, 24, 128), F32),
             scratch((72, 1024), F32),
             scratch((72, 1024), F32),
-            pltpu.SemaphoreType.DMA((7,)),
+            pltpu.SemaphoreType.DMA((8,)),
         ],
         1,
-        (info, xl, xh, r1, r2, s0, g0, d0, v1, edge),
-        [VMEM] * 6 + [ANY] * 2,
+        (info, xl, xh, zl, zh, r1, r2, s0, g0, v1, edge, uptake),
+        [VMEM] * 7 + [ANY] * 3,
         in_hbm=5,
     )
     mzl, mzh = both_ways(mzl, mzh, "gz")
@@ -944,6 +999,9 @@
         (c1, r1, mzl, mzh),
     )
     mxl, mxh = both_ways(mxl, mxh, "xy")
+    vzl, vzh, f1 = lax.optimization_barrier((vzl, vzh, f1))
+    vzl, vzh = both_ways(vzl, vzh, "gz")
+    vzl, vzh, pxl, pxh = lax.optimization_barrier((vzl, vzh, pxl, pxh))
     pxl, pxh = call(
         sides_kernel,
         [half(240, 1024), half(240, 1024)],
@@ -991,10 +1049,12 @@
             scratch((C, C, 1024), F32),
             scratch((16, 1024), F32),
             scratch((16, 1024), F32),
-            pltpu.SemaphoreType.DMA((3,)),
+            scratch((C, C, 1024), F32),
+            pltpu.SemaphoreType.DMA((7,)),
         ],
         1,
-        (info, f1, g1, v1, mzl, mzh, vxl, vxh, own2, nl, nh, fl, fh, q2, v2, gg, supply),
+        (info, f1, g1, v1, vzl, vzh, vxl, vxh, own2, nl, nh, fl, fh, q2, v2, gg, supply),
+        [ANY],
         in_hbm=3,
     )
     return supply, concentration

time: 172 us -> 165 us (0.959)
  Pallas kernels: 89 us -> 81.6 us
    pallas_call x10, Pallas kernels: 89 us -> 81.6 us  [call(): pl.pallas_call(kernel, out_shape=tuple(outs), in_specs=[SMEM] * smem + [V...]
    ppermute x1, starting transfers between devices: 17.4 us -> 11.4 us  [two_away(): came = lax.ppermute(to_low, 'gz', [(i, (i + 2) % 4) for i in range(4)])]
    ppermute x16 -> x18, starting transfers between devices: 47.5 us -> 53.4 us  [both_ways(): return (lax.ppermute(to_high, axis, up), lax.ppermute(to_low, axis, down))]
    ppermute x16 -> x18, waiting for transfers between devices: 10.3 us -> 10.9 us  [both_ways(): return (lax.ppermute(to_high, axis, up), lax.ppermute(to_low, axis, down))]
    unnamed x34 -> x38, local copies, waits for them, and re-layouts: 5.03 us -> 4.72 us
  transfers between devices with their start and end apart: 17 -> 19, of which waited for: 5 -> 6; matrix products, arithmetic and copies ran while one was open for 0% -> 0% of each run, Pallas kernels for 19% -> 17%
where the time goes in v2:
time: 165 us; the launch traced here: 164 us
  Pallas kernels  81.6 us (49%)
  starting transfers between devices  64.8 us (39%)
  waiting for transfers between devices  10.9 us (7%)
  local copies, waits for them, and re-layouts  4.72 us (3%)
    pallas_call x10, Pallas kernels, call(): pl.pallas_call(kernel, out_shape=tuple(outs), in_specs=[SMEM] * smem + [V...  81.6 us
    ppermute x18, starting transfers between devices, both_ways(): return (lax.ppermute(to_high, axis, up), lax.ppermute(to_low, axis, down))  53.4 us
    ppermute x1, starting transfers between devices, two_away(): came = lax.ppermute(to_low, 'gz', [(i, (i + 2) % 4) for i in range(4)])  11.4 us
    ppermute x18, waiting for transfers between devices, both_ways(): return (lax.ppermute(to_high, axis, up), lax.ppermute(to_low, axis, down))  10.9 us
    unnamed x38, local copies, waits for them, and re-layouts  4.72 us
  transfers between devices with their start and end apart: 19, of which 6 were waited for; matrix products, arithmetic and copies ran while one was open for 0% of the time, Pallas kernels for 17%

profile of v2, /device:TPU:0, one launch (start us, length us, event | category | flops | bytes accessed | tf_op | source)
XLA Modules:
  0.0 163.8 jit_solution(230612853235486339)
XLA Ops:
  0.6 4.7 %shard_map.68 = (bf16[272,384]{1,0:T(8,128)(2,1)}, bf16[464,384]{1,0:T(8,128)(2,1)}, bf16[464,384]{1,0:T(8,128)(2,1)}) custom-call(s32[72]{0:T(128)} %refs_0_.1, s32[1,9]{1,0:T(1,128)} %refs_1_.1, bf16[72,4096]{1,0:T(8,128)(2,1)} %refs_2_.1, f32[32,32,1024]{2,1,0:T(8,128)} %refs_11_.1), custom_call_target="tpu_custom_call" | custom-call | flops 114121040 | bytes 5706052 | tf_op jit(solution)/shard_map/pallas_call | solution.py:878
  5.3 2.4 %collective-permute-start = (bf16[464,384]{1,0:T(8,128)(2,1)}, bf16[464,384]{1,0:T(8,128)(2,1)S(1)}, u32[]{:S(2)}, u32[]{:S(2)}) collective-permute-start(bf16[464,384]{1,0:T(8,128)(2,1)} %get-tuple-element.54), channel_id=1, source_target_pairs={{0,8},{8,16},{16,24},{1,9},{9,17},{17,25},{2,10},{10,18},{18,26},{... | collective-permute-start | bytes 1069064 | tf_op jit(solution)/shard_map/ppermute | solution.py:897
  7.7 1.3 collective-permute-start.1
  9.0 4.5 %shard_map.69 = (f32[16,16,512]{2,1,0:T(8,128)}, f32[64,256]{1,0:T(8,128)}, bf16[64,1024]{1,0:T(8,128)(2,1)}, bf16[64,1024]{1,0:T(8,128)(2,1)}) custom-call(f32[32,32,1024]{2,1,0:T(8,128)} %refs_11_.1), custom_call_target="tpu_custom_call" | custom-call | flops 100925440 | bytes 5046272 | tf_op jit(solution)/shard_map/pallas_call | solution.py:878
  14.4 2.3 %shard_map.70 = (bf16[464,384]{1,0:T(8,128)(2,1)}, bf16[464,384]{1,0:T(8,128)(2,1)}) custom-call(bf16[272,384]{1,0:T(8,128)(2,1)} %get-tuple-element.50.own.refs_1_, bf16[64,1024]{1,0:T(8,128)(2,1)} %get-tuple-element.52.uxl, bf16[64,1024]{1,0:T(8,128)(2,1)} %get-tuple-element.53.uxh, bf16[464,384]{1,0:T(8,128)(2,1)} %copy-done, bf16[464,384]{1,0:T(8,128)(2,1)} %copy-done.1), custom_call_target="tpu_custom_call" | custom-call | flops 37928960 | bytes 1896448 | tf_op jit(solution)/shard_map/pallas_call | solution.py:878
  16.6 4.2 %collective-permute-start.2 = (bf16[464,384]{1,0:T(8,128)(2,1)}, bf16[464,384]{1,0:T(8,128)(2,1)S(1)}, u32[]{:S(2)}, u32[]{:S(2)}) collective-permute-start(bf16[464,384]{1,0:T(8,128)(2,1)} %get-tuple-element.56), channel_id=1, source_target_pairs={{0,1},{1,2},{2,3},{3,4},{4,5},{5,6},{6,7},{8,9},{9,10},{10,11},{11... | collective-permute-start | bytes 1069064 | tf_op jit(solution)/shard_map/ppermute | solution.py:897
  20.9 1.3 collective-permute-start.3
  22.8 12.1 %shard_map.71 = (f32[32,32,1024]{2,1,0:T(8,128)}, f32[36,32,1024]{2,1,0:T(8,128)}, f32[34,32,1024]{2,1,0:T(8,128)}, f32[32,8,1024]{2,1,0:T(8,128)}) custom-call(s32[2]{0:T(128)} %pad_add_fusion.refs_0_, bf16[272,384]{1,0:T(8,128)(2,1)} %get-tuple-element.50.own.refs_1_, bf16[464,384]{1,0:T(8,128)(2,1)} %copy-done, bf16[464,384]{1,0:T(8,128)(2,1)} %copy-done.1, ...), custom_call_target="tpu_custom_call" | custom-call | flops 474562720 | bytes 23728136 | tf_op jit(solution)/shard_map/pallas_call | solution.py:878
  35.8 21.5 %shard_map.72 = (f32[20,24,512]{2,1,0:T(8,128)}, bf16[160,1024]{1,0:T(8,128)(2,1)}, bf16[160,1024]{1,0:T(8,128)(2,1)}, bf16[208,1024]{1,0:T(8,128)(2,1)}, bf16[2...) custom-call(s32[2]{0:T(128)} %pad_add_fusion.refs_0_, ...), custom_call_target="tpu_custom_call" | custom-call | flops 796590208 | bytes 39829512 | tf_op jit(solution)/shard_map/pallas_call | solution.py:878
  57.3 6.4 %collective-permute-start.4 = (bf16[160,1024]{1,0:T(8,128)(2,1)}, bf16[160,1024]{1,0:T(8,128)(2,1)S(1)}, u32[]{:S(2)}, u32[]{:S(2)}) collective-permute-start(bf16[160,1024]{1,0:T(8,128)(2,1)} %get-tuple-element.68), channel_id=1, source_target_pairs={{0,8},{8,16},{16,24},{1,9},{9,17},{17,25},{2,10},{10,18},{18,26},{... | collective-permute-start | bytes 983048 | tf_op jit(solution)/shard_map/ppermute | solution.py:897
  63.7 1.3 collective-permute-start.5
  65.1 2.3 %collective-permute-done.5.mzh.zh = bf16[160,1024]{1,0:T(8,128)(2,1)S(1)} collective-permute-done((bf16[160,1024]{1,0:T(8,128)(2,1)}, bf16[160,1024]{1,0:T(8,128)(2,1)S(1)}, u32[]{:S(2)}, u32[]{:S(2)}) %collective-permute-start.5) | collective-permute-done | bytes 327712 | tf_op jit(solution)/shard_map/ppermute | solution.py:897
  68.1 3.0 %shard_map.73 = (f32[24,24,512]{2,1,0:T(8,128)}, f32[24,16,512]{2,1,0:T(8,128)}, bf16[240,512]{1,0:T(8,128)(2,1)}, bf16[240,512]{1,0:T(8,128)(2,1)}) custom-call(f32[20,24,512]{2,1,0:T(8,128)} %get-tuple-element.67.c1, f32[16,16,512]{2,1,0:T(8,128)} %get-tuple-element.58.refs_5_.r1, bf16[160,1024]{1,0:T(8,128)(2,1)} %copy-done.2, bf16[160,1024]{1,0:T(8,128)(2,1)} %copy-done.3), custom_call_target="tpu_custom_call" | custom-call | flops 92405760 | bytes 4620288 | tf_op jit(solution)/shard_map/pallas_call | solution.py:878
  71.1 7.0 %collective-permute-start.6 = (bf16[208,1024]{1,0:T(8,128)(2,1)}, bf16[208,1024]{1,0:T(8,128)(2,1)S(1)}, u32[]{:S(2)}, u32[]{:S(2)}) collective-permute-start(bf16[208,1024]{1,0:T(8,128)(2,1)} %get-tuple-element.72), channel_id=1, source_target_pairs={{0,8},{8,16},{16,24},{1,9},{9,17},{17,25},{2,10},{10,18},{18,26},{... | collective-permute-start | bytes 1277960 | tf_op jit(solution)/shard_map/ppermute | solution.py:897
  78.1 1.3 collective-permute-start.7
  79.4 4.6 %collective-permute-start.8 = (bf16[240,512]{1,0:T(8,128)(2,1)}, bf16[240,512]{1,0:T(8,128)(2,1)S(1)}, u32[]{:S(2)}, u32[]{:S(2)}) collective-permute-start(bf16[240,512]{1,0:T(8,128)(2,1)} %get-tuple-element.82), channel_id=1, source_target_pairs={{0,1},{1,2},{2,3},{3,4},{4,5},{5,6},{6,7},{8,9},{9,10},{10,11},{11... | collective-permute-start | bytes 737288 | tf_op jit(solution)/shard_map/ppermute | solution.py:897
  84.0 1.3 collective-permute-start.9
  85.3 2.6 %shard_map.74 = (bf16[240,1024]{1,0:T(8,128)(2,1)}, bf16[240,1024]{1,0:T(8,128)(2,1)}) custom-call(bf16[176,1024]{1,0:T(8,128)(2,1)} %get-tuple-element.76.pxl, bf16[176,1024]{1,0:T(8,128)(2,1)} %get-tuple-element.77.pxh, bf16[160,1024]{1,0:T(8,128)(2,1)} %copy-done.2, bf16[160,1024]{1,0:T(8,128)(2,1)} %copy-done.3, ...), custom_call_target="tpu_custom_call" | custom-call | flops 48496640 | bytes 2424832 | tf_op jit(solution)/shard_map/pallas_call | solution.py:878
  88.0 1.3 collective-permute-start.11
  89.3 5.8 %collective-permute-start.10 = (bf16[240,1024]{1,0:T(8,128)(2,1)}, bf16[240,1024]{1,0:T(8,128)(2,1)S(1)}, u32[]{:S(2)}, u32[]{:S(2)}) collective-permute-start(bf16[240,1024]{1,0:T(8,128)(2,1)} %get-tuple-element.79), channel_id=1, source_target_pairs={{0,1},{1,2},{2,3},{3,4},{4,5},{5,6},{6,7},{8,9},{9,10},{10,11},{11... | collective-permute-start | bytes 1474568 | tf_op jit(solution)/shard_map/ppermute | solution.py:897
  95.9 6.6 %shard_map.75 = (f32[24,24,512]{2,1,0:T(8,128)}, f32[24,24,512]{2,1,0:T(8,128)}, f32[24,24,512]{2,1,0:T(8,128)}, f32[64,256]{1,0:T(8,128)}, f32[64,256]{1,0:T(8,128)}, /*index=5*/f32[64,256]{1,0:T(8,128)}) custom-call(s32[2]{0:T(128)} %pad_add_fusion.refs_0_, f32[24,24,512]{2,1,0:T(8,128)} %get-tuple-element.80.refs_1_, ...), custom_call_target="tpu_custom_call" | custom-call | flops 125173920 | bytes 6258696 | tf_op jit(solution)/shard_map/pallas_call | solution.py:878
  102.5 11.4 %collective-permute-start.14 = (f32[64,256]{1,0:T(8,128)}, f32[64,256]{1,0:T(8,128)S(1)}, u32[]{:S(2)}, u32[]{:S(2)}) collective-permute-start(f32[64,256]{1,0:T(8,128)} %get-tuple-element.90), channel_id=1, source_target_pairs={{0,16},{8,24},{16,0},{24,8},{1,17},{9,25},{17,1},{25,9},{2,18},{10... | collective-permute-start | bytes 196616 | tf_op jit(solution)/shard_map/ppermute | solution.py:904
  113.8 1.3 collective-permute-start.13
  115.1 3.0 %collective-permute-start.12 = (f32[64,256]{1,0:T(8,128)}, f32[64,256]{1,0:T(8,128)S(1)}, u32[]{:S(2)}, u32[]{:S(2)}) collective-permute-start(f32[64,256]{1,0:T(8,128)} %get-tuple-element.89.own), channel_id=1, source_target_pairs={{0,8},{8,16},{16,24},{1,9},{9,17},{17,25},{2,10},{10,18},{18,26},{... | collective-permute-start | bytes 196616 | tf_op jit(solution)/shard_map/ppermute | solution.py:897
  118.2 1.1 collective-permute-done.12.low
  119.9 2.2 %shard_map.76 = (f32[32,8,256]{2,1,0:T(8,128)}, f32[32,8,256]{2,1,0:T(8,128)}, bf16[320,256]{1,0:T(8,128)(2,1)}, bf16[256,256]{1,0:T(8,128)(2,1)}, bf16[256,256]{1,0:T(8,128)(2,1)}) custom-call(f32[64,256]{1,0:T(8,128)} %get-tuple-element.89.own, f32[64,256]{1,0:T(8,128)} %copy-done.18, f32[64,256]{1,0:T(8,128)} %copy-done.17, f32[64,256]{1,0:T(8,128)} %copy-done.10, ...), custom_call_target="tpu_custom_call" | custom-call | flops 39976960 | bytes 1998848 | tf_op jit(solution)/shard_map/pallas_call | solution.py:878
  122.1 1.3 collective-permute-start.17
  123.4 1.3 collective-permute-start.16
  124.7 7.2 %collective-permute-start.15 = (bf16[320,256]{1,0:T(8,128)(2,1)}, bf16[320,256]{1,0:T(8,128)(2,1)S(1)}, u32[]{:S(2)}, u32[]{:S(2)}) collective-permute-start(bf16[320,256]{1,0:T(8,128)(2,1)} %get-tuple-element.92), channel_id=1, source_target_pairs={{0,1},{1,2},{2,3},{3,4},{4,5},{5,6},{6,7},{8,9},{9,10},{10,11},{11... | collective-permute-start | bytes 491528 | tf_op jit(solution)/shard_map/ppermute | solution.py:897
  131.9 1.3 collective-permute-start.18
  133.2 7.1 %collective-permute-done.18.refs_12_ = bf16[256,256]{1,0:T(8,128)(2,1)S(1)} collective-permute-done((bf16[256,256]{1,0:T(8,128)(2,1)}, bf16[256,256]{1,0:T(8,128)(2,1)S(1)}, u32[]{:S(2)}, u32[]{:S(2)}) %collective-permute-start.18) | collective-permute-done | bytes 131104 | tf_op jit(solution)/shard_map/ppermute | solution.py:897
  141.5 22.2 %shard_map.77 = f32[32,32,1024]{2,1,0:T(8,128)} custom-call(s32[2]{0:T(128)} %pad_add_fusion.refs_0_, f32[24,24,512]{2,1,0:T(8,128)} %get-tuple-element.84.refs_1_, f32[24,24,512]{2,1,0:T(8,128)} %get-tuple-element.85.refs_2_, f32[24,24,512]{2,1,0:T(8,128)} %get-tuple-element.86.refs_3_, bf16[208,1024]{1,0:T(8,128)(2,1)} %copy-done.6, ...), custom_call_target="tpu_custom_call" | custom-call | flops 533463200 | bytes 26673160 | tf_op jit(solution)/shard_map/pallas_call | solution.py:878
  (55 shorter events, 5.7 us)
Async XLA Ops:
  5.3 8.2 %collective-permute-start = (bf16[464,384]{1,0:T(8,128)(2,1)}, bf16[464,384]{1,0:T(8,128)(2,1)S(1)}, u32[]{:S(2)}, u32[]{:S(2)}) collective-permute-start(bf16[464,384]{1,0:T(8,128)(2,1)} %get-tuple-element.54), channel_id=1, source_target_pairs={{0,8},{8,16},{16,24},{1,9},{9,17},{17,25},{2,10},{10,18},{18,26},{... | collective-permute-start | bytes 1069064 | tf_op jit(solution)/shard_map/ppermute | solution.py:897
  7.7 5.9 %collective-permute-start.1 = (bf16[464,384]{1,0:T(8,128)(2,1)}, bf16[464,384]{1,0:T(8,128)(2,1)S(1)}, u32[]{:S(2)}, u32[]{:S(2)}) collective-permute-start(bf16[464,384]{1,0:T(8,128)(2,1)} %get-tuple-element.55), channel_id=1, source_target_pairs={{8,0},{16,8},{24,16},{9,1},{17,9},{25,17},{10,2},{18,10},{26,18},{... | collective-permute-start | bytes 1069064 | tf_op jit(solution)/shard_map/ppermute | solution.py:897
  13.5 0.8 copy-start
  13.6 0.8 copy-start.1
  16.6 18.3 %collective-permute-start.2 = (bf16[464,384]{1,0:T(8,128)(2,1)}, bf16[464,384]{1,0:T(8,128)(2,1)S(1)}, u32[]{:S(2)}, u32[]{:S(2)}) collective-permute-start(bf16[464,384]{1,0:T(8,128)(2,1)} %get-tuple-element.56), channel_id=1, source_target_pairs={{0,1},{1,2},{2,3},{3,4},{4,5},{5,6},{6,7},{8,9},{9,10},{10,11},{11... | collective-permute-start | bytes 1069064 | tf_op jit(solution)/shard_map/ppermute | solution.py:897
  20.9 14.1 %collective-permute-start.3 = (bf16[464,384]{1,0:T(8,128)(2,1)}, bf16[464,384]{1,0:T(8,128)(2,1)S(1)}, u32[]{:S(2)}, u32[]{:S(2)}) collective-permute-start(bf16[464,384]{1,0:T(8,128)(2,1)} %get-tuple-element.57), channel_id=1, source_target_pairs={{1,0},{2,1},{3,2},{4,3},{5,4},{6,5},{7,6},{9,8},{10,9},{11,10},{12... | collective-permute-start | bytes 1069064 | tf_op jit(solution)/shard_map/ppermute | solution.py:897
  34.9 0.8 copy-start.8
  35.0 0.8 copy-start.9
  57.3 7.8 %collective-permute-start.4 = (bf16[160,1024]{1,0:T(8,128)(2,1)}, bf16[160,1024]{1,0:T(8,128)(2,1)S(1)}, u32[]{:S(2)}, u32[]{:S(2)}) collective-permute-start(bf16[160,1024]{1,0:T(8,128)(2,1)} %get-tuple-element.68), channel_id=1, source_target_pairs={{0,8},{8,16},{16,24},{1,9},{9,17},{17,25},{2,10},{10,18},{18,26},{... | collective-permute-start | bytes 983048 | tf_op jit(solution)/shard_map/ppermute | solution.py:897
  63.7 3.7 %collective-permute-start.5 = (bf16[160,1024]{1,0:T(8,128)(2,1)}, bf16[160,1024]{1,0:T(8,128)(2,1)S(1)}, u32[]{:S(2)}, u32[]{:S(2)}) collective-permute-start(bf16[160,1024]{1,0:T(8,128)(2,1)} %get-tuple-element.69), channel_id=1, source_target_pairs={{8,0},{16,8},{24,16},{9,1},{17,9},{25,17},{10,2},{18,10},{26,18},{... | collective-permute-start | bytes 983048 | tf_op jit(solution)/shard_map/ppermute | solution.py:897
  65.1 2.3 %copy-start.2 = (bf16[160,1024]{1,0:T(8,128)(2,1)}, bf16[160,1024]{1,0:T(8,128)(2,1)S(1)}, u32[]{:S(2)}) copy-start(bf16[160,1024]{1,0:T(8,128)(2,1)S(1)} %collective-permute-done.4.mzl.zl) | copy-start | bytes 983044
  71.1 14.2 %collective-permute-start.6 = (bf16[208,1024]{1,0:T(8,128)(2,1)}, bf16[208,1024]{1,0:T(8,128)(2,1)S(1)}, u32[]{:S(2)}, u32[]{:S(2)}) collective-permute-start(bf16[208,1024]{1,0:T(8,128)(2,1)} %get-tuple-element.72), channel_id=1, source_target_pairs={{0,8},{8,16},{16,24},{1,9},{9,17},{17,25},{2,10},{10,18},{18,26},{... | collective-permute-start | bytes 1277960 | tf_op jit(solution)/shard_map/ppermute | solution.py:897
  78.1 7.2 %collective-permute-start.7 = (bf16[208,1024]{1,0:T(8,128)(2,1)}, bf16[208,1024]{1,0:T(8,128)(2,1)S(1)}, u32[]{:S(2)}, u32[]{:S(2)}) collective-permute-start(bf16[208,1024]{1,0:T(8,128)(2,1)} %get-tuple-element.73), channel_id=1, source_target_pairs={{8,0},{16,8},{24,16},{9,1},{17,9},{25,17},{10,2},{18,10},{26,18},{... | collective-permute-start | bytes 1277960 | tf_op jit(solution)/shard_map/ppermute | solution.py:897
  79.4 15.6 %collective-permute-start.8 = (bf16[240,512]{1,0:T(8,128)(2,1)}, bf16[240,512]{1,0:T(8,128)(2,1)S(1)}, u32[]{:S(2)}, u32[]{:S(2)}) collective-permute-start(bf16[240,512]{1,0:T(8,128)(2,1)} %get-tuple-element.82), channel_id=1, source_target_pairs={{0,1},{1,2},{2,3},{3,4},{4,5},{5,6},{6,7},{8,9},{9,10},{10,11},{11... | collective-permute-start | bytes 737288 | tf_op jit(solution)/shard_map/ppermute | solution.py:897
  84.0 11.2 %collective-permute-start.9 = (bf16[240,512]{1,0:T(8,128)(2,1)}, bf16[240,512]{1,0:T(8,128)(2,1)S(1)}, u32[]{:S(2)}, u32[]{:S(2)}) collective-permute-start(bf16[240,512]{1,0:T(8,128)(2,1)} %get-tuple-element.83), channel_id=1, source_target_pairs={{1,0},{2,1},{3,2},{4,3},{5,4},{6,5},{7,6},{9,8},{10,9},{11,10},{12... | collective-permute-start | bytes 737288 | tf_op jit(solution)/shard_map/ppermute | solution.py:897
  85.3 55.1 %copy-start.6 = (bf16[208,1024]{1,0:T(8,128)(2,1)}, bf16[208,1024]{1,0:T(8,128)(2,1)S(1)}, u32[]{:S(2)}) copy-start(bf16[208,1024]{1,0:T(8,128)(2,1)S(1)} %collective-permute-done.6.refs_4_) | copy-start | bytes 1277956
  85.3 55.1 %copy-start.7 = (bf16[208,1024]{1,0:T(8,128)(2,1)}, bf16[208,1024]{1,0:T(8,128)(2,1)S(1)}, u32[]{:S(2)}) copy-start(bf16[208,1024]{1,0:T(8,128)(2,1)S(1)} %collective-permute-done.7.refs_5_) | copy-start | bytes 1277956
  88.0 52.4 %collective-permute-start.11 = (bf16[240,1024]{1,0:T(8,128)(2,1)}, bf16[240,1024]{1,0:T(8,128)(2,1)S(1)}, u32[]{:S(2)}, u32[]{:S(2)}) collective-permute-start(bf16[240,1024]{1,0:T(8,128)(2,1)} %get-tuple-element.78), channel_id=1, source_target_pairs={{1,0},{2,1},{3,2},{4,3},{5,4},{6,5},{7,6},{9,8},{10,9},{11,10},{12... | collective-permute-start | bytes 1474568 | tf_op jit(solution)/shard_map/ppermute | solution.py:897
  89.3 51.1 %collective-permute-start.10 = (bf16[240,1024]{1,0:T(8,128)(2,1)}, bf16[240,1024]{1,0:T(8,128)(2,1)S(1)}, u32[]{:S(2)}, u32[]{:S(2)}) collective-permute-start(bf16[240,1024]{1,0:T(8,128)(2,1)} %get-tuple-element.79), channel_id=1, source_target_pairs={{0,1},{1,2},{2,3},{3,4},{4,5},{5,6},{6,7},{8,9},{9,10},{10,11},{11... | collective-permute-start | bytes 1474568 | tf_op jit(solution)/shard_map/ppermute | solution.py:897
  102.5 15.7 %collective-permute-start.14 = (f32[64,256]{1,0:T(8,128)}, f32[64,256]{1,0:T(8,128)S(1)}, u32[]{:S(2)}, u32[]{:S(2)}) collective-permute-start(f32[64,256]{1,0:T(8,128)} %get-tuple-element.90), channel_id=1, source_target_pairs={{0,16},{8,24},{16,0},{24,8},{1,17},{9,25},{17,1},{25,9},{2,18},{10... | collective-permute-start | bytes 196616 | tf_op jit(solution)/shard_map/ppermute | solution.py:904
  113.8 4.4 %collective-permute-start.13 = (f32[64,256]{1,0:T(8,128)}, f32[64,256]{1,0:T(8,128)S(1)}, u32[]{:S(2)}, u32[]{:S(2)}) collective-permute-start(f32[64,256]{1,0:T(8,128)} %get-tuple-element.89.own), channel_id=1, source_target_pairs={{8,0},{16,8},{24,16},{9,1},{17,9},{25,17},{10,2},{18,10},{26,18},{... | collective-permute-start | bytes 196616 | tf_op jit(solution)/shard_map/ppermute | solution.py:897
  115.1 4.1 %collective-permute-start.12 = (f32[64,256]{1,0:T(8,128)}, f32[64,256]{1,0:T(8,128)S(1)}, u32[]{:S(2)}, u32[]{:S(2)}) collective-permute-start(f32[64,256]{1,0:T(8,128)} %get-tuple-element.89.own), channel_id=1, source_target_pairs={{0,8},{8,16},{16,24},{1,9},{9,17},{17,25},{2,10},{10,18},{18,26},{... | collective-permute-start | bytes 196616 | tf_op jit(solution)/shard_map/ppermute | solution.py:897
  118.2 1.1 copy-start.10
  118.2 1.1 copy-start.17
  122.1 9.8 %collective-permute-start.17 = (bf16[256,256]{1,0:T(8,128)(2,1)}, bf16[256,256]{1,0:T(8,128)(2,1)S(1)}, u32[]{:S(2)}, u32[]{:S(2)}) collective-permute-start(bf16[256,256]{1,0:T(8,128)(2,1)} %get-tuple-element.93), channel_id=1, source_target_pairs={{0,2},{1,3},{2,4},{3,5},{4,6},{5,7},{8,10},{9,11},{10,12},{11,13},... | collective-permute-start | bytes 393224 | tf_op jit(solution)/shard_map/ppermute | solution.py:897
  123.4 16.9 %collective-permute-start.16 = (bf16[320,256]{1,0:T(8,128)(2,1)}, bf16[320,256]{1,0:T(8,128)(2,1)S(1)}, u32[]{:S(2)}, u32[]{:S(2)}) collective-permute-start(bf16[320,256]{1,0:T(8,128)(2,1)} %get-tuple-element.92), channel_id=1, source_target_pairs={{1,0},{2,1},{3,2},{4,3},{5,4},{6,5},{7,6},{9,8},{10,9},{11,10},{12... | collective-permute-start | bytes 491528 | tf_op jit(solution)/shard_map/ppermute | solution.py:897
  124.7 15.6 %collective-permute-start.15 = (bf16[320,256]{1,0:T(8,128)(2,1)}, bf16[320,256]{1,0:T(8,128)(2,1)S(1)}, u32[]{:S(2)}, u32[]{:S(2)}) collective-permute-start(bf16[320,256]{1,0:T(8,128)(2,1)} %get-tuple-element.92), channel_id=1, source_target_pairs={{0,1},{1,2},{2,3},{3,4},{4,5},{5,6},{6,7},{8,9},{9,10},{10,11},{11... | collective-permute-start | bytes 491528 | tf_op jit(solution)/shard_map/ppermute | solution.py:897
  131.9 8.5 %copy-start.15 = (bf16[256,256]{1,0:T(8,128)(2,1)}, bf16[256,256]{1,0:T(8,128)(2,1)S(1)}, u32[]{:S(2)}) copy-start(bf16[256,256]{1,0:T(8,128)(2,1)S(1)} %collective-permute-done.17.refs_11_) | copy-start | bytes 393220
  131.9 8.4 %collective-permute-start.18 = (bf16[256,256]{1,0:T(8,128)(2,1)}, bf16[256,256]{1,0:T(8,128)(2,1)S(1)}, u32[]{:S(2)}, u32[]{:S(2)}) collective-permute-start(bf16[256,256]{1,0:T(8,128)(2,1)} %get-tuple-element.94), channel_id=1, source_target_pairs={{2,0},{3,1},{4,2},{5,3},{6,4},{7,5},{10,8},{11,9},{12,10},{13,11},... | collective-permute-start | bytes 393224 | tf_op jit(solution)/shard_map/ppermute | solution.py:897
  140.3 0.7 copy-start.14
  140.4 0.9 copy-start.4
  140.4 1.1 copy-start.5
  (6 other events, 4.1 us)

commit v3 on v2

--- a/solution.py
+++ b/solution.py
@@ -265,31 +265,24 @@
 BASE = 1.0 + 6.0 * KAPPA
 
 
-def spots(blocks, hot):
-    lane = iota((1, 128), 1)
-    at_y = iota((1024, 128), 0)
-    tiles = []
+def scatter(blocks, hot, left):
+    lane = iota((128, 128), 1)
     for i, (ref, part) in enumerate(blocks):
         name = ref[256:272, part].astype(F32).astype(jnp.int32)[0:1]
-        tiles.append(lax.shift_right_logical(name, 6))
-        y = (name & 63) * 16 + (lane & 15)
-        hot[:, lanes(i)] = jnp.where(at_y == y, 1.0, 0.0).astype(BF16)
-    return tiles
-
-
-def scatter(blocks, hot):
-    tiles = spots(blocks, hot)
-    for tile in range(4):
-        bz, bx = tile // 2, tile % 2
-        left = [
-            jnp.where(tiles[i] == tile, ref[0:256, part].astype(F32), 0.0).astype(BF16)
-            for i, (ref, part) in enumerate(blocks)
-        ]
-        left = jnp.concatenate(left, axis=1)
-        for n in range(4):
-            cols = slice(n * 256, (n + 1) * 256)
-            sums = lax.dot_general(left, hot[cols, :], (((1,), (1,)), ((), ())), preferred_element_type=F32)
-            yield 16 * bz, slice(16 * bx, 16 * bx + 16), cols, sums.reshape(16, 16, 256)
+        tiles = lax.shift_right_logical(name, 6)
+        at_y = (name & 63) * 16 + (lane[0:1] & 15)
+        at_y = jnp.broadcast_to(at_y.astype(F32), (128, 128)).T.astype(jnp.int32)
+        for t in range(NT):
+            hot[128 * i : 128 * i + 128, lanes(t)] = jnp.where(at_y == lane + 128 * t, 1.0, 0.0).astype(BF16)
+        values = ref[0:256, part].astype(F32)
+        for tile in range(4):
+            left[256 * tile : 256 * tile + 256, lanes(i)] = jnp.where(tiles == tile, values, 0.0).astype(BF16)
+    for n in range(4):
+        cols = slice(n * 256, (n + 1) * 256)
+        sums = jnp.dot(left[...], hot[:, cols], preferred_element_type=F32)
+        for tile in range(4):
+            bz, bx = tile // 2, tile % 2
+            yield 16 * bz, slice(16 * bx, 16 * bx + 16), cols, sums[256 * tile : 256 * tile + 256].reshape(16, 16, 256)
 
 
 def sweep(src, dst, source, gg, z, sourced):
@@ -306,7 +299,7 @@
 
 def own_kernel(
     nz, info, own, zl, zh, density, uptake, s_out, g_out, v_out, edge_out,
-    dens, upt, s0, g0, v1, edge, va, hot, sems,
+    dens, upt, s0, g0, v1, edge, va, hot, left, sems,
 ):
     iz = info[0]
     loads = [pltpu.make_async_copy(density, dens, sems.at[0]), pltpu.make_async_copy(uptake, upt, sems.at[1])]
@@ -327,7 +320,7 @@
 
     blocks = [(ref, lanes(1)) for ref in (own, zl, zh)]
     waiting = list(loads[0:1])
-    for z, rows, cols, sums in scatter(blocks, hot):
+    for z, rows, cols, sums in scatter(blocks, hot, left):
         while waiting:
             waiting.pop().wait()
         planes = slice(z, z + 16)
@@ -364,7 +357,7 @@
 def pre_kernel(
     nz, nx, info, xl, xh, zl, zh, r1, r2, s0, g0, v1, edge_in, uptake,
     c1, mzl, mzh, vzl, vzh, pxl, pxh, v_out, g_out, s_out,
-    va, vb, supply, upt, dh, gg, edge, hot, rs, xp, usl, ush, sems,
+    va, vb, supply, upt, dh, gg, edge, hot, left, rs, xp, usl, ush, sems,
 ):
     iz, ix = info[0], info[1]
     k = KAPPA
@@ -418,7 +411,7 @@
 
     blocks = [(ref, lanes(n)) for ref in (xl, xh) for n in range(3)]
     waiting = list(loads[0:3])
-    for z, rows, cols, sums in scatter(blocks, hot):
+    for z, rows, cols, sums in scatter(blocks, hot, left):
         while waiting:
             waiting.pop().wait()
         supply[z : z + 16, rows, cols] = supply[z : z + 16, rows, cols] + sums
@@ -946,6 +939,7 @@
             scratch((34, C, 1024), F32),
             scratch((C, 8, 1024), F32),
             scratch((42, 40, 1024), F32),
+            scratch((384, 1024), BF16),
             scratch((1024, 384), BF16),
             pltpu.SemaphoreType.DMA((6,)),
         ],
@@ -978,6 +972,7 @@
             scratch((36, 8, 1024), F32),
             scratch((36, 40, 1024), F32),
             scratch((C, 8, 1024), F32),
+            scratch((768, 1024), BF16),
             scratch((1024, 768), BF16),
             scratch((8, 40, 128), F32),
             scratch((8, 20, 24, 128), F32),
@@ -999,9 +994,7 @@
         (c1, r1, mzl, mzh),
     )
     mxl, mxh = both_ways(mxl, mxh, "xy")
-    vzl, vzh, f1 = lax.optimization_barrier((vzl, vzh, f1))
-    vzl, vzh = both_ways(vzl, vzh, "gz")
-    vzl, vzh, pxl, pxh = lax.optimization_barrier((vzl, vzh, pxl, pxh))
+    pxl, pxh, f1 = lax.optimization_barrier((pxl, pxh, f1))
     pxl, pxh = call(
         sides_kernel,
         [half(240, 1024), half(240, 1024)],
@@ -1009,8 +1002,8 @@
         0,
         (pxl, pxh, mzl, mzh, r2),
     )
-    vxl, vxh = both_ways(pxl, pxh, "xy")
-    f1, pxl, pxh = lax.optimization_barrier((f1, pxl, pxh))
+    vzl, vzh, pxl, pxh, f1 = lax.optimization_barrier((vzl, vzh, pxl, pxh, f1))
+    vzl, vzh = both_ways(vzl, vzh, "gz")
     f1, g1, v1, g2, g2l, g2h = call(
         lambda *refs: middle_kernel(nz, nx, *refs),
         [full(24, 24, 512), full(24, 24, 512), full(24, 24, 512), full(64, 256), full(64, 256), full(64, 256)],
@@ -1018,6 +1011,8 @@
         1,
         (info, f1, q1, r2, mxl, mxh),
     )
+    pxl, pxh, g2 = lax.optimization_barrier((pxl, pxh, g2))
+    vxl, vxh = both_ways(pxl, pxh, "xy")
     low, high = both_ways(g2, g2, "gz")
     low2, high2 = two_away(g2l, g2h)
     own2, q2, near, fl, fh = call(

time: 165 us -> 163 us (0.988)
  starting transfers between devices: 64.8 us -> 60.3 us
  waiting for transfers between devices: 10.9 us -> 14.3 us
    ppermute x1, starting transfers between devices: 11.4 us -> 2.69 us  [two_away(): came = lax.ppermute(to_low, 'gz', [(i, (i + 2) % 4) for i in range(4)])]
    ppermute x18, starting transfers between devices: 53.4 us -> 57.6 us  [both_ways(): return (lax.ppermute(to_high, axis, up), lax.ppermute(to_low, axis, down))]
    ppermute x1, waiting for transfers between devices: 0.01 us -> 2.45 us  [two_away(): came = lax.ppermute(to_low, 'gz', [(i, (i + 2) % 4) for i in range(4)])]
  transfers between devices with their start and end apart: 19 -> 19, of which waited for: 6 -> 7; matrix products, arithmetic and copies ran while one was open for 0% -> 0% of each run, Pallas kernels for 17% -> 17%
where the time goes in v3:
time: 163 us
  Pallas kernels  81.6 us (50%)
  starting transfers between devices  60.3 us (37%)
  waiting for transfers between devices  14.3 us (9%)
  local copies, waits for them, and re-layouts  4.75 us (3%)
    pallas_call x10, Pallas kernels, call(): pl.pallas_call(kernel, out_shape=tuple(outs), in_specs=[SMEM] * smem + [V...  81.6 us
    ppermute x18, starting transfers between devices, both_ways(): return (lax.ppermute(to_high, axis, up), lax.ppermute(to_low, axis, down))  57.6 us
    ppermute x18, waiting for transfers between devices, both_ways(): return (lax.ppermute(to_high, axis, up), lax.ppermute(to_low, axis, down))  11.8 us
    unnamed x38, local copies, waits for them, and re-layouts  4.75 us
  transfers between devices with their start and end apart: 19, of which 7 were waited for; matrix products, arithmetic and copies ran while one was open for 0% of the time, Pallas kernels for 17%

profile of v3, /device:TPU:0, one launch (start us, length us, event | category | flops | bytes accessed | tf_op | source)
XLA Modules:
  0.0 162.6 jit_solution(3506649370979790060)
XLA Ops:
  0.6 4.7 %shard_map.68 = (bf16[272,384]{1,0:T(8,128)(2,1)}, bf16[464,384]{1,0:T(8,128)(2,1)}, bf16[464,384]{1,0:T(8,128)(2,1)}) custom-call(s32[72]{0:T(128)} %refs_0_.1, s32[1,9]{1,0:T(1,128)} %refs_1_.1, bf16[72,4096]{1,0:T(8,128)(2,1)} %refs_2_.1, f32[32,32,1024]{2,1,0:T(8,128)} %refs_11_.1), custom_call_target="tpu_custom_call" | custom-call | flops 114121040 | bytes 5706052 | tf_op jit(solution)/shard_map/pallas_call | solution.py:871
  5.3 2.4 %collective-permute-start = (bf16[464,384]{1,0:T(8,128)(2,1)}, bf16[464,384]{1,0:T(8,128)(2,1)S(1)}, u32[]{:S(2)}, u32[]{:S(2)}) collective-permute-start(bf16[464,384]{1,0:T(8,128)(2,1)} %get-tuple-element.57), channel_id=1, source_target_pairs={{0,8},{8,16},{16,24},{1,9},{9,17},{17,25},{2,10},{10,18},{18,26},{... | collective-permute-start | bytes 1069064 | tf_op jit(solution)/shard_map/ppermute | solution.py:890
  7.7 1.3 collective-permute-start.1
  9.0 4.5 %shard_map.69 = (f32[16,16,512]{2,1,0:T(8,128)}, f32[64,256]{1,0:T(8,128)}, bf16[64,1024]{1,0:T(8,128)(2,1)}, bf16[64,1024]{1,0:T(8,128)(2,1)}) custom-call(f32[32,32,1024]{2,1,0:T(8,128)} %refs_11_.1), custom_call_target="tpu_custom_call" | custom-call | flops 100925440 | bytes 5046272 | tf_op jit(solution)/shard_map/pallas_call | solution.py:871
  14.4 2.3 %shard_map.70 = (bf16[464,384]{1,0:T(8,128)(2,1)}, bf16[464,384]{1,0:T(8,128)(2,1)}) custom-call(bf16[272,384]{1,0:T(8,128)(2,1)} %get-tuple-element.53.own.refs_1_, bf16[64,1024]{1,0:T(8,128)(2,1)} %get-tuple-element.55.uxl, bf16[64,1024]{1,0:T(8,128)(2,1)} %get-tuple-element.56.uxh, bf16[464,384]{1,0:T(8,128)(2,1)} %copy-done, bf16[464,384]{1,0:T(8,128)(2,1)} %copy-done.1), custom_call_target="tpu_custom_call" | custom-call | flops 37928960 | bytes 1896448 | tf_op jit(solution)/shard_map/pallas_call | solution.py:871
  16.6 4.2 %collective-permute-start.2 = (bf16[464,384]{1,0:T(8,128)(2,1)}, bf16[464,384]{1,0:T(8,128)(2,1)S(1)}, u32[]{:S(2)}, u32[]{:S(2)}) collective-permute-start(bf16[464,384]{1,0:T(8,128)(2,1)} %get-tuple-element.59), channel_id=1, source_target_pairs={{0,1},{1,2},{2,3},{3,4},{4,5},{5,6},{6,7},{8,9},{9,10},{10,11},{11... | collective-permute-start | bytes 1069064 | tf_op jit(solution)/shard_map/ppermute | solution.py:890
  20.9 1.3 collective-permute-start.3
  22.8 12.2 %shard_map.71 = (f32[32,32,1024]{2,1,0:T(8,128)}, f32[36,32,1024]{2,1,0:T(8,128)}, f32[34,32,1024]{2,1,0:T(8,128)}, f32[32,8,1024]{2,1,0:T(8,128)}) custom-call(s32[2]{0:T(128)} %pad_add_fusion.refs_0_, bf16[272,384]{1,0:T(8,128)(2,1)} %get-tuple-element.53.own.refs_1_, bf16[464,384]{1,0:T(8,128)(2,1)} %copy-done, bf16[464,384]{1,0:T(8,128)(2,1)} %copy-done.1, ...), custom_call_target="tpu_custom_call" | custom-call | flops 474562720 | bytes 23728136 | tf_op jit(solution)/shard_map/pallas_call | solution.py:871
  35.8 21.7 %shard_map.72 = (f32[20,24,512]{2,1,0:T(8,128)}, bf16[160,1024]{1,0:T(8,128)(2,1)}, bf16[160,1024]{1,0:T(8,128)(2,1)}, bf16[208,1024]{1,0:T(8,128)(2,1)}, bf16[2...) custom-call(s32[2]{0:T(128)} %pad_add_fusion.refs_0_, ...), custom_call_target="tpu_custom_call" | custom-call | flops 796590208 | bytes 39829512 | tf_op jit(solution)/shard_map/pallas_call | solution.py:871
  57.5 6.4 %collective-permute-start.4 = (bf16[160,1024]{1,0:T(8,128)(2,1)}, bf16[160,1024]{1,0:T(8,128)(2,1)S(1)}, u32[]{:S(2)}, u32[]{:S(2)}) collective-permute-start(bf16[160,1024]{1,0:T(8,128)(2,1)} %get-tuple-element.73), channel_id=1, source_target_pairs={{0,8},{8,16},{16,24},{1,9},{9,17},{17,25},{2,10},{10,18},{18,26},{... | collective-permute-start | bytes 983048 | tf_op jit(solution)/shard_map/ppermute | solution.py:890
  63.9 1.3 collective-permute-start.5
  65.3 2.3 %collective-permute-done.5.mzh.zh = bf16[160,1024]{1,0:T(8,128)(2,1)S(1)} collective-permute-done((bf16[160,1024]{1,0:T(8,128)(2,1)}, bf16[160,1024]{1,0:T(8,128)(2,1)S(1)}, u32[]{:S(2)}, u32[]{:S(2)}) %collective-permute-start.5) | collective-permute-done | bytes 327712 | tf_op jit(solution)/shard_map/ppermute | solution.py:890
  68.4 3.0 %shard_map.73 = (f32[24,24,512]{2,1,0:T(8,128)}, f32[24,16,512]{2,1,0:T(8,128)}, bf16[240,512]{1,0:T(8,128)(2,1)}, bf16[240,512]{1,0:T(8,128)(2,1)}) custom-call(f32[20,24,512]{2,1,0:T(8,128)} %get-tuple-element.72.c1, f32[16,16,512]{2,1,0:T(8,128)} %get-tuple-element.61.refs_5_.r1, bf16[160,1024]{1,0:T(8,128)(2,1)} %copy-done.2, bf16[160,1024]{1,0:T(8,128)(2,1)} %copy-done.3), custom_call_target="tpu_custom_call" | custom-call | flops 92405760 | bytes 4620288 | tf_op jit(solution)/shard_map/pallas_call | solution.py:871
  71.4 4.3 %collective-permute-start.6 = (bf16[240,512]{1,0:T(8,128)(2,1)}, bf16[240,512]{1,0:T(8,128)(2,1)S(1)}, u32[]{:S(2)}, u32[]{:S(2)}) collective-permute-start(bf16[240,512]{1,0:T(8,128)(2,1)} %get-tuple-element.83), channel_id=1, source_target_pairs={{0,1},{1,2},{2,3},{3,4},{4,5},{5,6},{6,7},{8,9},{9,10},{10,11},{11... | collective-permute-start | bytes 737288 | tf_op jit(solution)/shard_map/ppermute | solution.py:890
  75.7 1.3 collective-permute-start.7
  77.0 2.3 %shard_map.74 = (bf16[240,1024]{1,0:T(8,128)(2,1)}, bf16[240,1024]{1,0:T(8,128)(2,1)}) custom-call(bf16[176,1024]{1,0:T(8,128)(2,1)} %get-tuple-element.76.pxl, bf16[176,1024]{1,0:T(8,128)(2,1)} %get-tuple-element.77.pxh, bf16[160,1024]{1,0:T(8,128)(2,1)} %copy-done.2, bf16[160,1024]{1,0:T(8,128)(2,1)} %copy-done.3, ...), custom_call_target="tpu_custom_call" | custom-call | flops 48496640 | bytes 2424832 | tf_op jit(solution)/shard_map/pallas_call | solution.py:871
  79.3 7.0 %collective-permute-start.8 = (bf16[208,1024]{1,0:T(8,128)(2,1)}, bf16[208,1024]{1,0:T(8,128)(2,1)S(1)}, u32[]{:S(2)}, u32[]{:S(2)}) collective-permute-start(bf16[208,1024]{1,0:T(8,128)(2,1)} %get-tuple-element.88), channel_id=1, source_target_pairs={{0,8},{8,16},{16,24},{1,9},{9,17},{17,25},{2,10},{10,18},{18,26},{... | collective-permute-start | bytes 1277960 | tf_op jit(solution)/shard_map/ppermute | solution.py:890
  86.3 1.5 collective-permute-start.9
  88.6 6.6 %shard_map.75 = (f32[24,24,512]{2,1,0:T(8,128)}, f32[24,24,512]{2,1,0:T(8,128)}, f32[24,24,512]{2,1,0:T(8,128)}, f32[64,256]{1,0:T(8,128)}, f32[64,256]{1,0:T(8,128)}, /*index=5*/f32[64,256]{1,0:T(8,128)}) custom-call(s32[2]{0:T(128)} %pad_add_fusion.refs_0_, f32[24,24,512]{2,1,0:T(8,128)} %get-tuple-element.81.refs_1_, ...), custom_call_target="tpu_custom_call" | custom-call | flops 125173920 | bytes 6258696 | tf_op jit(solution)/shard_map/pallas_call | solution.py:871
  95.1 5.0 %collective-permute-start.10 = (bf16[240,1024]{1,0:T(8,128)(2,1)}, bf16[240,1024]{1,0:T(8,128)(2,1)S(1)}, u32[]{:S(2)}, u32[]{:S(2)}) collective-permute-start(bf16[240,1024]{1,0:T(8,128)(2,1)} %get-tuple-element.93), channel_id=1, source_target_pairs={{0,1},{1,2},{2,3},{3,4},{4,5},{5,6},{6,7},{8,9},{9,10},{10,11},{11... | collective-permute-start | bytes 1474568 | tf_op jit(solution)/shard_map/ppermute | solution.py:890
  100.1 1.3 collective-permute-start.11
  101.4 1.3 collective-permute-start.13
  102.7 2.4 %collective-permute-done.13.high = f32[64,256]{1,0:T(8,128)S(1)} collective-permute-done((f32[64,256]{1,0:T(8,128)}, f32[64,256]{1,0:T(8,128)S(1)}, u32[]{:S(2)}, u32[]{:S(2)}) %collective-permute-start.13) | collective-permute-done | bytes 65568 | tf_op jit(solution)/shard_map/ppermute | solution.py:890
  105.1 5.1 %collective-permute-start.12 = (f32[64,256]{1,0:T(8,128)}, f32[64,256]{1,0:T(8,128)S(1)}, u32[]{:S(2)}, u32[]{:S(2)}) collective-permute-start(f32[64,256]{1,0:T(8,128)} %get-tuple-element.95.own), channel_id=1, source_target_pairs={{0,8},{8,16},{16,24},{1,9},{9,17},{17,25},{2,10},{10,18},{18,26},{... | collective-permute-start | bytes 196616 | tf_op jit(solution)/shard_map/ppermute | solution.py:890
  111.3 2.7 %collective-permute-start.14 = (f32[64,256]{1,0:T(8,128)}, f32[64,256]{1,0:T(8,128)S(1)}, u32[]{:S(2)}, u32[]{:S(2)}) collective-permute-start(f32[64,256]{1,0:T(8,128)} %get-tuple-element.96), channel_id=1, source_target_pairs={{0,16},{8,24},{16,0},{24,8},{1,17},{9,25},{17,1},{25,9},{2,18},{10... | collective-permute-start | bytes 196616 | tf_op jit(solution)/shard_map/ppermute | solution.py:897
  114.0 2.5 %collective-permute-done.14.low2.high2 = f32[64,256]{1,0:T(8,128)S(1)} collective-permute-done((f32[64,256]{1,0:T(8,128)}, f32[64,256]{1,0:T(8,128)S(1)}, u32[]{:S(2)}, u32[]{:S(2)}) %collective-permute-start.14) | collective-permute-done | bytes 65568 | tf_op jit(solution)/shard_map/ppermute | solution.py:897
  117.1 2.2 %shard_map.76 = (f32[32,8,256]{2,1,0:T(8,128)}, f32[32,8,256]{2,1,0:T(8,128)}, bf16[320,256]{1,0:T(8,128)(2,1)}, bf16[256,256]{1,0:T(8,128)(2,1)}, bf16[256,256]{1,0:T(8,128)(2,1)}) custom-call(f32[64,256]{1,0:T(8,128)} %get-tuple-element.95.own, f32[64,256]{1,0:T(8,128)} %copy-done.18, f32[64,256]{1,0:T(8,128)} %copy-done.17, f32[64,256]{1,0:T(8,128)} %copy-done.10, ...), custom_call_target="tpu_custom_call" | custom-call | flops 39976960 | bytes 1998848 | tf_op jit(solution)/shard_map/pallas_call | solution.py:871
  119.3 6.8 %collective-permute-start.17 = (bf16[256,256]{1,0:T(8,128)(2,1)}, bf16[256,256]{1,0:T(8,128)(2,1)S(1)}, u32[]{:S(2)}, u32[]{:S(2)}) collective-permute-start(bf16[256,256]{1,0:T(8,128)(2,1)} %get-tuple-element.99), channel_id=1, source_target_pairs={{0,2},{1,3},{2,4},{3,5},{4,6},{5,7},{8,10},{9,11},{10,12},{11,13},... | collective-permute-start | bytes 393224 | tf_op jit(solution)/shard_map/ppermute | solution.py:890
  126.2 1.3 collective-permute-start.16
  127.5 4.6 %collective-permute-start.15 = (bf16[320,256]{1,0:T(8,128)(2,1)}, bf16[320,256]{1,0:T(8,128)(2,1)S(1)}, u32[]{:S(2)}, u32[]{:S(2)}) collective-permute-start(bf16[320,256]{1,0:T(8,128)(2,1)} %get-tuple-element.98), channel_id=1, source_target_pairs={{0,1},{1,2},{2,3},{3,4},{4,5},{5,6},{6,7},{8,9},{9,10},{10,11},{11... | collective-permute-start | bytes 491528 | tf_op jit(solution)/shard_map/ppermute | solution.py:890
  133.4 5.8 %collective-permute-done.18.refs_12_ = bf16[256,256]{1,0:T(8,128)(2,1)S(1)} collective-permute-done((bf16[256,256]{1,0:T(8,128)(2,1)}, bf16[256,256]{1,0:T(8,128)(2,1)S(1)}, u32[]{:S(2)}, u32[]{:S(2)}) %collective-permute-start.18) | collective-permute-done | bytes 131104 | tf_op jit(solution)/shard_map/ppermute | solution.py:890
  140.3 22.2 %shard_map.77 = f32[32,32,1024]{2,1,0:T(8,128)} custom-call(s32[2]{0:T(128)} %pad_add_fusion.refs_0_, f32[24,24,512]{2,1,0:T(8,128)} %get-tuple-element.85.refs_1_, f32[24,24,512]{2,1,0:T(8,128)} %get-tuple-element.86.refs_2_, f32[24,24,512]{2,1,0:T(8,128)} %get-tuple-element.87.refs_3_, bf16[208,1024]{1,0:T(8,128)(2,1)} %copy-done.6, ...), custom_call_target="tpu_custom_call" | custom-call | flops 533463200 | bytes 26673160 | tf_op jit(solution)/shard_map/pallas_call | solution.py:871
  (55 shorter events, 8.0 us)
Async XLA Ops:
  5.3 8.2 %collective-permute-start = (bf16[464,384]{1,0:T(8,128)(2,1)}, bf16[464,384]{1,0:T(8,128)(2,1)S(1)}, u32[]{:S(2)}, u32[]{:S(2)}) collective-permute-start(bf16[464,384]{1,0:T(8,128)(2,1)} %get-tuple-element.57), channel_id=1, source_target_pairs={{0,8},{8,16},{16,24},{1,9},{9,17},{17,25},{2,10},{10,18},{18,26},{... | collective-permute-start | bytes 1069064 | tf_op jit(solution)/shard_map/ppermute | solution.py:890
  7.7 5.9 %collective-permute-start.1 = (bf16[464,384]{1,0:T(8,128)(2,1)}, bf16[464,384]{1,0:T(8,128)(2,1)S(1)}, u32[]{:S(2)}, u32[]{:S(2)}) collective-permute-start(bf16[464,384]{1,0:T(8,128)(2,1)} %get-tuple-element.58), channel_id=1, source_target_pairs={{8,0},{16,8},{24,16},{9,1},{17,9},{25,17},{10,2},{18,10},{26,18},{... | collective-permute-start | bytes 1069064 | tf_op jit(solution)/shard_map/ppermute | solution.py:890
  13.5 0.8 copy-start
  13.6 0.8 copy-start.1
  16.6 18.3 %collective-permute-start.2 = (bf16[464,384]{1,0:T(8,128)(2,1)}, bf16[464,384]{1,0:T(8,128)(2,1)S(1)}, u32[]{:S(2)}, u32[]{:S(2)}) collective-permute-start(bf16[464,384]{1,0:T(8,128)(2,1)} %get-tuple-element.59), channel_id=1, source_target_pairs={{0,1},{1,2},{2,3},{3,4},{4,5},{5,6},{6,7},{8,9},{9,10},{10,11},{11... | collective-permute-start | bytes 1069064 | tf_op jit(solution)/shard_map/ppermute | solution.py:890
  20.9 14.1 %collective-permute-start.3 = (bf16[464,384]{1,0:T(8,128)(2,1)}, bf16[464,384]{1,0:T(8,128)(2,1)S(1)}, u32[]{:S(2)}, u32[]{:S(2)}) collective-permute-start(bf16[464,384]{1,0:T(8,128)(2,1)} %get-tuple-element.60), channel_id=1, source_target_pairs={{1,0},{2,1},{3,2},{4,3},{5,4},{6,5},{7,6},{9,8},{10,9},{11,10},{12... | collective-permute-start | bytes 1069064 | tf_op jit(solution)/shard_map/ppermute | solution.py:890
  35.0 0.8 copy-start.8
  35.0 0.8 copy-start.9
  57.5 7.8 %collective-permute-start.4 = (bf16[160,1024]{1,0:T(8,128)(2,1)}, bf16[160,1024]{1,0:T(8,128)(2,1)S(1)}, u32[]{:S(2)}, u32[]{:S(2)}) collective-permute-start(bf16[160,1024]{1,0:T(8,128)(2,1)} %get-tuple-element.73), channel_id=1, source_target_pairs={{0,8},{8,16},{16,24},{1,9},{9,17},{17,25},{2,10},{10,18},{18,26},{... | collective-permute-start | bytes 983048 | tf_op jit(solution)/shard_map/ppermute | solution.py:890
  63.9 3.7 %collective-permute-start.5 = (bf16[160,1024]{1,0:T(8,128)(2,1)}, bf16[160,1024]{1,0:T(8,128)(2,1)S(1)}, u32[]{:S(2)}, u32[]{:S(2)}) collective-permute-start(bf16[160,1024]{1,0:T(8,128)(2,1)} %get-tuple-element.74), channel_id=1, source_target_pairs={{8,0},{16,8},{24,16},{9,1},{17,9},{25,17},{10,2},{18,10},{26,18},{... | collective-permute-start | bytes 983048 | tf_op jit(solution)/shard_map/ppermute | solution.py:890
  65.3 2.3 %copy-start.2 = (bf16[160,1024]{1,0:T(8,128)(2,1)}, bf16[160,1024]{1,0:T(8,128)(2,1)S(1)}, u32[]{:S(2)}) copy-start(bf16[160,1024]{1,0:T(8,128)(2,1)S(1)} %collective-permute-done.4.mzl.zl) | copy-start | bytes 983044
  71.4 16.4 %collective-permute-start.6 = (bf16[240,512]{1,0:T(8,128)(2,1)}, bf16[240,512]{1,0:T(8,128)(2,1)S(1)}, u32[]{:S(2)}, u32[]{:S(2)}) collective-permute-start(bf16[240,512]{1,0:T(8,128)(2,1)} %get-tuple-element.83), channel_id=1, source_target_pairs={{0,1},{1,2},{2,3},{3,4},{4,5},{5,6},{6,7},{8,9},{9,10},{10,11},{11... | collective-permute-start | bytes 737288 | tf_op jit(solution)/shard_map/ppermute | solution.py:890
  75.7 12.1 %collective-permute-start.7 = (bf16[240,512]{1,0:T(8,128)(2,1)}, bf16[240,512]{1,0:T(8,128)(2,1)S(1)}, u32[]{:S(2)}, u32[]{:S(2)}) collective-permute-start(bf16[240,512]{1,0:T(8,128)(2,1)} %get-tuple-element.84), channel_id=1, source_target_pairs={{1,0},{2,1},{3,2},{4,3},{5,4},{6,5},{7,6},{9,8},{10,9},{11,10},{12... | collective-permute-start | bytes 737288 | tf_op jit(solution)/shard_map/ppermute | solution.py:890
  79.3 46.9 %collective-permute-start.8 = (bf16[208,1024]{1,0:T(8,128)(2,1)}, bf16[208,1024]{1,0:T(8,128)(2,1)S(1)}, u32[]{:S(2)}, u32[]{:S(2)}) collective-permute-start(bf16[208,1024]{1,0:T(8,128)(2,1)} %get-tuple-element.88), channel_id=1, source_target_pairs={{0,8},{8,16},{16,24},{1,9},{9,17},{17,25},{2,10},{10,18},{18,26},{... | collective-permute-start | bytes 1277960 | tf_op jit(solution)/shard_map/ppermute | solution.py:890
  86.3 41.2 %collective-permute-start.9 = (bf16[208,1024]{1,0:T(8,128)(2,1)}, bf16[208,1024]{1,0:T(8,128)(2,1)S(1)}, u32[]{:S(2)}, u32[]{:S(2)}) collective-permute-start(bf16[208,1024]{1,0:T(8,128)(2,1)} %get-tuple-element.89), channel_id=1, source_target_pairs={{8,0},{16,8},{24,16},{9,1},{17,9},{25,17},{10,2},{18,10},{26,18},{... | collective-permute-start | bytes 1277960 | tf_op jit(solution)/shard_map/ppermute | solution.py:890
  95.1 44.1 %collective-permute-start.10 = (bf16[240,1024]{1,0:T(8,128)(2,1)}, bf16[240,1024]{1,0:T(8,128)(2,1)S(1)}, u32[]{:S(2)}, u32[]{:S(2)}) collective-permute-start(bf16[240,1024]{1,0:T(8,128)(2,1)} %get-tuple-element.93), channel_id=1, source_target_pairs={{0,1},{1,2},{2,3},{3,4},{4,5},{5,6},{6,7},{8,9},{9,10},{10,11},{11... | collective-permute-start | bytes 1474568 | tf_op jit(solution)/shard_map/ppermute | solution.py:890
  100.1 39.1 %collective-permute-start.11 = (bf16[240,1024]{1,0:T(8,128)(2,1)}, bf16[240,1024]{1,0:T(8,128)(2,1)S(1)}, u32[]{:S(2)}, u32[]{:S(2)}) collective-permute-start(bf16[240,1024]{1,0:T(8,128)(2,1)} %get-tuple-element.94), channel_id=1, source_target_pairs={{1,0},{2,1},{3,2},{4,3},{5,4},{6,5},{7,6},{9,8},{10,9},{11,10},{12... | collective-permute-start | bytes 1474568 | tf_op jit(solution)/shard_map/ppermute | solution.py:890
  101.4 3.7 %collective-permute-start.13 = (f32[64,256]{1,0:T(8,128)}, f32[64,256]{1,0:T(8,128)S(1)}, u32[]{:S(2)}, u32[]{:S(2)}) collective-permute-start(f32[64,256]{1,0:T(8,128)} %get-tuple-element.95.own), channel_id=1, source_target_pairs={{8,0},{16,8},{24,16},{9,1},{17,9},{25,17},{10,2},{18,10},{26,18},{... | collective-permute-start | bytes 196616 | tf_op jit(solution)/shard_map/ppermute | solution.py:890
  105.1 11.4 %copy-start.17 = (f32[64,256]{1,0:T(8,128)}, f32[64,256]{1,0:T(8,128)S(1)}, u32[]{:S(2)}) copy-start(f32[64,256]{1,0:T(8,128)S(1)} %collective-permute-done.13.high) | copy-start | bytes 196612
  105.1 6.2 %collective-permute-start.12 = (f32[64,256]{1,0:T(8,128)}, f32[64,256]{1,0:T(8,128)S(1)}, u32[]{:S(2)}, u32[]{:S(2)}) collective-permute-start(f32[64,256]{1,0:T(8,128)} %get-tuple-element.95.own), channel_id=1, source_target_pairs={{0,8},{8,16},{16,24},{1,9},{9,17},{17,25},{2,10},{10,18},{18,26},{... | collective-permute-start | bytes 196616 | tf_op jit(solution)/shard_map/ppermute | solution.py:890
  111.3 5.1 %copy-start.18 = (f32[64,256]{1,0:T(8,128)}, f32[64,256]{1,0:T(8,128)S(1)}, u32[]{:S(2)}) copy-start(f32[64,256]{1,0:T(8,128)S(1)} %collective-permute-done.12.low) | copy-start | bytes 196612
  111.3 5.1 %collective-permute-start.14 = (f32[64,256]{1,0:T(8,128)}, f32[64,256]{1,0:T(8,128)S(1)}, u32[]{:S(2)}, u32[]{:S(2)}) collective-permute-start(f32[64,256]{1,0:T(8,128)} %get-tuple-element.96), channel_id=1, source_target_pairs={{0,16},{8,24},{16,0},{24,8},{1,17},{9,25},{17,1},{25,9},{2,18},{10... | collective-permute-start | bytes 196616 | tf_op jit(solution)/shard_map/ppermute | solution.py:897
  119.3 12.8 %collective-permute-start.17 = (bf16[256,256]{1,0:T(8,128)(2,1)}, bf16[256,256]{1,0:T(8,128)(2,1)S(1)}, u32[]{:S(2)}, u32[]{:S(2)}) collective-permute-start(bf16[256,256]{1,0:T(8,128)(2,1)} %get-tuple-element.99), channel_id=1, source_target_pairs={{0,2},{1,3},{2,4},{3,5},{4,6},{5,7},{8,10},{9,11},{10,12},{11,13},... | collective-permute-start | bytes 393224 | tf_op jit(solution)/shard_map/ppermute | solution.py:890
  126.2 13.1 %copy-start.6 = (bf16[208,1024]{1,0:T(8,128)(2,1)}, bf16[208,1024]{1,0:T(8,128)(2,1)S(1)}, u32[]{:S(2)}) copy-start(bf16[208,1024]{1,0:T(8,128)(2,1)S(1)} %collective-permute-done.8.refs_4_) | copy-start | bytes 1277956
  126.2 13.0 %collective-permute-start.16 = (bf16[320,256]{1,0:T(8,128)(2,1)}, bf16[320,256]{1,0:T(8,128)(2,1)S(1)}, u32[]{:S(2)}, u32[]{:S(2)}) collective-permute-start(bf16[320,256]{1,0:T(8,128)(2,1)} %get-tuple-element.98), channel_id=1, source_target_pairs={{1,0},{2,1},{3,2},{4,3},{5,4},{6,5},{7,6},{9,8},{10,9},{11,10},{12... | collective-permute-start | bytes 491528 | tf_op jit(solution)/shard_map/ppermute | solution.py:890
  127.5 11.7 %copy-start.7 = (bf16[208,1024]{1,0:T(8,128)(2,1)}, bf16[208,1024]{1,0:T(8,128)(2,1)S(1)}, u32[]{:S(2)}) copy-start(bf16[208,1024]{1,0:T(8,128)(2,1)S(1)} %collective-permute-done.9.refs_5_) | copy-start | bytes 1277956
  127.5 11.7 %collective-permute-start.15 = (bf16[320,256]{1,0:T(8,128)(2,1)}, bf16[320,256]{1,0:T(8,128)(2,1)S(1)}, u32[]{:S(2)}, u32[]{:S(2)}) collective-permute-start(bf16[320,256]{1,0:T(8,128)(2,1)} %get-tuple-element.98), channel_id=1, source_target_pairs={{0,1},{1,2},{2,3},{3,4},{4,5},{5,6},{6,7},{8,9},{9,10},{10,11},{11... | collective-permute-start | bytes 491528 | tf_op jit(solution)/shard_map/ppermute | solution.py:890
  132.1 7.2 %copy-start.15 = (bf16[256,256]{1,0:T(8,128)(2,1)}, bf16[256,256]{1,0:T(8,128)(2,1)S(1)}, u32[]{:S(2)}) copy-start(bf16[256,256]{1,0:T(8,128)(2,1)S(1)} %collective-permute-done.17.refs_11_) | copy-start | bytes 393220
  132.1 7.1 %collective-permute-start.18 = (bf16[256,256]{1,0:T(8,128)(2,1)}, bf16[256,256]{1,0:T(8,128)(2,1)S(1)}, u32[]{:S(2)}, u32[]{:S(2)}) collective-permute-start(bf16[256,256]{1,0:T(8,128)(2,1)} %get-tuple-element.100), channel_id=1, source_target_pairs={{2,0},{3,1},{4,2},{5,3},{6,4},{7,5},{10,8},{11,9},{12,10},{13,11},... | collective-permute-start | bytes 393224 | tf_op jit(solution)/shard_map/ppermute | solution.py:890
  139.2 0.8 copy-start.14
  139.2 0.9 copy-start.4
  139.2 1.1 copy-start.5
  (6 other events, 4.2 us)

commit v4 on v3

--- a/solution.py
+++ b/solution.py
@@ -97,7 +97,8 @@
 
 
 BLOCK = 272
-FIRST_ROWS = BLOCK + 3 * 64
+X_ROWS = BLOCK + 3 * 64
+Z_ROWS = BLOCK + 5 * 64
 
 
 def uptake_part(t):
@@ -137,19 +138,12 @@
             block(3 * i + d, out, lanes(d))
 
 
-def first_kernel(bricks_x, ids, counts, bricks, uptake, own, zl, zh, xs, edges, sems):
-    copies = [pltpu.make_async_copy(uptake.at[pl.ds(30 * i, 2)], edges.at[i], sems.at[i]) for i in range(2)]
-    for copy in copies:
-        copy.start()
+def first_kernel(bricks_x, ids, counts, bricks, uptake_in, own, r1, r2, zl, zh, xl, xh, rs, xp, rs1, xp1, xs, uptake, sems):
+    load = pltpu.make_async_copy(uptake_in, uptake, sems.at[0])
+    load.start()
     transposed_bricks(bricks_x, ids, counts, bricks, xs, (zl, own, zh))
-    for i, ref in enumerate((zl, zh)):
-        copies[i].wait()
-        for t in range(8):
-            ref[uptake_part(t)] = edges[i, :, :, lanes(t)].reshape(64, 128).astype(BF16)
-        ref[uptake_part(8)] = jnp.zeros((64, 128), BF16)
-
-
-def rates_kernel(uptake, r1, r2, xl, xh, rs, xp, rs1, xp1):
+    load.wait()
+
     def pair(m):
         for t in range(NT):
             both = uptake[2 * m, :, lanes(t)] + uptake[2 * m + 1, :, lanes(t)]
@@ -167,6 +161,14 @@
     loop(0, 8, pair1)
     for t, tile in enumerate(halve_lanes(xp1, 8, 8)):
         r2[:, lanes(t)] = tile.reshape(64, 128)
+    for ref, u, r in ((zl, slice(0, 2), slice(0, 4)), (zh, slice(30, 32), slice(12, 16))):
+        for t in range(8):
+            ref[uptake_part(t)] = uptake[u, :, lanes(t)].reshape(64, 128).astype(BF16)
+        for t in range(4):
+            ref[uptake_part(8 + t)] = r1[r, :, lanes(t)].reshape(64, 128).astype(BF16)
+        for t in range(2):
+            ref[uptake_part(12 + t)] = r2[:, lanes(t)].astype(BF16)
+        ref[uptake_part(14)] = jnp.zeros((64, 128), BF16)
 
     sub = iota((8, 1024), 0)
 
@@ -219,7 +221,11 @@
     return jnp.stack([even, odd], axis=1).reshape(-1, 8, width)
 
 
-def first_x_kernel(own, uxl, uxh, zl, zh, xl, xh):
+def first_x_kernel(own, r1, uxl, uxh, zl, zh, q1, xl, xh):
+    q1[4:20] = r1[...]
+    for ref, planes in ((zl, slice(0, 4)), (zh, slice(20, 24))):
+        for t in range(4):
+            q1[planes, :, lanes(t)] = ref[uptake_part(8 + t)].astype(F32).reshape(4, 16, 128)
     for ref, d in ((xl, 0), (xh, 2)):
         for n, src in enumerate((own, zl, zh)):
             ref[0:BLOCK, lanes(n)] = src[0:BLOCK, lanes(d)]
@@ -241,21 +247,32 @@
     xh[uptake_part(8)] = jnp.concatenate(highs, axis=0).astype(BF16)
 
 
-def window_planes(own, low, high, low2, high2):
-    parts = (low2, low, own, high, high2)
-    return jnp.concatenate([a.reshape(-1, 8, 256) for a in parts], axis=0)
-
-
-def source_window_kernel(own, low, high, low2, high2, r2, zl, zh, f2, q2, near, fl, fh):
-    planes = window_planes(own[...], low[...], high[...], low2[0:32, :], high2[0:32, :])
-    f2[...] = planes
-    below, above = [ref[80:144, 512:768].astype(F32) for ref in (zl, zh)]
-    rates = window_planes(r2[...], below, above, low2[32:64, :], high2[32:64, :])
-    q2[...] = rates
-    near[0:256, :] = planes.reshape(256, 256).astype(BF16)
-    near[256:320, :] = jnp.concatenate([low2[32:64, :], high2[32:64, :]], axis=0).astype(BF16)
-    for i, values in enumerate((planes, rates)):
-        to_low, to_high = far_messages(values)
+FAR = 80
+
+
+def source_window_kernel(nz, info, own, zl, zh, z2l, z2h, r2, firstl, firsth, f2, q2, near, fl, fh):
+    iz = info[0]
+    zeros = jnp.zeros((10, 8, 256), F32)
+    f2[0:10] = zeros
+    f2[22:32] = zeros
+    f2[10:22] = own[...].reshape(12, 8, 256)
+    for ref, planes in ((zl, slice(2, 14)), (zh, slice(18, 30))):
+        part = jnp.concatenate([ref[240:288, 0:256], ref[240:288, 256:512]], axis=0).astype(F32)
+        f2[planes] = f2[planes] + part.reshape(12, 8, 256)
+    for ref, planes, exists in ((z2l, slice(0, 6), iz >= 2), (z2h, slice(26, 32), iz < nz - 2)):
+        part = jnp.where(exists, ref[0:48, :].astype(F32), 0.0)
+        f2[planes] = f2[planes] + part.reshape(6, 8, 256)
+    q2[0:4] = z2l[48:80, :].astype(F32).reshape(4, 8, 256)
+    q2[28:32] = z2h[48:80, :].astype(F32).reshape(4, 8, 256)
+    q2[12:20] = r2[...].reshape(8, 8, 256)
+    for ref, planes in ((firstl, slice(4, 12)), (firsth, slice(20, 28))):
+        for t in range(2):
+            q2[planes, :, lanes(t)] = ref[uptake_part(12 + t)].astype(F32).reshape(8, 8, 128)
+    near[0:256, :] = f2[...].reshape(256, 256).astype(BF16)
+    near[256:288, :] = z2l[48:80, :]
+    near[288:320, :] = z2h[48:80, :]
+    for i, ref in enumerate((f2, q2)):
+        to_low, to_high = far_messages(ref[...])
         fl[128 * i : 128 * i + 128, :] = to_low.astype(BF16)
         fh[128 * i : 128 * i + 128, :] = to_high.astype(BF16)
 
@@ -355,8 +372,8 @@
 
 
 def pre_kernel(
-    nz, nx, info, xl, xh, zl, zh, r1, r2, s0, g0, v1, edge_in, uptake,
-    c1, mzl, mzh, vzl, vzh, pxl, pxh, v_out, g_out, s_out,
+    nz, nx, info, xl, xh, zl, zh, q1, s0, g0, v1, edge_in, uptake,
+    c1, mxl, mxh, vzl, vzh, pxl, pxh, v_out, g_out, s_out,
     va, vb, supply, upt, dh, gg, edge, hot, left, rs, xp, usl, ush, sems,
 ):
     iz, ix = info[0], info[1]
@@ -476,24 +493,27 @@
 
     empty = jnp.zeros((1, 8, 1024), F32)
     blank = jnp.zeros((8, 1024), F32)
-    edges = (
-        (mzl, vzl, slice(0, 6), slice(0, 4), 3, 0),
-        (mzh, vzh, slice(14, 20), slice(12, 16), 35, 31),
-    )
-    for ref, level0, planes, rates, p, z in edges:
-        source = c1[planes].reshape(144, 512)
-        ref[0:80, 0:512] = source[0:80].astype(BF16)
-        ref[0:64, 512:1024] = source[80:144].astype(BF16)
-        ref[64:80, 512:1024] = jnp.zeros((16, 512), BF16)
-        ref[80:144, 0:512] = r1[rates].reshape(64, 512).astype(BF16)
-        ref[80:144, 512:768] = r2[...].astype(BF16)
-        corner = jnp.concatenate([pack_low(va[p], va[p + 1]), pack_low(va[p + 2], va[p + 3])], axis=0).astype(BF16)
-        for n in range(4):
-            ref[80 + 16 * n : 96 + 16 * n, 768:1024] = corner[:, n * 256 : n * 256 + 256]
-        corner = jnp.concatenate([pack_high(va[p], va[p + 1]), pack_high(va[p + 2], va[p + 3])], axis=0).astype(BF16)
-        ref[144:160, :] = corner
+    sub1 = iota((5, 8, 512), 1)
+    first, last, halo = [c1[:, 8 * n : 8 * n + 8].reshape(5, 4, 8, 512) for n in range(3)]
+    sub4 = iota((5, 4, 8, 512), 2)
+    to_high = in_three(sub1, jnp.where(sub4 >= 4, last, halo), *HIGH_PACK)
+    to_low = in_three(sub1, jnp.where(sub4 >= 4, halo, first), *LOW_PACK)
+    sub1 = iota((12, 8, 512), 1)
+    first = q1[:, 0:8, :].reshape(12, 2, 8, 512)
+    last = q1[:, 8:16, :].reshape(12, 2, 8, 512)
+    low_rates = halves(sub1, first[:, 0], first[:, 1]).reshape(96, 512)
+    high_rates = uppers(sub1, last[:, 0], last[:, 1]).reshape(96, 512)
+    filler = jnp.zeros((8, 512), F32)
+    for ref, sources, rates in ((mxl, to_low, low_rates), (mxh, to_high, high_rates)):
+        ref[0:128, :] = jnp.concatenate([sources.reshape(120, 512), filler], axis=0).astype(BF16)
+        ref[128:224, :] = rates.astype(BF16)
+
+    for level0, p, z in ((vzl, 3, 0), (vzh, 35, 31)):
         values = jnp.concatenate([va[p : p + 4], jnp.concatenate([supply[z : z + 1], empty], axis=1)], axis=0)
-        level0[...] = jnp.concatenate([values.reshape(200, 1024), blank], axis=0).astype(BF16)
+        level0[0:208, :] = jnp.concatenate([values.reshape(200, 1024), blank], axis=0).astype(BF16)
+        for i, pack in enumerate((pack_low, pack_high)):
+            corner = jnp.concatenate([pack(va[p], va[p + 1]), pack(va[p + 2], va[p + 3])], axis=0)
+            level0[208 + 16 * i : 224 + 16 * i, :] = corner.astype(BF16)
 
     def sides(i):
         lows, highs = [], []
@@ -547,16 +567,18 @@
     return pack_pair(sub, a, b)
 
 
-def sides_kernel(pxl, pxh, mzl, mzh, r2, out_l, out_h):
+def sides_kernel(pxl, pxh, vzl, vzh, firstl, firsth, r2, out_l, out_h):
     for ref, out in ((pxl, out_l), (pxh, out_h)):
         out[0:176, :] = ref[...]
-        for n, rates in enumerate((mzl[80:144, 512:768], r2[...].astype(BF16), mzh[80:144, 512:768])):
-            out[176:240, n * 256 : n * 256 + 256] = rates
+        for t in range(2):
+            out[176:240, lanes(t)] = firstl[uptake_part(12 + t)]
+            out[176:240, lanes(2 + t)] = r2[:, lanes(t)].astype(BF16)
+            out[176:240, lanes(4 + t)] = firsth[uptake_part(12 + t)]
         out[176:240, 768:1024] = jnp.zeros((64, 256), BF16)
-    for message, start in ((mzl, 0), (mzh, 128)):
-        low = jnp.concatenate([message[80 + 16 * n : 96 + 16 * n, 768:1024] for n in range(4)], axis=1)
+    for message, start in ((vzl, 0), (vzh, 128)):
         rows = slice(start, start + 16)
-        for ref, out, corner in ((pxl, out_l, low), (pxh, out_h, message[144:160, :])):
+        for i, (ref, out) in enumerate(((pxl, out_l), (pxh, out_h))):
+            corner = message[208 + 16 * i : 224 + 16 * i, :]
             out[rows, :] = (ref[rows, :].astype(F32) + corner.astype(F32)).astype(BF16)
 
 
@@ -581,43 +603,20 @@
 LOW_PACK = (4, (-2, 4, 2))
 
 
-def merge_kernel(c1, r1, mzl, mzh, f1, q1, mxl, mxh):
-    zeros = jnp.zeros((24, 512), F32)
-    for p in (0, 1, 22, 23):
-        f1[p] = zeros
-    f1[2:22] = c1[...]
-    for ref, planes in ((mzl, slice(0, 6)), (mzh, slice(18, 24))):
-        parts = [ref[0:80, 0:512].astype(F32), ref[0:64, 512:1024].astype(F32)]
-        f1[planes] = f1[planes] + jnp.concatenate(parts, axis=0).reshape(6, 24, 512)
-    sub = iota((6, 8, 512), 1)
-    first, last, halo = [f1[:, 8 * n : 8 * n + 8].reshape(6, 4, 8, 512) for n in range(3)]
-    sub4 = iota((6, 4, 8, 512), 2)
-    to_high = in_three(sub, jnp.where(sub4 >= 4, last, halo), *HIGH_PACK)
-    to_low = in_three(sub, jnp.where(sub4 >= 4, halo, first), *LOW_PACK)
-    mxh[0:144, :] = to_high.reshape(144, 512).astype(BF16)
-    mxl[0:144, :] = to_low.reshape(144, 512).astype(BF16)
-    q1[0:4] = mzl[80:144, 0:512].astype(F32).reshape(4, 16, 512)
-    q1[4:20] = r1[...]
-    q1[20:24] = mzh[80:144, 0:512].astype(F32).reshape(4, 16, 512)
-    sub1 = iota((12, 8, 512), 1)
-    first = q1[:, 0:8, :].reshape(12, 2, 8, 512)
-    last = q1[:, 8:16, :].reshape(12, 2, 8, 512)
-    mxl[144:240, :] = halves(sub1, first[:, 0], first[:, 1]).reshape(96, 512).astype(BF16)
-    mxh[144:240, :] = uppers(sub1, last[:, 0], last[:, 1]).reshape(96, 512).astype(BF16)
-
-
-def middle_kernel(nz, nx, info, f0, q_in, r2, mxl, mxh, f1, g1, v1, g2, g2l, g2h, q0, va, rs, xp):
+def middle_kernel(nz, nx, info, c1, q_in, r2, mxl, mxh, f1, g1, v1, g2, z1l, z1h, z2l, z2h, q0, va, vv, rs, xp):
     iz, ix = info[0], info[1]
     k = spread(1)
     base = 1.0 + 6.0 * k
-    sub6 = iota((6, 8, 512), 1)
-    low = out_of_three(sub6, mxl[0:144, :].astype(F32).reshape(6, 3, 8, 512), *HIGH_PACK).reshape(24, 8, 512)
-    high = out_of_three(sub6, mxh[0:144, :].astype(F32).reshape(6, 3, 8, 512), *LOW_PACK).reshape(24, 8, 512)
-    sub = iota((24, 8, 512), 1)
-    f1[:, 0:8] = f0[:, 0:8] + jnp.where(sub < 2, low, 0.0)
-    f1[:, 8:16] = f0[:, 8:16] + jnp.where(sub >= 6, high, 0.0)
-    f1[:, 16:24] = f0[:, 16:24] + jnp.where(sub >= 4, low, high)
-    low, high = [ref[144:240, :].astype(F32).reshape(12, 8, 512) for ref in (mxl, mxh)]
+    sub5 = iota((5, 8, 512), 1)
+    low = out_of_three(sub5, mxl[0:128, :].astype(F32)[0:120].reshape(5, 3, 8, 512), *HIGH_PACK).reshape(20, 8, 512)
+    high = out_of_three(sub5, mxh[0:128, :].astype(F32)[0:120].reshape(5, 3, 8, 512), *LOW_PACK).reshape(20, 8, 512)
+    sub = iota((20, 8, 512), 1)
+    for p in (0, 1, 22, 23):
+        f1[p] = jnp.zeros((24, 512), F32)
+    f1[2:22, 0:8] = c1[:, 0:8] + jnp.where(sub < 2, low, 0.0)
+    f1[2:22, 8:16] = c1[:, 8:16] + jnp.where(sub >= 6, high, 0.0)
+    f1[2:22, 16:24] = c1[:, 16:24] + jnp.where(sub >= 4, low, high)
+    low, high = [ref[128:224, :].astype(F32).reshape(12, 8, 512) for ref in (mxl, mxh)]
     sub12 = iota((12, 8, 512), 1)
     even = jnp.where(sub12 >= 4, shifted(low, 4, 1), high)
     odd = jnp.where(sub12 >= 4, low, shifted(high, 4, 1))
@@ -629,39 +628,46 @@
         g = jnp.where(valid, OMEGA, 0.0) / (q0[:, :, lanes(t)] + base)
         g1[:, :, lanes(t)] = g
         va[:, :, lanes(t)] = g * f1[:, :, lanes(t)]
-    v1[0] = va[0]
-    v1[23] = va[23]
+    for p in (0, 1, 24, 25):
+        vv[p] = jnp.zeros((24, 512), F32)
 
     def sweep(p):
         for t, here, sums in plane(va, p):
-            v1[p, :, lanes(t)] = KEEP * here + g1[p, :, lanes(t)] * (f1[p, :, lanes(t)] + k * sums)
+            vv[p + 1, :, lanes(t)] = KEEP * here + g1[p, :, lanes(t)] * (f1[p, :, lanes(t)] + k * sums)
 
     loop(1, 23, sweep, 2)
+    v1[...] = vv[1:25]
 
     def residual(p):
-        for t, here, sums in plane(v1, p):
+        for t, here, sums in plane(vv, p + 1):
             yield t, f1[p, :, lanes(t)] + k * sums - (q0[p, :, lanes(t)] + base) * here
 
     def coarse(m):
-        for (t, first), (_, second) in zip(residual(2 * m + 4), residual(2 * m + 5)):
+        for (t, first), (_, second) in zip(residual(2 * m), residual(2 * m + 1)):
             xp[t, m] = halve_rows((first + second)[0:16], rs, t)
 
-    loop(0, 8, coarse)
-    for t, tile in enumerate(halve_lanes(xp, 8, 8)):
-        g2[:, lanes(t)] = tile.reshape(64, 128)
-        low, high = far_along_z(nz, iz, tile[0:4].reshape(32, 128), tile[4:8].reshape(32, 128))
-        g2l[0:32, lanes(t)] = low
-        g2h[0:32, lanes(t)] = high
+    loop(0, 12, coarse)
+    for t, tile in enumerate(halve_lanes(xp, 12, 8)):
+        g2[:, lanes(t)] = tile.reshape(96, 128)
+        for ref in (z1l, z1h):
+            ref[240:288, lanes(t)] = tile[0:6].reshape(48, 128).astype(BF16)
+            ref[240:288, lanes(2 + t)] = tile[6:12].reshape(48, 128).astype(BF16)
+    for ref, p in ((z1l, 2), (z1h, 18)):
+        ref[0:144, :] = vv[p : p + 6].reshape(144, 512).astype(BF16)
+        ref[144:240, :] = f1[p : p + 4].reshape(96, 512).astype(BF16)
+    low, high = far_along_z(nz, iz, g2[0:48, :], g2[48:96, :])
+    z2l[0:48, :] = low.astype(BF16)
+    z2h[0:48, :] = high.astype(BF16)
     low, high = far_along_z(nz, iz, r2[0:32, :], r2[32:64, :])
-    g2l[32:64, :] = low
-    g2h[32:64, :] = high
+    z2l[48:80, :] = low.astype(BF16)
+    z2h[48:80, :] = high.astype(BF16)
 
 
 def back_kernel(
-    nz, nx, info, f1, g1, v1, vzl, vzh, vxl, vxh, own2, n2l, n2h, m2l, m2h, q_own, v_in, g_in, s_in,
+    nz, nx, info, f_in, g1, v1, z1l, z1h, vzl, vzh, vxl, vxh, own2, n2l, n2h, m2l, m2h, q_own, v_in, g_in, s_in,
     out_hbm,
     f2, q2, h2, a2, b2, rs, xp, xpr, wa, w1, zsl, zsh, vb, ws,
-    v2, gg, supply, fsl, fsh, out, sems,
+    v2, gg, supply, fsl, fsh, out, f1, sems,
 ):
     iz, ix = info[0], info[1]
     matrix = doubling()
@@ -671,6 +677,12 @@
     ]
     for copy in level0:
         copy.start()
+
+    f1[...] = f_in[...]
+    wa[...] = v1[...]
+    for ref, p in ((z1l, 1), (z1h, 17)):
+        wa[p : p + 6] = wa[p : p + 6] + ref[0:144, :].astype(F32).reshape(6, 24, 512)
+        f1[p + 1 : p + 5] = f1[p + 1 : p + 5] + ref[144:240, :].astype(F32).reshape(4, 24, 512)
 
     f2[:, 0:8, :] = own2[...]
     f2[:, 8:16, :] = n2h[0:256, :].astype(F32).reshape(32, 8, 256)
@@ -764,7 +776,7 @@
             rs[t, pl.ds(1, 16, stride=2), :] = part
             for j in range(2):
                 p = 2 * m + j
-                wa[p, :, lanes(t)] = v1[p, :, lanes(t)] + rs[t, 0:24, :]
+                wa[p, :, lanes(t)] = wa[p, :, lanes(t)] + rs[t, 0:24, :]
     k1 = spread(1)
 
     def sweep1(src, dst):
@@ -786,8 +798,8 @@
 
     for copy in level0:
         copy.wait()
-    zsl[...] = vzl[...].astype(F32)
-    zsh[...] = vzh[...].astype(F32)
+    zsl[...] = vzl[0:208, :].astype(F32)
+    zsh[...] = vzh[0:208, :].astype(F32)
     for i in range(4):
         v2[i] = v2[i] + zsl[40 * i : 40 * i + 40, :]
         v2[32 + i] = v2[32 + i] + zsh[40 * i : 40 * i + 40, :]
@@ -905,28 +917,28 @@
     half = lambda *shape: shaped(shape, BF16)
     full = lambda *shape: shaped(shape, F32)
 
-    own, zl, zh = call(
+    own, r1, r2, zl, zh, uxl, uxh = call(
         lambda *refs: first_kernel(2 * nx, *refs),
-        [half(BLOCK, 384), half(FIRST_ROWS, 384), half(FIRST_ROWS, 384)],
-        [scratch((SLOTS, BRICK), F32), scratch((2, 2, C, 1024), F32), pltpu.SemaphoreType.DMA((2,))],
+        [
+            half(BLOCK, 384), full(16, 16, 512), full(64, 256), half(Z_ROWS, 384), half(Z_ROWS, 384),
+            half(64, 1024), half(64, 1024),
+        ],
+        [
+            scratch((8, 32, 128), F32), scratch((8, 16, 16, 128), F32), scratch((4, 16, 128), F32),
+            scratch((4, 8, 8, 128), F32), scratch((SLOTS, BRICK), F32), scratch((C, C, 1024), F32),
+            pltpu.SemaphoreType.DMA((1,)),
+        ],
         2,
         (brick_ids, slot_counts, brick_values, uptake),
         in_hbm=1,
     )
     zl, zh = both_ways(zl, zh, "gz")
-    r1, r2, uxl, uxh = call(
-        rates_kernel,
-        [full(16, 16, 512), full(64, 256), half(64, 1024), half(64, 1024)],
-        [scratch((8, 32, 128), F32), scratch((8, 16, 16, 128), F32), scratch((4, 16, 128), F32), scratch((4, 8, 8, 128), F32)],
-        0,
-        (lax.optimization_barrier((uptake, own))[0],),
-    )
-    xl, xh = call(
+    q1, xl, xh = call(
         first_x_kernel,
-        [half(FIRST_ROWS, 384), half(FIRST_ROWS, 384)],
+        [full(24, 16, 512), half(X_ROWS, 384), half(X_ROWS, 384)],
         [],
         0,
-        (own, uxl, uxh, zl, zh),
+        (own, r1, uxl, uxh, zl, zh),
     )
     s0, g0, v1, edge = call(
         lambda *refs: own_kernel(nz, *refs),
@@ -950,14 +962,14 @@
     )
     xl, xh = both_ways(xl, xh, "xy")
 
-    c1, mzl, mzh, vzl, vzh, pxl, pxh, v2, gg, supply = call(
+    c1, mxl, mxh, vzl, vzh, pxl, pxh, v2, gg, supply = call(
         lambda *refs: pre_kernel(nz, nx, *refs),
         [
             full(20, 24, 512),
-            half(160, 1024),
-            half(160, 1024),
-            half(208, 1024),
-            half(208, 1024),
+            half(224, 512),
+            half(224, 512),
+            half(240, 1024),
+            half(240, 1024),
             half(176, 1024),
             half(176, 1024),
             full(36, 40, 1024),
@@ -981,46 +993,42 @@
             pltpu.SemaphoreType.DMA((8,)),
         ],
         1,
-        (info, xl, xh, zl, zh, r1, r2, s0, g0, v1, edge, uptake),
+        (info, xl, xh, zl, zh, q1, s0, g0, v1, edge, uptake),
         [VMEM] * 7 + [ANY] * 3,
         in_hbm=5,
     )
-    mzl, mzh = both_ways(mzl, mzh, "gz")
-    f1, q1, mxl, mxh = call(
-        merge_kernel,
-        [full(24, 24, 512), full(24, 16, 512), half(240, 512), half(240, 512)],
-        [],
-        0,
-        (c1, r1, mzl, mzh),
-    )
     mxl, mxh = both_ways(mxl, mxh, "xy")
-    pxl, pxh, f1 = lax.optimization_barrier((pxl, pxh, f1))
+    vzl, vzh = both_ways(vzl, vzh, "gz")
     pxl, pxh = call(
         sides_kernel,
         [half(240, 1024), half(240, 1024)],
         [],
         0,
-        (pxl, pxh, mzl, mzh, r2),
+        (pxl, pxh, vzl, vzh, zl, zh, r2),
     )
-    vzl, vzh, pxl, pxh, f1 = lax.optimization_barrier((vzl, vzh, pxl, pxh, f1))
-    vzl, vzh = both_ways(vzl, vzh, "gz")
-    f1, g1, v1, g2, g2l, g2h = call(
+    c1, mxl, mxh, pxl, pxh = lax.optimization_barrier((c1, mxl, mxh, pxl, pxh))
+    vxl, vxh = both_ways(pxl, pxh, "xy")
+    f1, g1, v1, g2, z1l, z1h, z2l, z2h = call(
         lambda *refs: middle_kernel(nz, nx, *refs),
-        [full(24, 24, 512), full(24, 24, 512), full(24, 24, 512), full(64, 256), full(64, 256), full(64, 256)],
-        [scratch((24, 24, 512), F32), scratch((24, 24, 512), F32), scratch((4, 16, 128), F32), scratch((4, 8, 8, 128), F32)],
+        [
+            full(24, 24, 512), full(24, 24, 512), full(24, 24, 512), full(96, 256),
+            half(288, 512), half(288, 512), half(FAR, 256), half(FAR, 256),
+        ],
+        [
+            scratch((24, 24, 512), F32), scratch((24, 24, 512), F32), scratch((26, 24, 512), F32),
+            scratch((4, 16, 128), F32), scratch((4, 12, 8, 128), F32),
+        ],
         1,
-        (info, f1, q1, r2, mxl, mxh),
+        (info, c1, q1, r2, mxl, mxh),
     )
-    pxl, pxh, g2 = lax.optimization_barrier((pxl, pxh, g2))
-    vxl, vxh = both_ways(pxl, pxh, "xy")
-    low, high = both_ways(g2, g2, "gz")
-    low2, high2 = two_away(g2l, g2h)
+    z1l, z1h = both_ways(z1l, z1h, "gz")
+    z2l, z2h = two_away(z2l, z2h)
     own2, q2, near, fl, fh = call(
-        source_window_kernel,
+        lambda *refs: source_window_kernel(nz, *refs),
         [full(32, 8, 256), full(32, 8, 256), half(320, 256), half(256, 256), half(256, 256)],
         [],
-        0,
-        (g2, low, high, low2, high2, r2, mzl, mzh),
+        1,
+        (info, g2, z1l, z1h, z2l, z2h, r2, zl, zh),
     )
     nl, nh = both_ways(near, near, "xy")
     fl, fh = both_ways(fl, fh, "xy", 2)
@@ -1045,10 +1053,11 @@
             scratch((16, 1024), F32),
             scratch((16, 1024), F32),
             scratch((C, C, 1024), F32),
+            window1,
             pltpu.SemaphoreType.DMA((7,)),
         ],
         1,
-        (info, f1, g1, v1, vzl, vzh, vxl, vxh, own2, nl, nh, fl, fh, q2, v2, gg, supply),
+        (info, f1, g1, v1, z1l, z1h, vzl, vzh, vxl, vxh, own2, nl, nh, fl, fh, q2, v2, gg, supply),
         [ANY],
         in_hbm=3,
     )

time: 163 us -> 157 us (0.963); the launches traced: 163 us -> 155 us
  starting transfers between devices: 60.3 us -> 50.2 us
  waiting for transfers between devices: 14.3 us -> 18.5 us
  Pallas kernels: 81.6 us -> 79.1 us
    ppermute x18 -> x16, starting transfers between devices: 57.6 us -> 47.4 us  [both_ways(): return (lax.ppermute(to_high, axis, up), lax.ppermute(to_low, axis, down))]
    ppermute x18 -> x16, waiting for transfers between devices: 11.8 us -> 16.4 us  [both_ways(): return (lax.ppermute(to_high, axis, up), lax.ppermute(to_low, axis, down))]
    pallas_call x10 -> x8, Pallas kernels: 81.6 us -> 79.1 us  [call(): pl.pallas_call(kernel, out_shape=tuple(outs), in_specs=[SMEM] * smem + [V...]
    unnamed x38 -> x34, local copies, waits for them, and re-layouts: 4.75 us -> 5.21 us
  transfers between devices with their start and end apart: 19 -> 17, of which waited for: 7 -> 6; matrix products, arithmetic and copies ran while one was open for 0% -> 0% of each run, Pallas kernels for 17% -> 11%
where the time goes in v4:
time: 157 us; the launch traced here: 155 us
  Pallas kernels  79.1 us (50%)
  starting transfers between devices  50.2 us (32%)
  waiting for transfers between devices  18.5 us (12%)
  local copies, waits for them, and re-layouts  5.21 us (3%)
    pallas_call x8, Pallas kernels, call(): pl.pallas_call(kernel, out_shape=tuple(outs), in_specs=[SMEM] * smem + [V...  79.1 us
    ppermute x16, starting transfers between devices, both_ways(): return (lax.ppermute(to_high, axis, up), lax.ppermute(to_low, axis, down))  47.4 us
    ppermute x16, waiting for transfers between devices, both_ways(): return (lax.ppermute(to_high, axis, up), lax.ppermute(to_low, axis, down))  16.4 us
    unnamed x34, local copies, waits for them, and re-layouts  5.21 us
  transfers between devices with their start and end apart: 17, of which 6 were waited for; matrix products, arithmetic and copies ran while one was open for 0% of the time, Pallas kernels for 11%

profile of v4, /device:TPU:0, one launch (start us, length us, event | category | flops | bytes accessed | tf_op | source)
XLA Modules:
  0.0 154.8 jit_solution(9649421631633438436)
XLA Ops:
  0.6 7.4 %shard_map.68 = (bf16[272,384]{1,0:T(8,128)(2,1)}, f32[16,16,512]{2,1,0:T(8,128)}, f32[64,256]{1,0:T(8,128)}, bf16[592,384]{1,0:T(8,128)(2,1)}, bf16[592,384]{1,...) custom-call(s32[72]{0:T(128)} %refs_0_.1, s32[1,9]{1,0:T(1,128)} %refs_1_.1, ...), custom_call_target="tpu_custom_call" | custom-call | flops 135092560 | bytes 6754628 | tf_op jit(solution)/shard_map/pallas_call | solution.py:883
  8.0 2.4 %collective-permute-start = (bf16[592,384]{1,0:T(8,128)(2,1)}, bf16[592,384]{1,0:T(8,128)(2,1)S(1)}, u32[]{:S(2)}, u32[]{:S(2)}) collective-permute-start(bf16[592,384]{1,0:T(8,128)(2,1)} %get-tuple-element.49), channel_id=1, source_target_pairs={{0,8},{8,16},{16,24},{1,9},{9,17},{17,25},{2,10},{10,18},{18,26},{... | collective-permute-start | bytes 1363976 | tf_op jit(solution)/shard_map/ppermute | solution.py:902
  10.4 1.3 collective-permute-start.1
  12.0 4.4 %collective-permute-done.1.zh.refs_3_.refs_4_.firsth.refs_8_ = bf16[592,384]{1,0:T(8,128)(2,1)S(1)} collective-permute-done((bf16[592,384]{1,0:T(8,128)(2,1)}, bf16[592,384]{1,0:T(8,128)(2,1)S(1)}, u32[]{:S(2)}, u32[]{:S(2)}) %collective-permute-start.1) | collective-permute-done | bytes 454688 | tf_op jit(solution)/shard_map/ppermute | solution.py:902
  16.5 0.8 copy-done.1
  17.2 2.6 %shard_map.69 = (f32[24,16,512]{2,1,0:T(8,128)}, bf16[464,384]{1,0:T(8,128)(2,1)}, bf16[464,384]{1,0:T(8,128)(2,1)}) custom-call(bf16[272,384]{1,0:T(8,128)(2,1)} %get-tuple-element.45.own.refs_1_, f32[16,16,512]{2,1,0:T(8,128)} %get-tuple-element.46.r1, bf16[64,1024]{1,0:T(8,128)(2,1)} %get-tuple-element.47.uxl, bf16[64,1024]{1,0:T(8,128)(2,1)} %get-tuple-element.48.uxh, ...), custom_call_target="tpu_custom_call" | custom-call | flops 68075520 | bytes 3403776 | tf_op jit(solution)/shard_map/pallas_call | solution.py:883
  19.9 3.4 %collective-permute-start.2 = (bf16[464,384]{1,0:T(8,128)(2,1)}, bf16[464,384]{1,0:T(8,128)(2,1)S(1)}, u32[]{:S(2)}, u32[]{:S(2)}) collective-permute-start(bf16[464,384]{1,0:T(8,128)(2,1)} %get-tuple-element.51), channel_id=1, source_target_pairs={{0,1},{1,2},{2,3},{3,4},{4,5},{5,6},{6,7},{8,9},{9,10},{10,11},{11... | collective-permute-start | bytes 1069064 | tf_op jit(solution)/shard_map/ppermute | solution.py:902
  23.3 1.3 collective-permute-start.3
  25.2 12.2 %shard_map.70 = (f32[32,32,1024]{2,1,0:T(8,128)}, f32[36,32,1024]{2,1,0:T(8,128)}, f32[34,32,1024]{2,1,0:T(8,128)}, f32[32,8,1024]{2,1,0:T(8,128)}) custom-call(s32[2]{0:T(128)} %pad_add_fusion.refs_0_, bf16[272,384]{1,0:T(8,128)(2,1)} %get-tuple-element.45.own.refs_1_, bf16[592,384]{1,0:T(8,128)(2,1)} %copy-done, bf16[592,384]{1,0:T(8,128)(2,1)} %copy-done.1, ...), custom_call_target="tpu_custom_call" | custom-call | flops 478494880 | bytes 23924744 | tf_op jit(solution)/shard_map/pallas_call | solution.py:883
  38.3 21.9 %shard_map.71 = (f32[20,24,512]{2,1,0:T(8,128)}, bf16[224,512]{1,0:T(8,128)(2,1)}, bf16[224,512]{1,0:T(8,128)(2,1)}, bf16[240,1024]{1,0:T(8,128)(2,1)}, bf16[240...) custom-call(s32[2]{0:T(128)} %pad_add_fusion.refs_0_, ...), custom_call_target="tpu_custom_call" | custom-call | flops 803143808 | bytes 40157192 | tf_op jit(solution)/shard_map/pallas_call | solution.py:883
  60.3 8.2 %collective-permute-start.6 = (bf16[240,1024]{1,0:T(8,128)(2,1)}, bf16[240,1024]{1,0:T(8,128)(2,1)S(1)}, u32[]{:S(2)}, u32[]{:S(2)}) collective-permute-start(bf16[240,1024]{1,0:T(8,128)(2,1)} %get-tuple-element.64), channel_id=1, source_target_pairs={{0,8},{8,16},{16,24},{1,9},{9,17},{17,25},{2,10},{10,18},{18,26},{... | collective-permute-start | bytes 1474568 | tf_op jit(solution)/shard_map/ppermute | solution.py:902
  68.5 1.3 collective-permute-start.7
  69.8 4.3 %collective-permute-start.4 = (bf16[224,512]{1,0:T(8,128)(2,1)}, bf16[224,512]{1,0:T(8,128)(2,1)S(1)}, u32[]{:S(2)}, u32[]{:S(2)}) collective-permute-start(bf16[224,512]{1,0:T(8,128)(2,1)} %get-tuple-element.60), channel_id=1, source_target_pairs={{0,1},{1,2},{2,3},{3,4},{4,5},{5,6},{6,7},{8,9},{9,10},{10,11},{11... | collective-permute-start | bytes 688136 | tf_op jit(solution)/shard_map/ppermute | solution.py:902
  74.0 1.3 collective-permute-start.5
  75.4 0.8 copy-done.2
  76.3 2.7 %shard_map.72 = (bf16[240,1024]{1,0:T(8,128)(2,1)}, bf16[240,1024]{1,0:T(8,128)(2,1)}) custom-call(bf16[176,1024]{1,0:T(8,128)(2,1)} %get-tuple-element.62.pxl, bf16[176,1024]{1,0:T(8,128)(2,1)} %get-tuple-element.63.pxh, bf16[240,1024]{1,0:T(8,128)(2,1)} %copy-done.2, bf16[240,1024]{1,0:T(8,128)(2,1)} %copy-done.3, bf16[592,384]{1,0:T(8,128)(2,1)} %copy-done, ...), custom_call_target="tpu_custom_call" | custom-call | flops 73236480 | bytes 3661824 | tf_op jit(solution)/shard_map/pallas_call | solution.py:883
  79.0 1.1 collective-permute-done.4.refs_4_
  80.2 4.7 %collective-permute-done.5.refs_5_ = bf16[224,512]{1,0:T(8,128)(2,1)S(1)} collective-permute-done((bf16[224,512]{1,0:T(8,128)(2,1)}, bf16[224,512]{1,0:T(8,128)(2,1)S(1)}, u32[]{:S(2)}, u32[]{:S(2)}) %collective-permute-start.5) | collective-permute-done | bytes 229408 | tf_op jit(solution)/shard_map/ppermute | solution.py:902
  85.6 7.2 %shard_map.73 = (f32[24,24,512]{2,1,0:T(8,128)}, f32[24,24,512]{2,1,0:T(8,128)}, f32[24,24,512]{2,1,0:T(8,128)}, f32[96,256]{1,0:T(8,128)}, bf16[288,512]{1,0:T(...) custom-call(s32[2]{0:T(128)} %pad_add_fusion.refs_0_, ...), custom_call_target="tpu_custom_call" | custom-call | flops 132055200 | bytes 6602760 | tf_op jit(solution)/shard_map/pallas_call | solution.py:883
  92.8 2.0 %collective-permute-start.8 = (bf16[288,512]{1,0:T(8,128)(2,1)}, bf16[288,512]{1,0:T(8,128)(2,1)S(1)}, u32[]{:S(2)}, u32[]{:S(2)}) collective-permute-start(bf16[288,512]{1,0:T(8,128)(2,1)} %get-tuple-element.75), channel_id=1, source_target_pairs={{0,8},{8,16},{16,24},{1,9},{9,17},{17,25},{2,10},{10,18},{18,26},{... | collective-permute-start | bytes 884744 | tf_op jit(solution)/shard_map/ppermute | solution.py:902
  94.8 1.5 collective-permute-start.9
  96.3 4.8 %collective-permute-start.10 = (bf16[240,1024]{1,0:T(8,128)(2,1)}, bf16[240,1024]{1,0:T(8,128)(2,1)S(1)}, u32[]{:S(2)}, u32[]{:S(2)}) collective-permute-start(bf16[240,1024]{1,0:T(8,128)(2,1)} %get-tuple-element.77), channel_id=1, source_target_pairs={{0,1},{1,2},{2,3},{3,4},{4,5},{5,6},{6,7},{8,9},{9,10},{10,11},{11... | collective-permute-start | bytes 1474568 | tf_op jit(solution)/shard_map/ppermute | solution.py:902
  101.1 1.3 collective-permute-start.11
  102.4 2.8 %collective-permute-start.12 = (bf16[80,256]{1,0:T(8,128)(2,1)}, bf16[80,256]{1,0:T(8,128)(2,1)S(1)}, u32[]{:S(2)}, u32[]{:S(2)}) collective-permute-start(bf16[80,256]{1,0:T(8,128)(2,1)} %get-tuple-element.80), channel_id=1, source_target_pairs={{0,16},{8,24},{16,0},{24,8},{1,17},{9,25},{17,1},{25,9},{2,18},{10... | collective-permute-start | bytes 122888 | tf_op jit(solution)/shard_map/ppermute | solution.py:909
  105.2 2.2 %collective-permute-done.12.refs_4_.refs_5_ = bf16[80,256]{1,0:T(8,128)(2,1)S(1)} collective-permute-done((bf16[80,256]{1,0:T(8,128)(2,1)}, bf16[80,256]{1,0:T(8,128)(2,1)S(1)}, u32[]{:S(2)}, u32[]{:S(2)}) %collective-permute-start.12) | collective-permute-done | bytes 40992 | tf_op jit(solution)/shard_map/ppermute | solution.py:909
  108.3 2.4 %shard_map.74 = (f32[32,8,256]{2,1,0:T(8,128)}, f32[32,8,256]{2,1,0:T(8,128)}, bf16[320,256]{1,0:T(8,128)(2,1)}, bf16[256,256]{1,0:T(8,128)(2,1)}, bf16[256,256]{1,0:T(8,128)(2,1)}) custom-call(s32[2]{0:T(128)} %pad_add_fusion.refs_0_, f32[96,256]{1,0:T(8,128)} %get-tuple-element.79.refs_1_, bf16[288,512]{1,0:T(8,128)(2,1)} %copy-done.4, ...), custom_call_target="tpu_custom_call" | custom-call | flops 53903520 | bytes 2695176 | tf_op jit(solution)/shard_map/pallas_call | solution.py:883
  110.7 7.2 %collective-permute-start.15 = (bf16[256,256]{1,0:T(8,128)(2,1)}, bf16[256,256]{1,0:T(8,128)(2,1)S(1)}, u32[]{:S(2)}, u32[]{:S(2)}) collective-permute-start(bf16[256,256]{1,0:T(8,128)(2,1)} %get-tuple-element.83), channel_id=1, source_target_pairs={{0,2},{1,3},{2,4},{3,5},{4,6},{5,7},{8,10},{9,11},{10,12},{11,13},... | collective-permute-start | bytes 393224 | tf_op jit(solution)/shard_map/ppermute | solution.py:902
  117.9 1.3 collective-permute-start.14
  119.2 4.6 %collective-permute-start.13 = (bf16[320,256]{1,0:T(8,128)(2,1)}, bf16[320,256]{1,0:T(8,128)(2,1)S(1)}, u32[]{:S(2)}, u32[]{:S(2)}) collective-permute-start(bf16[320,256]{1,0:T(8,128)(2,1)} %get-tuple-element.82), channel_id=1, source_target_pairs={{0,1},{1,2},{2,3},{3,4},{4,5},{5,6},{6,7},{8,9},{9,10},{10,11},{11... | collective-permute-start | bytes 491528 | tf_op jit(solution)/shard_map/ppermute | solution.py:902
  123.8 1.3 collective-permute-start.16
  125.1 5.8 %collective-permute-done.16.refs_14_ = bf16[256,256]{1,0:T(8,128)(2,1)S(1)} collective-permute-done((bf16[256,256]{1,0:T(8,128)(2,1)}, bf16[256,256]{1,0:T(8,128)(2,1)S(1)}, u32[]{:S(2)}, u32[]{:S(2)}) %collective-permute-start.16) | collective-permute-done | bytes 131104 | tf_op jit(solution)/shard_map/ppermute | solution.py:902
  132.0 22.6 %shard_map.75 = f32[32,32,1024]{2,1,0:T(8,128)} custom-call(s32[2]{0:T(128)} %pad_add_fusion.refs_0_, f32[24,24,512]{2,1,0:T(8,128)} %get-tuple-element.72.refs_1_, f32[24,24,512]{2,1,0:T(8,128)} %get-tuple-element.73.refs_2_, f32[24,24,512]{2,1,0:T(8,128)} %get-tuple-element.74.refs_3_, bf16[288,512]{1,0:T(8,128)(2,1)} %copy-done.4, ...), custom_call_target="tpu_custom_call" | custom-call | flops 547881088 | bytes 27394056 | tf_op jit(solution)/shard_map/pallas_call | solution.py:883
  (45 shorter events, 4.6 us)
Async XLA Ops:
  8.0 4.0 %collective-permute-start = (bf16[592,384]{1,0:T(8,128)(2,1)}, bf16[592,384]{1,0:T(8,128)(2,1)S(1)}, u32[]{:S(2)}, u32[]{:S(2)}) collective-permute-start(bf16[592,384]{1,0:T(8,128)(2,1)} %get-tuple-element.49), channel_id=1, source_target_pairs={{0,8},{8,16},{16,24},{1,9},{9,17},{17,25},{2,10},{10,18},{18,26},{... | collective-permute-start | bytes 1363976 | tf_op jit(solution)/shard_map/ppermute | solution.py:902
  10.4 6.0 %collective-permute-start.1 = (bf16[592,384]{1,0:T(8,128)(2,1)}, bf16[592,384]{1,0:T(8,128)(2,1)S(1)}, u32[]{:S(2)}, u32[]{:S(2)}) collective-permute-start(bf16[592,384]{1,0:T(8,128)(2,1)} %get-tuple-element.50), channel_id=1, source_target_pairs={{8,0},{16,8},{24,16},{9,1},{17,9},{25,17},{10,2},{18,10},{26,18},{... | collective-permute-start | bytes 1363976 | tf_op jit(solution)/shard_map/ppermute | solution.py:902
  12.0 4.4 %copy-start = (bf16[592,384]{1,0:T(8,128)(2,1)}, bf16[592,384]{1,0:T(8,128)(2,1)S(1)}, u32[]{:S(2)}) copy-start(bf16[592,384]{1,0:T(8,128)(2,1)S(1)} %collective-permute-done.zl.refs_2_.refs_3_.firstl.refs_7_) | copy-start | bytes 1363972
  16.4 0.8 copy-start.1
  19.9 17.5 %collective-permute-start.2 = (bf16[464,384]{1,0:T(8,128)(2,1)}, bf16[464,384]{1,0:T(8,128)(2,1)S(1)}, u32[]{:S(2)}, u32[]{:S(2)}) collective-permute-start(bf16[464,384]{1,0:T(8,128)(2,1)} %get-tuple-element.51), channel_id=1, source_target_pairs={{0,1},{1,2},{2,3},{3,4},{4,5},{5,6},{6,7},{8,9},{9,10},{10,11},{11... | collective-permute-start | bytes 1069064 | tf_op jit(solution)/shard_map/ppermute | solution.py:902
  23.3 14.1 %collective-permute-start.3 = (bf16[464,384]{1,0:T(8,128)(2,1)}, bf16[464,384]{1,0:T(8,128)(2,1)S(1)}, u32[]{:S(2)}, u32[]{:S(2)}) collective-permute-start(bf16[464,384]{1,0:T(8,128)(2,1)} %get-tuple-element.52), channel_id=1, source_target_pairs={{1,0},{2,1},{3,2},{4,3},{5,4},{6,5},{7,6},{9,8},{10,9},{11,10},{12... | collective-permute-start | bytes 1069064 | tf_op jit(solution)/shard_map/ppermute | solution.py:902
  37.4 0.8 copy-start.8
  37.4 0.9 copy-start.9
  60.3 15.1 %collective-permute-start.6 = (bf16[240,1024]{1,0:T(8,128)(2,1)}, bf16[240,1024]{1,0:T(8,128)(2,1)S(1)}, u32[]{:S(2)}, u32[]{:S(2)}) collective-permute-start(bf16[240,1024]{1,0:T(8,128)(2,1)} %get-tuple-element.64), channel_id=1, source_target_pairs={{0,8},{8,16},{16,24},{1,9},{9,17},{17,25},{2,10},{10,18},{18,26},{... | collective-permute-start | bytes 1474568 | tf_op jit(solution)/shard_map/ppermute | solution.py:902
  68.5 6.9 %collective-permute-start.7 = (bf16[240,1024]{1,0:T(8,128)(2,1)}, bf16[240,1024]{1,0:T(8,128)(2,1)S(1)}, u32[]{:S(2)}, u32[]{:S(2)}) collective-permute-start(bf16[240,1024]{1,0:T(8,128)(2,1)} %get-tuple-element.65), channel_id=1, source_target_pairs={{8,0},{16,8},{24,16},{9,1},{17,9},{25,17},{10,2},{18,10},{26,18},{... | collective-permute-start | bytes 1474568 | tf_op jit(solution)/shard_map/ppermute | solution.py:902
  69.8 10.4 %collective-permute-start.4 = (bf16[224,512]{1,0:T(8,128)(2,1)}, bf16[224,512]{1,0:T(8,128)(2,1)S(1)}, u32[]{:S(2)}, u32[]{:S(2)}) collective-permute-start(bf16[224,512]{1,0:T(8,128)(2,1)} %get-tuple-element.60), channel_id=1, source_target_pairs={{0,1},{1,2},{2,3},{3,4},{4,5},{5,6},{6,7},{8,9},{9,10},{10,11},{11... | collective-permute-start | bytes 688136 | tf_op jit(solution)/shard_map/ppermute | solution.py:902
  74.0 10.8 %collective-permute-start.5 = (bf16[224,512]{1,0:T(8,128)(2,1)}, bf16[224,512]{1,0:T(8,128)(2,1)S(1)}, u32[]{:S(2)}, u32[]{:S(2)}) collective-permute-start(bf16[224,512]{1,0:T(8,128)(2,1)} %get-tuple-element.61), channel_id=1, source_target_pairs={{1,0},{2,1},{3,2},{4,3},{5,4},{6,5},{7,6},{9,8},{10,9},{11,10},{12... | collective-permute-start | bytes 688136 | tf_op jit(solution)/shard_map/ppermute | solution.py:902
  75.4 0.8 copy-start.2
  75.4 0.9 copy-start.3
  80.2 4.7 %copy-start.10 = (bf16[224,512]{1,0:T(8,128)(2,1)}, bf16[224,512]{1,0:T(8,128)(2,1)S(1)}, u32[]{:S(2)}) copy-start(bf16[224,512]{1,0:T(8,128)(2,1)S(1)} %collective-permute-done.4.refs_4_) | copy-start | bytes 688132
  84.9 0.7 copy-start.11
  92.8 14.6 %collective-permute-start.8 = (bf16[288,512]{1,0:T(8,128)(2,1)}, bf16[288,512]{1,0:T(8,128)(2,1)S(1)}, u32[]{:S(2)}, u32[]{:S(2)}) collective-permute-start(bf16[288,512]{1,0:T(8,128)(2,1)} %get-tuple-element.75), channel_id=1, source_target_pairs={{0,8},{8,16},{16,24},{1,9},{9,17},{17,25},{2,10},{10,18},{18,26},{... | collective-permute-start | bytes 884744 | tf_op jit(solution)/shard_map/ppermute | solution.py:902
  94.8 12.6 %collective-permute-start.9 = (bf16[288,512]{1,0:T(8,128)(2,1)}, bf16[288,512]{1,0:T(8,128)(2,1)S(1)}, u32[]{:S(2)}, u32[]{:S(2)}) collective-permute-start(bf16[288,512]{1,0:T(8,128)(2,1)} %get-tuple-element.76), channel_id=1, source_target_pairs={{8,0},{16,8},{24,16},{9,1},{17,9},{25,17},{10,2},{18,10},{26,18},{... | collective-permute-start | bytes 884744 | tf_op jit(solution)/shard_map/ppermute | solution.py:902
  96.3 34.6 %collective-permute-start.10 = (bf16[240,1024]{1,0:T(8,128)(2,1)}, bf16[240,1024]{1,0:T(8,128)(2,1)S(1)}, u32[]{:S(2)}, u32[]{:S(2)}) collective-permute-start(bf16[240,1024]{1,0:T(8,128)(2,1)} %get-tuple-element.77), channel_id=1, source_target_pairs={{0,1},{1,2},{2,3},{3,4},{4,5},{5,6},{6,7},{8,9},{9,10},{10,11},{11... | collective-permute-start | bytes 1474568 | tf_op jit(solution)/shard_map/ppermute | solution.py:902
  101.1 29.8 %collective-permute-start.11 = (bf16[240,1024]{1,0:T(8,128)(2,1)}, bf16[240,1024]{1,0:T(8,128)(2,1)S(1)}, u32[]{:S(2)}, u32[]{:S(2)}) collective-permute-start(bf16[240,1024]{1,0:T(8,128)(2,1)} %get-tuple-element.78), channel_id=1, source_target_pairs={{1,0},{2,1},{3,2},{4,3},{5,4},{6,5},{7,6},{9,8},{10,9},{11,10},{12... | collective-permute-start | bytes 1474568 | tf_op jit(solution)/shard_map/ppermute | solution.py:902
  102.4 5.0 %collective-permute-start.12 = (bf16[80,256]{1,0:T(8,128)(2,1)}, bf16[80,256]{1,0:T(8,128)(2,1)S(1)}, u32[]{:S(2)}, u32[]{:S(2)}) collective-permute-start(bf16[80,256]{1,0:T(8,128)(2,1)} %get-tuple-element.80), channel_id=1, source_target_pairs={{0,16},{8,24},{16,0},{24,8},{1,17},{9,25},{17,1},{25,9},{2,18},{10... | collective-permute-start | bytes 122888 | tf_op jit(solution)/shard_map/ppermute | solution.py:909
  107.4 0.7 copy-start.4
  107.4 0.8 copy-start.5
  110.7 13.1 %collective-permute-start.15 = (bf16[256,256]{1,0:T(8,128)(2,1)}, bf16[256,256]{1,0:T(8,128)(2,1)S(1)}, u32[]{:S(2)}, u32[]{:S(2)}) collective-permute-start(bf16[256,256]{1,0:T(8,128)(2,1)} %get-tuple-element.83), channel_id=1, source_target_pairs={{0,2},{1,3},{2,4},{3,5},{4,6},{5,7},{8,10},{9,11},{10,12},{11,13},... | collective-permute-start | bytes 393224 | tf_op jit(solution)/shard_map/ppermute | solution.py:902
  117.9 13.0 %collective-permute-start.14 = (bf16[320,256]{1,0:T(8,128)(2,1)}, bf16[320,256]{1,0:T(8,128)(2,1)S(1)}, u32[]{:S(2)}, u32[]{:S(2)}) collective-permute-start(bf16[320,256]{1,0:T(8,128)(2,1)} %get-tuple-element.82), channel_id=1, source_target_pairs={{1,0},{2,1},{3,2},{4,3},{5,4},{6,5},{7,6},{9,8},{10,9},{11,10},{12... | collective-permute-start | bytes 491528 | tf_op jit(solution)/shard_map/ppermute | solution.py:902
  119.2 11.7 %collective-permute-start.13 = (bf16[320,256]{1,0:T(8,128)(2,1)}, bf16[320,256]{1,0:T(8,128)(2,1)S(1)}, u32[]{:S(2)}, u32[]{:S(2)}) collective-permute-start(bf16[320,256]{1,0:T(8,128)(2,1)} %get-tuple-element.82), channel_id=1, source_target_pairs={{0,1},{1,2},{2,3},{3,4},{4,5},{5,6},{6,7},{8,9},{9,10},{10,11},{11... | collective-permute-start | bytes 491528 | tf_op jit(solution)/shard_map/ppermute | solution.py:902
  123.8 7.1 %copy-start.15 = (bf16[256,256]{1,0:T(8,128)(2,1)}, bf16[256,256]{1,0:T(8,128)(2,1)S(1)}, u32[]{:S(2)}) copy-start(bf16[256,256]{1,0:T(8,128)(2,1)S(1)} %collective-permute-done.15.refs_13_) | copy-start | bytes 393220
  123.8 7.1 %collective-permute-start.16 = (bf16[256,256]{1,0:T(8,128)(2,1)}, bf16[256,256]{1,0:T(8,128)(2,1)S(1)}, u32[]{:S(2)}, u32[]{:S(2)}) collective-permute-start(bf16[256,256]{1,0:T(8,128)(2,1)} %get-tuple-element.84), channel_id=1, source_target_pairs={{2,0},{3,1},{4,2},{5,3},{6,4},{7,5},{10,8},{11,9},{12,10},{13,11},... | collective-permute-start | bytes 393224 | tf_op jit(solution)/shard_map/ppermute | solution.py:902
  130.9 0.7 copy-start.12
  130.9 0.8 copy-start.13
  130.9 0.9 copy-start.6
  130.9 1.1 copy-start.7
  (2 other events, 1.3 us)
